TPU v7x, 128 devices: a whole 4x4x4 slice. The times are simulated.
128 devices in a mesh: ctx: 16 (over z, x_hi, core), tp: 8 (over y, x_lo).
Axes of the slice: x: 4 (x_hi: 2, x_lo: 2; x = x_hi * 2 + x_lo), y: 4, z: 4, core: 2. Of those that a mesh axis runs over, the one named last changes fastest.
Arguments:
- att_query: bfloat16 [8192, 6144], P('ctx', 'tp'), may hold values from -8 to 8
- att_key: bfloat16 [8192, 1024], P('ctx', 'tp'), may hold values from -8 to 8
- att_value: bfloat16 [8192, 1024], P('ctx', 'tp'), may hold values from -140 to 140
- lh_query: bfloat16 [8192, 6144], P('ctx', 'tp'), may hold values from -6 to 6
- lh_key: bfloat16 [8192, 6144], P('ctx', 'tp'), may hold values from -36 to 36
- lh_value: bfloat16 [8192, 6144], P('ctx', 'tp'), may hold values from -36 to 36
- lh_step: float32 [8192, 48], P('ctx', 'tp'), may hold values from 0 to 1
- att_gain: float32 [6144], P('tp'), may hold values from 0.1 to 1.9
- lh_gain: float32 [6144], P('tp'), may hold values from 0.1 to 1.9
Outputs:
- mixed: bfloat16 [8192, 6144], P('ctx', 'tp')
All inputs are finite; a program needn't handle non-finite values.
Results may differ from a plain program's by a relative error of at most 0.012.
Values may be sent and summed in bfloat16 or wider, within the bound.
No kernel may reach another device: no remote copies, remote signals or barrier semaphores. Data moves between devices by JAX's collectives and lax.ppermute only.
A program may use at most 64 MiB of HBM per device.

v0:
```python
import functools
import math

import jax
import jax.numpy as jnp
from jax import lax
from jax.experimental import pallas as pl
from jax.experimental.pallas import tpu as pltpu
from jax.sharding import PartitionSpec as P

HD = 128
ROWS = 512
HEADS = 6
TILE = 256
EPS = 1e-06
MASKED = -1e30
LOG2E = math.log2(math.e)
SCORE_SCALE = LOG2E / math.sqrt(HD)
SAFE_EXPONENT = 100.0
STATE_ROWS = HEADS * HD + 8
NEVER = 1 << 20

VMEM = pl.BlockSpec(memory_space=pltpu.VMEM)
SMEM = pl.BlockSpec(memory_space=pltpu.SMEM)
f32 = jnp.float32
bf16 = jnp.bfloat16
highest = lax.Precision.HIGHEST


def dot(a, b, contract=((1,), (0,)), precision=None):
    return lax.dot_general(a, b, (contract, ((), ())), precision=precision, preferred_element_type=f32)


def params(megabytes):
    return pltpu.CompilerParams(vmem_limit_bytes=megabytes << 20)


def cost(us):
    return pl.CostEstimate(flops=int(us * 1e9), bytes_accessed=int(us * 1e6), transcendentals=int(us * 1e6))


def head(h):
    return slice(h * HD, (h + 1) * HD)


def recur_kernel(
    q_hbm, k_hbm, v_hbm, step_ref, local_ref, grow_ref, message_ref, padded
):
    k_ref, q_ref, v_ref = k_hbm, q_hbm, v_hbm
    padded[...] = jnp.full((8, ROWS), 0.5, f32)
    padded[:HEADS, :] = step_ref[...]
    step = padded[...]
    rate = step / (1.0 + step)
    total = -jnp.log(1.0 + step) * LOG2E
    place = lax.broadcasted_iota(jnp.int32, (8, ROWS), 1)
    reach = 1
    while reach < ROWS:
        total = total + jnp.where(place >= reach, pltpu.roll(total, reach, 1), 0.0)
        reach *= 2
    source = jnp.log(rate) * LOG2E - total
    end = total[:, ROWS - 1 : ROWS]
    tail = jnp.exp2(end + source)
    rows = jnp.concatenate([total, tail, jnp.zeros((HD - 16, ROWS), f32)], 0)
    columns = jnp.transpose(rows)
    grow_ref[...] = jnp.exp2(columns)
    message_ref[HEADS * HD :, :] = jnp.broadcast_to(end, (8, HD))
    at_row = lax.broadcasted_iota(jnp.int32, (TILE, TILE), 0)
    at_column = lax.broadcasted_iota(jnp.int32, (TILE, TILE), 1)
    seen = at_column <= at_row
    for h in range(HEADS):
        keys = k_ref[:, head(h)].astype(f32)
        keys = keys * lax.rsqrt(jnp.sum(keys * keys, -1, keepdims=True) + EPS)
        unit = keys.astype(bf16)
        values = v_ref[:, head(h)]
        for a in range(0, ROWS, TILE):
            result = None
            for b in range(0, a + TILE, TILE):
                scores = dot(q_ref[a : a + TILE, head(h)], unit[b : b + TILE], ((1,), (1,)))
                decay = jnp.exp2(columns[a : a + TILE, h : h + 1] + source[h : h + 1, b : b + TILE])
                weights = scores * decay
                if a == b:
                    weights = jnp.where(seen, weights, 0.0)
                part = dot(weights.astype(bf16), values[b : b + TILE])
                result = part if result is None else result + part
            local_ref[a : a + TILE, head(h)] = result
        tailed = (values.astype(f32) * columns[:, 8 + h : 9 + h]).astype(bf16)
        message_ref[head(h), :] = dot(unit, tailed, ((0,), (0,)))


def recur(lh_query, lh_key, lh_value, lh_step):
    return pl.pallas_call(
        recur_kernel,
        out_shape=(
            jax.ShapeDtypeStruct((ROWS, HEADS * HD), f32),
            jax.ShapeDtypeStruct((ROWS, HD), f32),
            jax.ShapeDtypeStruct((STATE_ROWS, HD), f32),
        ),
        in_specs=[VMEM] * 4,
        out_specs=(VMEM,) * 3,
        scratch_shapes=[pltpu.VMEM((8, ROWS), f32)]
,
        compiler_params=params(16),
        cost_estimate=cost(0.2),
        name="recur",
    )(lh_query, lh_key, lh_value, lh_step.T)


def beside_kernel(key_ref, value_ref, out_ref):
    out_ref[:, :HD] = key_ref[...]
    out_ref[:, HD:] = value_ref[...]


def beside(key, value):
    return pl.pallas_call(
        beside_kernel,
        out_shape=jax.ShapeDtypeStruct((ROWS, 2 * HD), bf16),
        in_specs=[VMEM, VMEM],
        out_specs=VMEM,
        compiler_params=params(14),
        name="beside",
    )(key, value)


def stack_kernel(one_ref, two_ref, out_ref):
    out_ref[:ROWS, :] = one_ref[...]
    out_ref[ROWS:, :] = two_ref[...]


def stack(one, two):
    return pl.pallas_call(
        stack_kernel,
        out_shape=jax.ShapeDtypeStruct((2 * ROWS, 2 * HD), bf16),
        in_specs=[VMEM, VMEM],
        out_specs=VMEM,
        compiler_params=params(14),
        name="stack",
    )(one, two)


def follow(early, late):
    logs = early[1] + late[1]
    states = [jnp.exp2(late[1][h : h + 1, :]) * early[0][h] + late[0][h] for h in range(HEADS)]
    return states, logs


def state_of(ref, wanted=None):
    states = [ref[head(h), :] for h in range(HEADS)]
    logs = ref[HEADS * HD :, :]
    if wanted is None:
        return states, logs
    return [jnp.where(wanted, state, 0.0) for state in states], jnp.where(wanted, logs, 0.0)


def put_state(ref, value):
    for h in range(HEADS):
        ref[head(h), :] = value[0][h]
    ref[HEADS * HD :, :] = value[1]


def join_kernel(bit, mine_ref, own_ref, other_ref, out_ref):
    own_first = (mine_ref[0] // bit) % 2 == 0
    own, other = state_of(own_ref), state_of(other_ref)

    def pick(one, two):
        return [jnp.where(own_first, a, b) for a, b in zip(one[0], two[0])], jnp.where(own_first, one[1], two[1])

    put_state(out_ref, follow(pick(own, other), pick(other, own)))


def join(bit, mine, own, other):
    return pl.pallas_call(
        functools.partial(join_kernel, bit),
        out_shape=jax.ShapeDtypeStruct((STATE_ROWS, HD), f32),
        in_specs=[SMEM, VMEM, VMEM],
        out_specs=VMEM,
        compiler_params=params(14),
        cost_estimate=cost(0.2),
        name="join",
    )(mine, own, other)


def hand_kernel(mine_ref, behind_ref, beyond_ref, out_ref):
    plane, core = mine_ref[0] // 4, mine_ref[0] % 2
    behind = state_of(behind_ref, (plane == 3) | (core == 0))
    beyond = state_of(beyond_ref, (plane >= 2) & (core == 1))
    put_state(out_ref, follow(behind, beyond))


def hand(mine, behind, beyond):
    return pl.pallas_call(
        hand_kernel,
        out_shape=jax.ShapeDtypeStruct((STATE_ROWS, HD), f32),
        in_specs=[SMEM, VMEM, VMEM],
        out_specs=VMEM,
        compiler_params=params(14),
        cost_estimate=cost(0.2),
        name="hand",
    )(mine, behind, beyond)


def attend_kernel(first, last, numbers_of, buffers, kept_numbers_of, kept, mine_ref, query_ref, own_ref, *refs):
    mine = mine_ref[0]
    refs = list(refs)

    def take(count):
        return [refs.pop(0) for _ in range(count)]

    if not first:
        carry_ref, count_ref, top_in_ref = take(3)
    block_refs = take(buffers)
    kept_refs = take(kept)
    if last:
        out_ref, square_ref, sums, keys, values, top_ref, tops = refs
    else:
        numerator_ref, counted_ref, top_ref, sums, keys, values = refs

    def highest_of(part):
        return jnp.max(jnp.abs(part).reshape(-1, 16, HD), 0)

    def fill(blocks, numbers):
        filled = jnp.int32(0)
        for block, number in zip(blocks, numbers):
            rows = block.shape[0]
            takes = number < mine
            place = filled

            @pl.when(takes)
            def _():
                at = pl.ds(pl.multiple_of(place * ROWS, ROWS), rows)
                keys[at, :] = block[:, :HD]
                values[at, :HD] = block[:, HD:]
                top_ref[16:32, :] = jnp.maximum(top_ref[16:32, :], highest_of(block[:, :HD]))

            filled = filled + jnp.where(takes, rows // ROWS, 0)
        return filled

    if first:
        top_ref[16:32, :] = highest_of(own_ref[:, :HD])
        longest = jnp.zeros((ROWS, HD), f32)
        ones = jnp.ones((HD, HD), bf16)
        for h in range(HEADS):
            query = query_ref[:, head(h)].astype(f32)
            longest = jnp.maximum(longest, dot((query * query).astype(bf16), ones))
        top_ref[0:16, :] = jnp.max(longest.reshape(-1, 16, HD), 0).astype(bf16)
    else:
        top_ref[...] = top_in_ref[...]
    values[:, HD:] = jnp.ones((values.shape[0], HD), bf16)
    filled = fill(block_refs, numbers_of(mine))
    sums[...] = jnp.zeros_like(sums)

    def visit(start, count):
        at = pl.ds(pl.multiple_of(start, ROWS), count)
        block_keys = keys[at, :]
        block_values = values[at, :]
        for h in range(HEADS):
            for a in range(0, ROWS, TILE):
                scores = dot(query_ref[a : a + TILE, head(h)], block_keys, ((1,), (1,)))
                weights = jnp.exp2(scores * SCORE_SCALE).astype(bf16)
                sums[h, a : a + TILE, :] += dot(weights, block_values)

    def pair(n, _):
        visit(n * 2 * ROWS, 2 * ROWS)
        return 0

    lax.fori_loop(0, filled // 2, pair, 0)

    if first:

        @pl.when(filled % 2 == 1)
        def _():
            visit((filled - 1) * ROWS, ROWS)

        at_row = lax.broadcasted_iota(jnp.int32, (TILE, TILE), 0)
        at_column = lax.broadcasted_iota(jnp.int32, (TILE, TILE), 1)
        seen = at_column <= at_row
        values[:ROWS, :HD] = own_ref[:, HD:]
        for h in range(HEADS):
            for a in range(0, ROWS, TILE):
                for b in range(0, a + TILE, TILE):
                    scores = dot(query_ref[a : a + TILE, head(h)], own_ref[b : b + TILE, :HD], ((1,), (1,)))
                    weights = jnp.exp2(scores * SCORE_SCALE)
                    if a == b:
                        weights = jnp.where(seen, weights, 0.0)
                    sums[h, a : a + TILE, :] += dot(weights.astype(bf16), values[b : b + TILE, :])
            numerator_ref[:, head(h)] = sums[h, :, :HD]
            counted_ref[:, h : h + 1] = sums[h, :, HD : HD + 1]
    elif not last:
        for h in range(HEADS):
            numerator_ref[:, head(h)] = sums[h, :, :HD] + carry_ref[:, head(h)]
            counted_ref[:, h : h + 1] = sums[h, :, HD : HD + 1] + count_ref[:, h : h + 1]
    else:
        key_top = jnp.max(top_ref[16:32, :].astype(f32), 0, keepdims=True)
        bound = jnp.max(top_ref[0:16, :].astype(f32)) * jnp.sum(key_top * key_top) * SCORE_SCALE**2
        large = bound * 1.05 > SAFE_EXPONENT * SAFE_EXPONENT

        @pl.when(large)
        def _():
            before = fill(kept_refs + block_refs, kept_numbers_of(mine) + numbers_of(mine))
            at = pl.ds(pl.multiple_of(before * ROWS, ROWS), ROWS)
            keys[at, :] = own_ref[:, :HD]
            values[at, :HD] = own_ref[:, HD:]
            sums[...] = jnp.zeros_like(sums)
            tops[...] = jnp.full_like(tops, MASKED)

            def step(n, _):
                at = pl.ds(pl.multiple_of((n // (2 * HEADS)) * ROWS, ROWS), ROWS)
                h = (n % (2 * HEADS)) // 2
                a = (n % 2) * TILE
                rows = pl.ds(pl.multiple_of(a, TILE), TILE)
                query = query_ref[rows, pl.ds(pl.multiple_of(h * HD, HD), HD)]
                scores = dot(query, keys[at, :], ((1,), (1,))) * SCORE_SCALE
                row = lax.broadcasted_iota(jnp.int32, (TILE, ROWS), 0) + a
                column = lax.broadcasted_iota(jnp.int32, (TILE, ROWS), 1)
                column = column - jnp.where(n // (2 * HEADS) < before, ROWS, 0)
                visible = column <= row
                scores = jnp.where(visible, scores, MASKED)
                old = tops[h, rows, :]
                new = jnp.maximum(old[:, :1], jnp.max(scores, 1, keepdims=True))
                weights = jnp.where(visible, jnp.exp2(scores - new), 0.0).astype(bf16)
                sums[h, rows, :] = sums[h, rows, :] * jnp.exp2(old[:, :1] - new) + dot(weights, values[at, :])
                tops[h, rows, :] = jnp.broadcast_to(new, (TILE, HD))
                return 0

            lax.fori_loop(0, (before + 1) * 2 * HEADS, step, 0)

        squares = jnp.zeros((ROWS, HD), f32)
        for h in range(HEADS):
            count = sums[h, :, HD:] + jnp.where(large, 0.0, count_ref[:, h : h + 1])
            result = (sums[h, :, :HD] + jnp.where(large, 0.0, carry_ref[:, head(h)])) / count
            result = result.astype(bf16)
            out_ref[:, head(h)] = result
            result = result.astype(f32)
            squares = squares + result * result
        square_ref[...] = dot(jnp.ones((8, HD), f32), squares, ((1,), (1,)), highest)


def attend(mine, query, own, carry, blocks, numbers_of, kept=None, kept_numbers_of=None):
    first, last = carry is None, kept is not None
    kept = kept or []
    size = sum(block.shape[0] for block in blocks)
    size = 16 * ROWS if last else size
    operands = [query, own] + list(carry or []) + list(blocks) + kept
    top = (32, HD)
    scratch = [
        pltpu.VMEM((HEADS, ROWS, 2 * HD), f32),
        pltpu.VMEM((size, HD), bf16),
        pltpu.VMEM((size, 2 * HD), bf16),
    ]
    if last:
        out_shape = (
            jax.ShapeDtypeStruct((ROWS, HEADS * HD), bf16),
            jax.ShapeDtypeStruct((8, ROWS), f32),
        )
        scratch += [pltpu.VMEM(top, bf16), pltpu.VMEM((HEADS, ROWS, HD), f32)]
    else:
        out_shape = (
            jax.ShapeDtypeStruct((ROWS, HEADS * HD), f32),
            jax.ShapeDtypeStruct((ROWS, HD), f32),
            jax.ShapeDtypeStruct(top, bf16),
        )
    return pl.pallas_call(
        functools.partial(attend_kernel, first, last, numbers_of, len(blocks), kept_numbers_of, len(kept)),
        out_shape=out_shape,
        in_specs=[SMEM] + [VMEM] * len(operands),
        out_specs=(VMEM,) * len(out_shape),
        scratch_shapes=scratch,
        compiler_params=params(20),
        cost_estimate=cost(0.2),
        name="attend_first" if first else "attend_last" if last else "attend_middle",
    )(mine, *operands)


def carry_kernel(
    mine_ref,
    query_hbm,
    local_ref,
    grow_ref,
    kept_ref,
    handed_ref,
    chip_ref,
    core_ref,
    gain_ref,
    out_ref,
):
    mine = mine_ref[0]
    query_ref = query_hbm
    plane, side, core = mine // 4, (mine // 2) % 2, mine % 2
    kept, handed = state_of(kept_ref), state_of(handed_ref)

    def pick(one, two, wanted):
        states = [jnp.where(wanted, jnp.where(core == 0, a, b), 0.0) for a, b in zip(one[0], two[0])]
        return states, jnp.where(wanted, jnp.where(core == 0, one[1], two[1]), 0.0)

    entering = pick(handed, kept, plane >= 2)
    entering = follow(entering, pick(kept, handed, plane >= 1))
    entering = follow(entering, state_of(chip_ref, side == 1))
    entering = follow(entering, state_of(core_ref, core == 1))
    grow = grow_ref[...]
    for h in range(HEADS):
        state = entering[0][h]
        upper = state.astype(bf16)
        lower = (state - upper.astype(f32)).astype(bf16)
        both = dot(query_ref[:, head(h)], jnp.concatenate([upper, lower], 1))
        entered = both[:, :HD] + both[:, HD:]
        result = local_ref[:, head(h)] + entered * grow[:, h : h + 1]
        square = jnp.mean(result * result, -1, keepdims=True)
        out_ref[:, head(h)] = result * lax.rsqrt(square + EPS) * gain_ref[head(h)][None, :]


def finish_kernel(features, attention_ref, square_ref, other_ref, linear_ref, gain_ref, out_ref):
    factor = lax.rsqrt((square_ref[...] + other_ref[...]) / features + EPS)
    factor = dot(factor, jnp.full((8, HD), 0.125, f32), ((0,), (0,)), highest)
    for h in range(HEADS):
        part = attention_ref[:, head(h)].astype(f32) * factor * gain_ref[head(h)][None, :]
        out_ref[:, head(h)] = (part + linear_ref[:, head(h)]).astype(bf16)


def carry_in(place, lh_query, *operands):
    return pl.pallas_call(
        carry_kernel,
        out_shape=jax.ShapeDtypeStruct((ROWS, HEADS * HD), f32),
        in_specs=[SMEM, VMEM] + [VMEM] * len(operands),
        out_specs=VMEM,
        compiler_params=params(14),
        cost_estimate=cost(0.2),
        name="carry",
    )(place, lh_query, *operands)


def finish(features, *operands):
    return pl.pallas_call(
        functools.partial(finish_kernel, features),
        out_shape=jax.ShapeDtypeStruct((ROWS, HEADS * HD), bf16),
        in_specs=[VMEM] * len(operands),
        out_specs=VMEM,
        compiler_params=params(14),
        cost_estimate=cost(0.2),
        name="finish",
    )(*operands)


def body(att_query, att_key, att_value, lh_query, lh_key, lh_value, lh_step, att_gain, lh_gain):
    mine = lax.axis_index("ctx")
    place = mine.reshape(1).astype(jnp.int32)

    def move(value, pairs):
        return lax.ppermute(value, "ctx", pairs)

    every = range(16)
    sibling = [(i, i ^ 1) for i in every]
    sideways = [(i, i ^ 2) for i in every]
    last_plane = [(i, i + 4) for i in every if i % 2 == 0 and i < 12] + [(i, i + 12) for i in (1, 3)]
    plane_before = [(i, i + 8) for i in every if i % 2 == 1 and i < 8]

    def tied(*values):
        return lax.optimization_barrier(values)

    lh_query, lh_key, lh_value, far_query, att_key, att_value = [
        array
        for array in (lh_query, lh_key, lh_value, att_query, att_key, att_value)
    ]
    near_query = att_query
    lh_query, lh_key, lh_value = [
        pltpu.with_memory_space_constraint(array, pltpu.HBM) for array in (lh_query, lh_key, lh_value)
    ]
    own = beside(att_key, att_value)
    across = move(own, [(i, i ^ 2) for i in every if i < 4 or i % 4 < 2])
    near = move(own, sibling)
    chip = stack(own, near)
    chip, lh_step = tied(chip, lh_step)
    behind = move(chip, last_plane)

    local, grow, message = recur(lh_query, lh_key, lh_value, lh_step)
    chip, across, message = tied(chip, across, message)
    beyond = move(chip, plane_before)
    across_near = move(across, sibling)
    first = move(message, sibling)
    of_chip = join(1, place, message, first)
    other_chip = move(of_chip, sideways)
    behind, of_chip = tied(behind, of_chip)
    behind_near = move(behind, sibling)
    level = move(behind, [(i, j) for i, j in sideways if (i % 2 == 0 and i >= 4) or i >= 12])

    def where(number, wanted):
        return jnp.where(wanted, number, NEVER)

    def parts(mine):
        return mine // 4, (mine // 2) % 2, mine % 2, mine - mine % 2

    def brought(mine, core):
        plane, _, _, even = parts(mine)
        if core == 0:
            return where(even - 4, plane >= 1)
        return where(even - 12, plane == 3)

    def behind_numbers(mine):
        _, _, core, _ = parts(mine)
        zero, one = brought(mine, 0), brought(mine, 1)
        return [jnp.where(core == 0, zero, one), jnp.where(core == 0, one, zero)]

    def beyond_numbers(mine):
        plane, _, core, even = parts(mine)
        number = where(even - 8, plane >= 2)
        return [where(number, core == 1), where(number, core == 0)]

    def first_numbers(mine):
        _, side, core, even = parts(mine)
        near_numbers = [where(mine - 1, core == 1)] + [where(even - 2, side == 1)] * 2
        return near_numbers + behind_numbers(mine)

    def middle_numbers(mine):
        return behind_numbers(mine) + beyond_numbers(mine)

    first_blocks = [near, across, across_near, behind, behind_near]
    carry = attend(place, near_query, own, None, first_blocks, first_numbers)
    carry, other_chip, beyond, level = tied(carry, other_chip, beyond, level)
    level_beyond = move(beyond, [(i, j) for i, j in sideways if i % 2 == 1 and i >= 8])
    beyond_near = move(beyond, sibling)
    level_near = move(level, sibling)
    of_plane = join(2, place, of_chip, other_chip)
    state_behind = move(of_plane, last_plane)
    state_beyond = move(of_plane, plane_before)
    middle_blocks = [level, level_near, beyond, beyond_near]
    middle_blocks, of_plane = tied(middle_blocks, of_plane)
    carry = attend(place, near_query, own, carry, middle_blocks, middle_numbers)
    carry, level_beyond, state_behind, state_beyond = tied(carry, level_beyond, state_behind, state_beyond)
    level_beyond_near = move(level_beyond, sibling)
    kept = hand(place, state_behind, state_beyond)
    handed = move(kept, sibling)
    last_blocks = [level_beyond, level_beyond_near]
    last_blocks, kept = tied(last_blocks, kept)
    attention, squares = attend(
        place,
        near_query,
        own,
        carry,
        last_blocks,
        beyond_numbers,
        first_blocks + middle_blocks,
        lambda mine: first_numbers(mine) + middle_numbers(mine),
    )
    squares, handed = tied(squares, handed)
    linear = carry_in(place, lh_query, local, grow, kept, handed, other_chip, first, lh_gain)

    def over(value, bit):
        return lax.ppermute(value, "tp", [(i, i ^ bit) for i in range(8)])

    first_round = over(squares, 1)
    first_round, linear = tied(first_round, linear)
    squares = squares + first_round
    squares = squares + over(squares, 2)
    features = HEADS * HD * lax.axis_size("tp")
    return finish(float(features), attention, squares, over(squares, 4), linear, att_gain)


def solution(mesh):
    placed = (P("ctx", "tp"),) * 7 + (P("tp"), P("tp"))
    return jax.shard_map(body, mesh=mesh, in_specs=placed, out_specs=P("ctx", "tp"), check_vma=False)
```

profile of v0, /device:TPU:101, one launch (start us, length us, event | category | flops | bytes accessed | tf_op | source)
XLA Modules:
  0.0 223.3 jit_solution(10324930232183669582)
XLA Ops:
  0.0 0.0 copy-start.5
  0.0 0.9 copy-done.5
  0.9 0.9 copy-done.6
  1.9 0.8 collective-permute-start
  2.6 1.3 collective-permute-start.1
  3.9 0.0 collective-permute-done.two_ref.refs_0_.refs_5_
  4.0 1.3 collective-permute-start.3
  5.3 0.0 copy-done.7
  5.3 0.0 copy-start
  5.3 5.1 %recur.1 = (f32[512,768]{1,0:T(8,128)S(1)}, f32[512,128]{1,0:T(8,128)S(1)}, f32[776,128]{1,0:T(8,128)S(1)}) custom-call(bf16[512,768]{1,0:T(8,128)(2,1)} %query_hbm.1, bf16[512,768]{1,0:T(8,128)(2,1)} %k_hbm.1, bf16[512,768]{1,0:T(8,128)(2,1)} %v_hbm.1, f32[6,512]{1,0:T(8,128)S(1)} %bitcast.2), custom_call_target="tpu_custom_call" | custom-call | flops 200000000 | bytes 200000 | tf_op jit(solution)/shard_map/recur/pallas_call | solution.py:91
  10.4 0.0 copy-start.1
  10.4 1.2 copy-done.1
  11.6 0.7 copy-done.3
  12.3 1.6 collective-permute-done.1.refs_1_.refs_6_
  13.9 0.8 collective-permute-start.4
  14.7 1.4 collective-permute-done.4.other_ref.core_ref
  16.1 0.1 join.2.own_ref
  16.2 0.0 collective-permute-done.3.refs_3_.refs_8_
  16.2 0.5 collective-permute-start.5
  16.6 1.3 collective-permute-start.7
  17.9 4.2 %collective-permute-start.8 = (bf16[1024,256]{1,0:T(8,128)(2,1)S(1)}, bf16[1024,256]{1,0:T(8,128)(2,1)S(1)}, u32[]{:S(2)}, u32[]{:S(2)}) collective-permute-start(bf16[1024,256]{1,0:T(8,128)(2,1)S(1)} %collective-permute-done.3.refs_3_.refs_8_), channel_id=1, source_target_pairs={{32,48},{48,32},{64,80},{80,64},{96,112},{104,120},{112,96},{120,1... | collective-permute-start | bytes 1572872 | tf_op jit(solution)/shard_map/ppermute | solution.py:447
  22.1 0.7 collective-permute-start.6
  22.9 0.1 collective-permute-start.2
  23.0 1.4 collective-permute-done.2.refs_2_.refs_7_
  24.4 0.0 collective-permute-done.5.refs_4_.refs_9_
  24.4 0.0 copy-done
  24.4 15.6 %attend_first.1 = (f32[512,768]{1,0:T(8,128)S(1)}, f32[512,128]{1,0:T(8,128)S(1)}, bf16[32,128]{1,0:T(8,128)(2,1)S(1)}) custom-call(s32[1]{0:T(128)} %bitcast.mine_ref, bf16[512,768]{1,0:T(8,128)(2,1)S(1)} %copy-done, bf16[512,256]{1,0:T(8,128)(2,1)S(1)} %beside.1.one_ref.own_ref, bf16[512,256]{1,0:T(8,128)(2,1)S(1)} %collective-permute-done.two_ref.refs_0_.refs_5_, ...), custom_call_target="tpu_custom_call" | custom-call | flops 200000000 | bytes 200000 | tf_op jit(solution)/shard_map/attend_first/pallas_call | solution.py:361
  40.0 0.0 collective-permute-done.7.refs_5_.refs_12_
  40.0 3.8 %collective-permute-done.6.other_ref.chip_ref = f32[776,128]{1,0:T(8,128)S(1)} collective-permute-done((f32[776,128]{1,0:T(8,128)S(1)}, f32[776,128]{1,0:T(8,128)S(1)}, u32[]{:S(2)}, u32[]{:S(2)}) %collective-permute-start.6) | collective-permute-done | bytes 397344 | tf_op jit(solution)/shard_map/ppermute | solution.py:447
  43.8 0.0 collective-permute-done.8.refs_3_.refs_10_
  43.8 0.4 collective-permute-start.10
  44.2 0.1 collective-permute-start.9
  44.3 4.1 %collective-permute-start.11 = (bf16[1024,256]{1,0:T(8,128)(2,1)S(1)}, bf16[1024,256]{1,0:T(8,128)(2,1)S(1)}, u32[]{:S(2)}, u32[]{:S(2)}) collective-permute-start(bf16[1024,256]{1,0:T(8,128)(2,1)S(1)} %collective-permute-done.7.refs_5_.refs_12_), channel_id=1, source_target_pairs={{72,88},{88,72},{104,120},{120,104},{73,89},{89,73},{105,121},{121... | collective-permute-start | bytes 1572872 | tf_op jit(solution)/shard_map/ppermute | solution.py:447
  48.4 0.1 join.3
  48.5 1.3 collective-permute-start.12
  49.8 1.3 collective-permute-start.13
  51.1 0.0 collective-permute-done.10.refs_6_.refs_13_
  51.1 0.0 collective-permute-done.9.refs_4_.refs_11_
  51.1 12.4 %attend_middle.1 = (f32[512,768]{1,0:T(8,128)S(1)}, f32[512,128]{1,0:T(8,128)S(1)}, bf16[32,128]{1,0:T(8,128)(2,1)S(1)}) custom-call(s32[1]{0:T(128)} %bitcast.mine_ref, bf16[512,768]{1,0:T(8,128)(2,1)S(1)} %copy-done, bf16[512,256]{1,0:T(8,128)(2,1)S(1)} %beside.1.one_ref.own_ref, f32[512,768]{1,0:T(8,128)S(1)} %get-tuple-element.56.refs_0_, ...), custom_call_target="tpu_custom_call" | custom-call | flops 200000000 | bytes 200000 | tf_op jit(solution)/shard_map/attend_middle/pallas_call | solution.py:361
  63.5 0.0 collective-permute-done.12.behind_ref
  63.5 0.0 collective-permute-done.13.beyond_ref
  63.6 0.0 collective-permute-done.11.refs_3_
  63.6 0.1 collective-permute-start.14
  63.7 0.1 hand.1.kept_ref
  63.7 0.0 copy-start.2
  63.8 0.0 copy-start.4
  63.8 0.0 copy-start.9
  63.8 0.6 collective-permute-start.15
  64.3 1.2 collective-permute-done.14.refs_4_
  65.6 146.1 %attend_last.1 = (bf16[512,768]{1,0:T(8,128)(2,1)S(1)}, f32[8,512]{1,0:T(8,128)S(1)}) custom-call(s32[1]{0:T(128)} %bitcast.mine_ref, bf16[512,768]{1,0:T(8,128)(2,1)S(1)} %copy-done, bf16[512,256]{1,0:T(8,128)(2,1)S(1)} %beside.1.one_ref.own_ref, f32[512,768]{1,0:T(8,128)S(1)} %get-tuple-element.70.refs_0_, f32[512,128]{1,0:T(8,128)S(1)} %get-tuple-element.71.refs_1_, ...), custom_call_target="tpu_custom_call" | custom-call | flops 200000000 | bytes 200000 | tf_op jit(solution)/shard_map/attend_last/pallas_call | solution.py:361
  211.7 0.0 collective-permute-done.15.handed_ref
  211.7 0.0 collective-permute-start.16
  211.7 0.0 copy-done.2
  211.7 0.0 copy-done.4
  211.7 0.0 copy-done.9
  211.7 0.0 copy-start.8
  211.7 2.5 %carry.1.linear_ref = f32[512,768]{1,0:T(8,128)S(1)} custom-call(s32[1]{0:T(128)} %bitcast.mine_ref, bf16[512,768]{1,0:T(8,128)(2,1)} %query_hbm.1, f32[512,768]{1,0:T(8,128)S(1)} %copy-done.2, f32[512,128]{1,0:T(8,128)S(1)} %copy-done.4, f32[776,128]{1,0:T(8,128)S(1)} %hand.1.kept_ref, f32[776,128]{1,0:T(8,128)S(1)} %collective-permute-done.15.handed_ref, ...), custom_call_target="tpu_custom_call" | custom-call | flops 200000000 | bytes 200000 | tf_op jit(solution)/shard_map/carry/pallas_call | solution.py:419
  214.2 0.4 collective-permute-done.16
  214.6 1.9 collective-permute-start.17
  216.5 1.1 collective-permute-done.17
  217.6 2.6 %collective-permute-start.18 = (f32[8,512]{1,0:T(8,128)S(1)}, f32[8,512]{1,0:T(8,128)S(1)}, u32[]{:S(2)}, u32[]{:S(2)}) collective-permute-start(f32[8,512]{1,0:T(8,128)S(1)} %add.7.square_ref), channel_id=1, source_target_pairs={{0,4},{1,5},{2,6},{3,7},{4,0},{5,1},{6,2},{7,3},{8,12},{9,13},{10,... | collective-permute-start | bytes 49160 | tf_op jit(solution)/shard_map/ppermute | solution.py:546
  220.3 1.5 collective-permute-done.18.other_ref
  221.7 0.0 copy-done.8
  221.7 1.5 finish.1
  (7 shorter events, 0.1 us)
Async XLA Ops:
  0.0 0.9 copy-start.5
  0.9 0.9 copy-start.6
  1.8 3.5 %copy-start.7 = (f32[512,6]{0,1:T(8,128)S(1)}, f32[512,6]{0,1:T(8,128)}, u32[]{:S(2)}) copy-start(f32[512,6]{0,1:T(8,128)} %param.15) | copy-start | bytes 36868
  1.9 2.0 collective-permute-start
  2.6 11.3 %collective-permute-start.1 = (bf16[512,256]{1,0:T(8,128)(2,1)S(1)}, bf16[512,256]{1,0:T(8,128)(2,1)S(1)}, u32[]{:S(2)}, u32[]{:S(2)}) collective-permute-start(bf16[512,256]{1,0:T(8,128)(2,1)S(1)} %beside.1.one_ref.own_ref), channel_id=1, source_target_pairs={{0,16},{8,24},{16,0},{24,8},{32,48},{40,56},{64,80},{72,88},{96,11... | collective-permute-start | bytes 786440 | tf_op jit(solution)/shard_map/ppermute | solution.py:447
  4.0 12.2 %collective-permute-start.3 = (bf16[1024,256]{1,0:T(8,128)(2,1)S(1)}, bf16[1024,256]{1,0:T(8,128)(2,1)S(1)}, u32[]{:S(2)}, u32[]{:S(2)}) collective-permute-start(bf16[1024,256]{1,0:T(8,128)(2,1)S(1)} %stack.1), channel_id=1, source_target_pairs={{0,32},{16,48},{32,64},{48,80},{64,96},{80,112},{8,104},{24,120},{... | collective-permute-start | bytes 1572872 | tf_op jit(solution)/shard_map/ppermute | solution.py:447
  5.3 19.2 %copy-start = (bf16[512,768]{1,0:T(8,128)(2,1)S(1)}, bf16[512,768]{1,0:T(8,128)(2,1)}, u32[]{:S(2)}) copy-start(bf16[512,768]{1,0:T(8,128)(2,1)} %query_ref.5) | copy-start | bytes 2359300
  10.4 1.2 copy-start.1
  11.6 0.7 copy-start.3
  13.9 2.2 collective-permute-start.4
  16.2 8.2 %collective-permute-start.5 = (bf16[1024,256]{1,0:T(8,128)(2,1)S(1)}, bf16[1024,256]{1,0:T(8,128)(2,1)S(1)}, u32[]{:S(2)}, u32[]{:S(2)}) collective-permute-start(bf16[1024,256]{1,0:T(8,128)(2,1)S(1)} %collective-permute-done.3.refs_3_.refs_8_), channel_id=1, source_target_pairs={{0,8},{8,0},{16,24},{24,16},{32,40},{40,32},{48,56},{56,48},{64,72... | collective-permute-start | bytes 1572872 | tf_op jit(solution)/shard_map/ppermute | solution.py:447
  16.6 23.4 %collective-permute-start.7 = (bf16[1024,256]{1,0:T(8,128)(2,1)S(1)}, bf16[1024,256]{1,0:T(8,128)(2,1)S(1)}, u32[]{:S(2)}, u32[]{:S(2)}) collective-permute-start(bf16[1024,256]{1,0:T(8,128)(2,1)S(1)} %stack.1), channel_id=1, source_target_pairs={{8,72},{24,88},{40,104},{56,120},{9,73},{25,89},{41,105},{57,121},... | collective-permute-start | bytes 1572872 | tf_op jit(solution)/shard_map/ppermute | solution.py:447
  17.9 25.9 %collective-permute-start.8 = (bf16[1024,256]{1,0:T(8,128)(2,1)S(1)}, bf16[1024,256]{1,0:T(8,128)(2,1)S(1)}, u32[]{:S(2)}, u32[]{:S(2)}) collective-permute-start(bf16[1024,256]{1,0:T(8,128)(2,1)S(1)} %collective-permute-done.3.refs_3_.refs_8_), channel_id=1, source_target_pairs={{32,48},{48,32},{64,80},{80,64},{96,112},{104,120},{112,96},{120,1... | collective-permute-start | bytes 1572872 | tf_op jit(solution)/shard_map/ppermute | solution.py:447
  22.1 21.6 %collective-permute-start.6 = (f32[776,128]{1,0:T(8,128)S(1)}, f32[776,128]{1,0:T(8,128)S(1)}, u32[]{:S(2)}, u32[]{:S(2)}) collective-permute-start(f32[776,128]{1,0:T(8,128)S(1)} %join.2.own_ref), channel_id=1, source_target_pairs={{0,16},{8,24},{16,0},{24,8},{32,48},{40,56},{48,32},{56,40},{64,80... | collective-permute-start | bytes 1191944 | tf_op jit(solution)/shard_map/ppermute | solution.py:447
  22.9 1.5 collective-permute-start.2
  43.8 7.3 %collective-permute-start.10 = (bf16[1024,256]{1,0:T(8,128)(2,1)S(1)}, bf16[1024,256]{1,0:T(8,128)(2,1)S(1)}, u32[]{:S(2)}, u32[]{:S(2)}) collective-permute-start(bf16[1024,256]{1,0:T(8,128)(2,1)S(1)} %collective-permute-done.7.refs_5_.refs_12_), channel_id=1, source_target_pairs={{0,8},{8,0},{16,24},{24,16},{32,40},{40,32},{48,56},{56,48},{64,72... | collective-permute-start | bytes 1572872 | tf_op jit(solution)/shard_map/ppermute | solution.py:447
  44.2 6.9 %collective-permute-start.9 = (bf16[1024,256]{1,0:T(8,128)(2,1)S(1)}, bf16[1024,256]{1,0:T(8,128)(2,1)S(1)}, u32[]{:S(2)}, u32[]{:S(2)}) collective-permute-start(bf16[1024,256]{1,0:T(8,128)(2,1)S(1)} %collective-permute-done.8.refs_3_.refs_10_), channel_id=1, source_target_pairs={{0,8},{8,0},{16,24},{24,16},{32,40},{40,32},{48,56},{56,48},{64,72... | collective-permute-start | bytes 1572872 | tf_op jit(solution)/shard_map/ppermute | solution.py:447
  44.3 19.3 %collective-permute-start.11 = (bf16[1024,256]{1,0:T(8,128)(2,1)S(1)}, bf16[1024,256]{1,0:T(8,128)(2,1)S(1)}, u32[]{:S(2)}, u32[]{:S(2)}) collective-permute-start(bf16[1024,256]{1,0:T(8,128)(2,1)S(1)} %collective-permute-done.7.refs_5_.refs_12_), channel_id=1, source_target_pairs={{72,88},{88,72},{104,120},{120,104},{73,89},{89,73},{105,121},{121... | collective-permute-start | bytes 1572872 | tf_op jit(solution)/shard_map/ppermute | solution.py:447
  48.5 15.1 %collective-permute-start.12 = (f32[776,128]{1,0:T(8,128)S(1)}, f32[776,128]{1,0:T(8,128)S(1)}, u32[]{:S(2)}, u32[]{:S(2)}) collective-permute-start(f32[776,128]{1,0:T(8,128)S(1)} %join.3), channel_id=1, source_target_pairs={{0,32},{16,48},{32,64},{48,80},{64,96},{80,112},{8,104},{24,120},{... | collective-permute-start | bytes 1191944 | tf_op jit(solution)/shard_map/ppermute | solution.py:447
  49.8 13.8 %collective-permute-start.13 = (f32[776,128]{1,0:T(8,128)S(1)}, f32[776,128]{1,0:T(8,128)S(1)}, u32[]{:S(2)}, u32[]{:S(2)}) collective-permute-start(f32[776,128]{1,0:T(8,128)S(1)} %join.3), channel_id=1, source_target_pairs={{8,72},{24,88},{40,104},{56,120},{9,73},{25,89},{41,105},{57,121},... | collective-permute-start | bytes 1191944 | tf_op jit(solution)/shard_map/ppermute | solution.py:447
  63.6 2.0 collective-permute-start.14
  63.7 147.9 %copy-start.2 = (f32[512,768]{1,0:T(8,128)S(1)}, f32[512,768]{1,0:T(8,128)}, u32[]{:S(2)}) copy-start(f32[512,768]{1,0:T(8,128)} %copy-done.1) | copy-start | bytes 4718596
  63.8 147.9 %copy-start.4 = (f32[512,128]{1,0:T(8,128)S(1)}, f32[512,128]{1,0:T(8,128)}, u32[]{:S(2)}) copy-start(f32[512,128]{1,0:T(8,128)} %copy-done.3) | copy-start | bytes 786436
  63.8 147.9 %copy-start.9 = (f32[768]{0:T(1024)S(1)}, f32[768]{0:T(1024)}, u32[]{:S(2)}) copy-start(f32[768]{0:T(1024)} %gain_ref.2) | copy-start | bytes 9220
  63.8 147.9 %collective-permute-start.15 = (f32[776,128]{1,0:T(8,128)S(1)}, f32[776,128]{1,0:T(8,128)S(1)}, u32[]{:S(2)}, u32[]{:S(2)}) collective-permute-start(f32[776,128]{1,0:T(8,128)S(1)} %hand.1.kept_ref), channel_id=1, source_target_pairs={{0,8},{8,0},{16,24},{24,16},{32,40},{40,32},{48,56},{56,48},{64,72... | collective-permute-start | bytes 1191944 | tf_op jit(solution)/shard_map/ppermute | solution.py:447
  211.7 2.9 %collective-permute-start.16 = (f32[8,512]{1,0:T(8,128)S(1)}, f32[8,512]{1,0:T(8,128)S(1)}, u32[]{:S(2)}, u32[]{:S(2)}) collective-permute-start(f32[8,512]{1,0:T(8,128)S(1)} %get-tuple-element.80), channel_id=1, source_target_pairs={{0,1},{1,0},{2,3},{3,2},{4,5},{5,4},{6,7},{7,6},{8,9},{9,8},{10,11... | collective-permute-start | bytes 49160 | tf_op jit(solution)/shard_map/ppermute | solution.py:546
  211.7 10.0 %copy-start.8 = (f32[768]{0:T(1024)S(1)}, f32[768]{0:T(1024)}, u32[]{:S(2)}) copy-start(f32[768]{0:T(1024)} %gain_ref.3) | copy-start | bytes 9220
  214.6 3.1 %collective-permute-start.17 = (f32[8,512]{1,0:T(8,128)S(1)}, f32[8,512]{1,0:T(8,128)S(1)}, u32[]{:S(2)}, u32[]{:S(2)}) collective-permute-start(f32[8,512]{1,0:T(8,128)S(1)} %add.6), channel_id=1, source_target_pairs={{0,2},{1,3},{2,0},{3,1},{4,6},{5,7},{6,4},{7,5},{8,10},{9,11},{10,... | collective-permute-start | bytes 49160 | tf_op jit(solution)/shard_map/ppermute | solution.py:546
  217.6 4.1 %collective-permute-start.18 = (f32[8,512]{1,0:T(8,128)S(1)}, f32[8,512]{1,0:T(8,128)S(1)}, u32[]{:S(2)}, u32[]{:S(2)}) collective-permute-start(f32[8,512]{1,0:T(8,128)S(1)} %add.7.square_ref), channel_id=1, source_target_pairs={{0,4},{1,5},{2,6},{3,7},{4,0},{5,1},{6,2},{7,3},{8,12},{9,13},{10,... | collective-permute-start | bytes 49160 | tf_op jit(solution)/shard_map/ppermute | solution.py:546
where the time goes:
time: 224 us; the launch traced here: 223 us
  Pallas kernels  184 us (82%)
  starting transfers between devices  23.3 us (10%)
  waiting for transfers between devices  12.4 us (6%)
  local copies, waits for them, and re-layouts  3.73 us (2%)
    pallas_call x3, Pallas kernels, attend(): pl.pallas_call(functools.partial(attend_kernel, first, last, numbers_of,...  174 us
    ppermute x16, starting transfers between devices, move(): return lax.ppermute(value, 'ctx', pairs)  18.8 us
    ppermute x16, waiting for transfers between devices, move(): return lax.ppermute(value, 'ctx', pairs)  9.42 us
    pallas_call x1, Pallas kernels, recur(): pl.pallas_call(recur_kernel, out_shape=(jax.ShapeDtypeStruct((ROWS, HEADS...  5.1 us
    ppermute x3, starting transfers between devices, over(): return lax.ppermute(value, 'tp', [(i, i ^ bit) for i in range(8)])  4.55 us
  transfers between devices with their start and end apart: 19, of which 8 were waited for; matrix products, arithmetic and copies ran while one was open for 0% of the time, Pallas kernels for 81%

commit v1 on v0

--- a/solution.py
+++ b/solution.py
@@ -460,8 +460,9 @@
         for array in (lh_query, lh_key, lh_value, att_query, att_key, att_value)
     ]
     near_query = att_query
-    lh_query, lh_key, lh_value = [
-        pltpu.with_memory_space_constraint(array, pltpu.HBM) for array in (lh_query, lh_key, lh_value)
+    lh_query, lh_key, lh_value, att_key, att_value = [
+        pltpu.with_memory_space_constraint(array, pltpu.HBM)
+        for array in (lh_query, lh_key, lh_value, att_key, att_value)
     ]
     own = beside(att_key, att_value)
     across = move(own, [(i, i ^ 2) for i in every if i < 4 or i % 4 < 2])
@@ -471,13 +472,10 @@
     behind = move(chip, last_plane)
 
     local, grow, message = recur(lh_query, lh_key, lh_value, lh_step)
-    chip, across, message = tied(chip, across, message)
+    chip, across, behind, message = tied(chip, across, behind, message)
     beyond = move(chip, plane_before)
     across_near = move(across, sibling)
     first = move(message, sibling)
-    of_chip = join(1, place, message, first)
-    other_chip = move(of_chip, sideways)
-    behind, of_chip = tied(behind, of_chip)
     behind_near = move(behind, sibling)
     level = move(behind, [(i, j) for i, j in sideways if (i % 2 == 0 and i >= 4) or i >= 12])
 
@@ -513,22 +511,22 @@
 
     first_blocks = [near, across, across_near, behind, behind_near]
     carry = attend(place, near_query, own, None, first_blocks, first_numbers)
-    carry, other_chip, beyond, level = tied(carry, other_chip, beyond, level)
+    carry, first, beyond, level = tied(carry, first, beyond, level)
+    of_chip = join(1, place, message, first)
+    other_chip = move(of_chip, sideways)
     level_beyond = move(beyond, [(i, j) for i, j in sideways if i % 2 == 1 and i >= 8])
     beyond_near = move(beyond, sibling)
     level_near = move(level, sibling)
+    middle_blocks = [level, level_near, beyond, beyond_near]
+    middle_blocks, of_chip = tied(middle_blocks, of_chip)
+    carry = attend(place, near_query, own, carry, middle_blocks, middle_numbers)
+    carry, level_beyond, other_chip = tied(carry, level_beyond, other_chip)
+    level_beyond_near = move(level_beyond, sibling)
     of_plane = join(2, place, of_chip, other_chip)
     state_behind = move(of_plane, last_plane)
     state_beyond = move(of_plane, plane_before)
-    middle_blocks = [level, level_near, beyond, beyond_near]
-    middle_blocks, of_plane = tied(middle_blocks, of_plane)
-    carry = attend(place, near_query, own, carry, middle_blocks, middle_numbers)
-    carry, level_beyond, state_behind, state_beyond = tied(carry, level_beyond, state_behind, state_beyond)
-    level_beyond_near = move(level_beyond, sibling)
-    kept = hand(place, state_behind, state_beyond)
-    handed = move(kept, sibling)
     last_blocks = [level_beyond, level_beyond_near]
-    last_blocks, kept = tied(last_blocks, kept)
+    last_blocks, of_plane = tied(last_blocks, of_plane)
     attention, squares = attend(
         place,
         near_query,
@@ -539,18 +537,19 @@
         first_blocks + middle_blocks,
         lambda mine: first_numbers(mine) + middle_numbers(mine),
     )
-    squares, handed = tied(squares, handed)
-    linear = carry_in(place, lh_query, local, grow, kept, handed, other_chip, first, lh_gain)
 
     def over(value, bit):
         return lax.ppermute(value, "tp", [(i, i ^ bit) for i in range(8)])
 
-    first_round = over(squares, 1)
-    first_round, linear = tied(first_round, linear)
-    squares = squares + first_round
-    squares = squares + over(squares, 2)
+    squares, state_behind, state_beyond = tied(squares, state_behind, state_beyond)
+    others = [over(squares, bit) for bit in (2, 4, 6)]
+    kept = hand(place, state_behind, state_beyond)
+    handed = move(kept, sibling)
+    linear = carry_in(place, lh_query, local, grow, kept, handed, other_chip, first, lh_gain)
+    others, linear = tied(others, linear)
+    squares = squares + others[0] + others[1] + others[2]
     features = HEADS * HD * lax.axis_size("tp")
-    return finish(float(features), attention, squares, over(squares, 4), linear, att_gain)
+    return finish(float(features), attention, squares, over(squares, 1), linear, att_gain)
 
 
 def solution(mesh):

time: 224 us -> 227 us (1.013); the launches traced: 223 us -> 224 us
  Pallas kernels: 184 us -> 190 us
  waiting for transfers between devices: 12.4 us -> 7.96 us
    ppermute x16, waiting for transfers between devices: 9.42 us -> 6.53 us  [move(): return lax.ppermute(value, 'ctx', pairs)]
    pallas_call x3, Pallas kernels: 174 us -> 176 us  [attend(): pl.pallas_call(functools.partial(attend_kernel, first, last, numbers_of,...]
    ppermute x3 -> x4, starting transfers between devices: 4.55 us -> 5.75 us  [over(): return lax.ppermute(value, 'tp', [(i, i ^ bit) for i in range(8)])]
  transfers between devices with their start and end apart: 19 -> 20, of which waited for: 8 -> 6; matrix products, arithmetic and copies ran while one was open for 0% -> 0% of each run, Pallas kernels for 81% -> 83%
where the time goes in v1:
time: 227 us; the launch traced here: 224 us
  Pallas kernels  190 us (84%)
  starting transfers between devices  24.1 us (11%)
  waiting for transfers between devices  7.96 us (4%)
    pallas_call x3, Pallas kernels, attend(): pl.pallas_call(functools.partial(attend_kernel, first, last, numbers_of,...  176 us
    ppermute x16, starting transfers between devices, move(): return lax.ppermute(value, 'ctx', pairs)  18.4 us
    ppermute x16, waiting for transfers between devices, move(): return lax.ppermute(value, 'ctx', pairs)  6.53 us
    pallas_call x1, Pallas kernels, recur(): pl.pallas_call(recur_kernel, out_shape=(jax.ShapeDtypeStruct((ROWS, HEADS...  5.79 us
    ppermute x4, starting transfers between devices, over(): return lax.ppermute(value, 'tp', [(i, i ^ bit) for i in range(8)])  5.75 us
  transfers between devices with their start and end apart: 20, of which 6 were waited for; matrix products, arithmetic and copies ran while one was open for 0% of the time, Pallas kernels for 83%

profile of v1, /device:TPU:101, one launch (start us, length us, event | category | flops | bytes accessed | tf_op | source)
XLA Modules:
  0.0 223.8 jit_solution(15994700108382603854)
XLA Ops:
  0.0 1.0 beside.1.one_ref.own_ref
  1.0 0.0 copy-start
  1.0 0.8 collective-permute-start
  1.8 1.2 collective-permute-done.two_ref.refs_0_.refs_5_
  3.0 0.8 stack.1
  3.8 1.3 collective-permute-start.2
  5.1 1.3 collective-permute-start.1
  6.4 0.0 copy-done.5
  6.4 5.8 %recur.1 = (f32[512,768]{1,0:T(8,128)S(1)}, f32[512,128]{1,0:T(8,128)S(1)}, f32[776,128]{1,0:T(8,128)}) custom-call(bf16[512,768]{1,0:T(8,128)(2,1)} %query_hbm.1, bf16[512,768]{1,0:T(8,128)(2,1)} %k_hbm.1, bf16[512,768]{1,0:T(8,128)(2,1)} %v_hbm.1, f32[6,512]{1,0:T(8,128)S(1)} %bitcast.2), custom_call_target="tpu_custom_call" | custom-call | flops 200000000 | bytes 200000 | tf_op jit(solution)/shard_map/recur/pallas_call | solution.py:91
  12.2 1.2 copy-done.1
  13.4 0.7 copy-done.3
  14.1 2.0 collective-permute-done.1.refs_1_.refs_6_
  16.1 0.0 collective-permute-done.2.refs_3_.refs_8_
  16.1 1.2 collective-permute-start.4
  17.3 3.6 %collective-permute-start.7 = (bf16[1024,256]{1,0:T(8,128)(2,1)S(1)}, bf16[1024,256]{1,0:T(8,128)(2,1)S(1)}, u32[]{:S(2)}, u32[]{:S(2)}) collective-permute-start(bf16[1024,256]{1,0:T(8,128)(2,1)S(1)} %collective-permute-done.2.refs_3_.refs_8_), channel_id=1, source_target_pairs={{32,48},{48,32},{64,80},{80,64},{96,112},{104,120},{112,96},{120,1... | collective-permute-start | bytes 1572872 | tf_op jit(solution)/shard_map/ppermute | solution.py:447
  20.9 1.3 collective-permute-start.6
  22.2 0.1 collective-permute-start.5
  22.3 0.5 collective-permute-start.3
  22.8 1.9 collective-permute-done.3.refs_2_.refs_7_
  24.8 0.0 collective-permute-done.4.refs_4_.refs_9_
  24.8 0.0 copy-done
  24.8 16.7 %attend_first.1 = (f32[512,768]{1,0:T(8,128)S(1)}, f32[512,128]{1,0:T(8,128)S(1)}, bf16[32,128]{1,0:T(8,128)(2,1)S(1)}) custom-call(s32[1]{0:T(128)} %bitcast.mine_ref, bf16[512,768]{1,0:T(8,128)(2,1)S(1)} %copy-done, bf16[512,256]{1,0:T(8,128)(2,1)S(1)} %beside.1.one_ref.own_ref, bf16[512,256]{1,0:T(8,128)(2,1)S(1)} %collective-permute-done.two_ref.refs_0_.refs_5_, ...), custom_call_target="tpu_custom_call" | custom-call | flops 200000000 | bytes 200000 | tf_op jit(solution)/shard_map/attend_first/pallas_call | solution.py:361
  41.5 0.0 collective-permute-done.5.other_ref.core_ref
  41.5 0.0 collective-permute-done.7.refs_3_.refs_10_
  41.5 0.0 collective-permute-done.6.refs_5_.refs_12_
  41.5 0.1 collective-permute-start.8
  41.6 0.5 collective-permute-start.9
  42.1 1.9 collective-permute-start.10
  44.0 1.2 join.2.own_ref
  45.2 3.0 %collective-permute-start.11 = (f32[776,128]{1,0:T(8,128)S(1)}, f32[776,128]{1,0:T(8,128)S(1)}, u32[]{:S(2)}, u32[]{:S(2)}) collective-permute-start(f32[776,128]{1,0:T(8,128)S(1)} %join.2.own_ref), channel_id=1, source_target_pairs={{0,16},{8,24},{16,0},{24,8},{32,48},{40,56},{48,32},{56,40},{64,80... | collective-permute-start | bytes 1191944 | tf_op jit(solution)/shard_map/ppermute | solution.py:447
  48.3 0.0 collective-permute-done.8.refs_4_.refs_11_
  48.3 0.0 collective-permute-done.9.refs_6_.refs_13_
  48.3 12.4 %attend_middle.1 = (f32[512,768]{1,0:T(8,128)S(1)}, f32[512,128]{1,0:T(8,128)S(1)}, bf16[32,128]{1,0:T(8,128)(2,1)S(1)}) custom-call(s32[1]{0:T(128)} %bitcast.mine_ref, bf16[512,768]{1,0:T(8,128)(2,1)S(1)} %copy-done, bf16[512,256]{1,0:T(8,128)(2,1)S(1)} %beside.1.one_ref.own_ref, f32[512,768]{1,0:T(8,128)S(1)} %get-tuple-element.57.refs_0_, ...), custom_call_target="tpu_custom_call" | custom-call | flops 200000000 | bytes 200000 | tf_op jit(solution)/shard_map/attend_middle/pallas_call | solution.py:361
  60.7 1.4 collective-permute-done.11.other_ref.chip_ref
  62.0 0.0 collective-permute-done.10.refs_3_
  62.0 0.0 collective-permute-start.12
  62.0 0.1 join.3
  62.1 0.0 copy-start.4
  62.1 0.0 copy-start.7
  62.2 1.4 collective-permute-start.13
  63.6 1.3 collective-permute-start.14
  64.9 0.0 collective-permute-done.12.refs_4_
  64.9 0.0 copy-start.2
  64.9 147.3 %attend_last.1 = (bf16[512,768]{1,0:T(8,128)(2,1)S(1)}, f32[8,512]{1,0:T(8,128)S(1)}) custom-call(s32[1]{0:T(128)} %bitcast.mine_ref, bf16[512,768]{1,0:T(8,128)(2,1)S(1)} %copy-done, bf16[512,256]{1,0:T(8,128)(2,1)S(1)} %beside.1.one_ref.own_ref, f32[512,768]{1,0:T(8,128)S(1)} %get-tuple-element.70.refs_0_, f32[512,128]{1,0:T(8,128)S(1)} %get-tuple-element.71.refs_1_, ...), custom_call_target="tpu_custom_call" | custom-call | flops 200000000 | bytes 200000 | tf_op jit(solution)/shard_map/attend_last/pallas_call | solution.py:361
  212.2 0.0 collective-permute-done.13.behind_ref
  212.2 0.0 collective-permute-done.14.beyond_ref
  212.2 0.1 hand.1.kept_ref
  212.3 0.1 collective-permute-start.18
  212.4 0.1 collective-permute-start.15
  212.5 3.0 %collective-permute-start.16 = (f32[8,512]{1,0:T(8,128)S(1)}, f32[8,512]{1,0:T(8,128)S(1)}, u32[]{:S(2)}, u32[]{:S(2)}) collective-permute-start(f32[8,512]{1,0:T(8,128)S(1)} %get-tuple-element.80), channel_id=1, source_target_pairs={{0,4},{1,5},{2,6},{3,7},{4,0},{5,1},{6,2},{7,3},{8,12},{9,13},{10,... | collective-permute-start | bytes 49160 | tf_op jit(solution)/shard_map/ppermute | solution.py:542
  215.5 0.9 collective-permute-start.17
  216.3 0.0 collective-permute-done.18.handed_ref
  216.3 0.0 copy-done.4
  216.3 0.0 copy-done.7
  216.3 0.0 copy-done.2
  216.3 0.0 copy-start.6
  216.4 2.6 %carry.1.linear_ref = f32[512,768]{1,0:T(8,128)S(1)} custom-call(s32[1]{0:T(128)} %bitcast.mine_ref, bf16[512,768]{1,0:T(8,128)(2,1)} %query_hbm.1, f32[512,768]{1,0:T(8,128)S(1)} %copy-done.2, f32[512,128]{1,0:T(8,128)S(1)} %copy-done.4, f32[776,128]{1,0:T(8,128)S(1)} %hand.1.kept_ref, f32[776,128]{1,0:T(8,128)S(1)} %collective-permute-done.18.handed_ref, ...), custom_call_target="tpu_custom_call" | custom-call | flops 200000000 | bytes 200000 | tf_op jit(solution)/shard_map/carry/pallas_call | solution.py:419
  218.9 0.0 collective-permute-done.15
  219.0 0.0 collective-permute-done.16
  219.0 0.3 collective-permute-done.17
  219.3 1.8 collective-permute-start.19
  221.1 1.1 collective-permute-done.19.other_ref
  222.2 0.0 copy-done.6
  222.2 1.5 finish.1
  (4 shorter events, 0.0 us)
Async XLA Ops:
  0.0 6.4 %copy-start.5 = (f32[512,6]{0,1:T(8,128)S(1)}, f32[512,6]{0,1:T(8,128)}, u32[]{:S(2)}) copy-start(f32[512,6]{0,1:T(8,128)} %param.15) | copy-start | bytes 36868
  1.0 23.7 %copy-start = (bf16[512,768]{1,0:T(8,128)(2,1)S(1)}, bf16[512,768]{1,0:T(8,128)(2,1)}, u32[]{:S(2)}) copy-start(bf16[512,768]{1,0:T(8,128)(2,1)} %query_ref.5) | copy-start | bytes 2359300
  1.0 1.9 collective-permute-start
  3.8 12.3 %collective-permute-start.2 = (bf16[1024,256]{1,0:T(8,128)(2,1)}, bf16[1024,256]{1,0:T(8,128)(2,1)S(1)}, u32[]{:S(2)}, u32[]{:S(2)}) collective-permute-start(bf16[1024,256]{1,0:T(8,128)(2,1)} %stack.1), channel_id=1, source_target_pairs={{0,32},{16,48},{32,64},{48,80},{64,96},{80,112},{8,104},{24,120},{... | collective-permute-start | bytes 1572872 | tf_op jit(solution)/shard_map/ppermute | solution.py:447
  5.1 11.0 %collective-permute-start.1 = (bf16[512,256]{1,0:T(8,128)(2,1)S(1)}, bf16[512,256]{1,0:T(8,128)(2,1)}, u32[]{:S(2)}, u32[]{:S(2)}) collective-permute-start(bf16[512,256]{1,0:T(8,128)(2,1)S(1)} %beside.1.one_ref.own_ref), channel_id=1, source_target_pairs={{0,16},{8,24},{16,0},{24,8},{32,48},{40,56},{64,80},{72,88},{96,11... | collective-permute-start | bytes 786440 | tf_op jit(solution)/shard_map/ppermute | solution.py:447
  12.2 1.2 copy-start.1
  13.4 0.7 copy-start.3
  16.1 8.7 %collective-permute-start.4 = (bf16[1024,256]{1,0:T(8,128)(2,1)S(1)}, bf16[1024,256]{1,0:T(8,128)(2,1)S(1)}, u32[]{:S(2)}, u32[]{:S(2)}) collective-permute-start(bf16[1024,256]{1,0:T(8,128)(2,1)S(1)} %collective-permute-done.2.refs_3_.refs_8_), channel_id=1, source_target_pairs={{0,8},{8,0},{16,24},{24,16},{32,40},{40,32},{48,56},{56,48},{64,72... | collective-permute-start | bytes 1572872 | tf_op jit(solution)/shard_map/ppermute | solution.py:447
  17.3 24.2 %collective-permute-start.7 = (bf16[1024,256]{1,0:T(8,128)(2,1)S(1)}, bf16[1024,256]{1,0:T(8,128)(2,1)S(1)}, u32[]{:S(2)}, u32[]{:S(2)}) collective-permute-start(bf16[1024,256]{1,0:T(8,128)(2,1)S(1)} %collective-permute-done.2.refs_3_.refs_8_), channel_id=1, source_target_pairs={{32,48},{48,32},{64,80},{80,64},{96,112},{104,120},{112,96},{120,1... | collective-permute-start | bytes 1572872 | tf_op jit(solution)/shard_map/ppermute | solution.py:447
  20.9 20.6 %collective-permute-start.6 = (bf16[1024,256]{1,0:T(8,128)(2,1)}, bf16[1024,256]{1,0:T(8,128)(2,1)S(1)}, u32[]{:S(2)}, u32[]{:S(2)}) collective-permute-start(bf16[1024,256]{1,0:T(8,128)(2,1)} %stack.1), channel_id=1, source_target_pairs={{8,72},{24,88},{40,104},{56,120},{9,73},{25,89},{41,105},{57,121},... | collective-permute-start | bytes 1572872 | tf_op jit(solution)/shard_map/ppermute | solution.py:447
  22.2 19.3 %collective-permute-start.5 = (f32[776,128]{1,0:T(8,128)}, f32[776,128]{1,0:T(8,128)}, u32[]{:S(2)}, u32[]{:S(2)}) collective-permute-start(f32[776,128]{1,0:T(8,128)} %get-tuple-element.55.own_ref), channel_id=1, source_target_pairs={{0,8},{8,0},{16,24},{24,16},{32,40},{40,32},{48,56},{56,48},{64,72... | collective-permute-start | bytes 1191944 | tf_op jit(solution)/shard_map/ppermute | solution.py:447
  22.3 2.4 %collective-permute-start.3 = (bf16[512,256]{1,0:T(8,128)(2,1)}, bf16[512,256]{1,0:T(8,128)(2,1)}, u32[]{:S(2)}, u32[]{:S(2)}) collective-permute-start(bf16[512,256]{1,0:T(8,128)(2,1)} %collective-permute-done.1.refs_1_.refs_6_), channel_id=1, source_target_pairs={{0,8},{8,0},{16,24},{24,16},{32,40},{40,32},{48,56},{56,48},{64,72... | collective-permute-start | bytes 786440 | tf_op jit(solution)/shard_map/ppermute | solution.py:447
  41.5 6.7 %collective-permute-start.8 = (bf16[1024,256]{1,0:T(8,128)(2,1)S(1)}, bf16[1024,256]{1,0:T(8,128)(2,1)S(1)}, u32[]{:S(2)}, u32[]{:S(2)}) collective-permute-start(bf16[1024,256]{1,0:T(8,128)(2,1)S(1)} %collective-permute-done.7.refs_3_.refs_10_), channel_id=1, source_target_pairs={{0,8},{8,0},{16,24},{24,16},{32,40},{40,32},{48,56},{56,48},{64,72... | collective-permute-start | bytes 1572872 | tf_op jit(solution)/shard_map/ppermute | solution.py:447
  41.6 6.6 %collective-permute-start.9 = (bf16[1024,256]{1,0:T(8,128)(2,1)S(1)}, bf16[1024,256]{1,0:T(8,128)(2,1)S(1)}, u32[]{:S(2)}, u32[]{:S(2)}) collective-permute-start(bf16[1024,256]{1,0:T(8,128)(2,1)S(1)} %collective-permute-done.6.refs_5_.refs_12_), channel_id=1, source_target_pairs={{0,8},{8,0},{16,24},{24,16},{32,40},{40,32},{48,56},{56,48},{64,72... | collective-permute-start | bytes 1572872 | tf_op jit(solution)/shard_map/ppermute | solution.py:447
  42.1 19.9 %collective-permute-start.10 = (bf16[1024,256]{1,0:T(8,128)(2,1)S(1)}, bf16[1024,256]{1,0:T(8,128)(2,1)S(1)}, u32[]{:S(2)}, u32[]{:S(2)}) collective-permute-start(bf16[1024,256]{1,0:T(8,128)(2,1)S(1)} %collective-permute-done.6.refs_5_.refs_12_), channel_id=1, source_target_pairs={{72,88},{88,72},{104,120},{120,104},{73,89},{89,73},{105,121},{121... | collective-permute-start | bytes 1572872 | tf_op jit(solution)/shard_map/ppermute | solution.py:447
  45.2 16.8 %collective-permute-start.11 = (f32[776,128]{1,0:T(8,128)S(1)}, f32[776,128]{1,0:T(8,128)S(1)}, u32[]{:S(2)}, u32[]{:S(2)}) collective-permute-start(f32[776,128]{1,0:T(8,128)S(1)} %join.2.own_ref), channel_id=1, source_target_pairs={{0,16},{8,24},{16,0},{24,8},{32,48},{40,56},{48,32},{56,40},{64,80... | collective-permute-start | bytes 1191944 | tf_op jit(solution)/shard_map/ppermute | solution.py:447
  62.0 2.8 %collective-permute-start.12 = (bf16[1024,256]{1,0:T(8,128)(2,1)S(1)}, bf16[1024,256]{1,0:T(8,128)(2,1)S(1)}, u32[]{:S(2)}, u32[]{:S(2)}) collective-permute-start(bf16[1024,256]{1,0:T(8,128)(2,1)S(1)} %collective-permute-done.10.refs_3_), channel_id=1, source_target_pairs={{0,8},{8,0},{16,24},{24,16},{32,40},{40,32},{48,56},{56,48},{64,72... | collective-permute-start | bytes 1572872 | tf_op jit(solution)/shard_map/ppermute | solution.py:447
  62.1 154.2 %copy-start.4 = (f32[512,128]{1,0:T(8,128)S(1)}, f32[512,128]{1,0:T(8,128)}, u32[]{:S(2)}) copy-start(f32[512,128]{1,0:T(8,128)} %copy-done.3) | copy-start | bytes 786436
  62.1 154.2 %copy-start.7 = (f32[768]{0:T(1024)S(1)}, f32[768]{0:T(1024)}, u32[]{:S(2)}) copy-start(f32[768]{0:T(1024)} %gain_ref.2) | copy-start | bytes 9220
  62.2 150.0 %collective-permute-start.13 = (f32[776,128]{1,0:T(8,128)S(1)}, f32[776,128]{1,0:T(8,128)S(1)}, u32[]{:S(2)}, u32[]{:S(2)}) collective-permute-start(f32[776,128]{1,0:T(8,128)S(1)} %join.3), channel_id=1, source_target_pairs={{0,32},{16,48},{32,64},{48,80},{64,96},{80,112},{8,104},{24,120},{... | collective-permute-start | bytes 1191944 | tf_op jit(solution)/shard_map/ppermute | solution.py:447
  63.6 148.6 %collective-permute-start.14 = (f32[776,128]{1,0:T(8,128)S(1)}, f32[776,128]{1,0:T(8,128)S(1)}, u32[]{:S(2)}, u32[]{:S(2)}) collective-permute-start(f32[776,128]{1,0:T(8,128)S(1)} %join.3), channel_id=1, source_target_pairs={{8,72},{24,88},{40,104},{56,120},{9,73},{25,89},{41,105},{57,121},... | collective-permute-start | bytes 1191944 | tf_op jit(solution)/shard_map/ppermute | solution.py:447
  64.9 151.4 %copy-start.2 = (f32[512,768]{1,0:T(8,128)S(1)}, f32[512,768]{1,0:T(8,128)}, u32[]{:S(2)}) copy-start(f32[512,768]{1,0:T(8,128)} %copy-done.1) | copy-start | bytes 4718596
  212.3 4.0 %collective-permute-start.18 = (f32[776,128]{1,0:T(8,128)S(1)}, f32[776,128]{1,0:T(8,128)S(1)}, u32[]{:S(2)}, u32[]{:S(2)}) collective-permute-start(f32[776,128]{1,0:T(8,128)S(1)} %hand.1.kept_ref), channel_id=1, source_target_pairs={{0,8},{8,0},{16,24},{24,16},{32,40},{40,32},{48,56},{56,48},{64,72... | collective-permute-start | bytes 1191944 | tf_op jit(solution)/shard_map/ppermute | solution.py:447
  212.4 6.6 %collective-permute-start.15 = (f32[8,512]{1,0:T(8,128)S(1)}, f32[8,512]{1,0:T(8,128)S(1)}, u32[]{:S(2)}, u32[]{:S(2)}) collective-permute-start(f32[8,512]{1,0:T(8,128)S(1)} %get-tuple-element.80), channel_id=1, source_target_pairs={{0,2},{1,3},{2,0},{3,1},{4,6},{5,7},{6,4},{7,5},{8,10},{9,11},{10,... | collective-permute-start | bytes 49160 | tf_op jit(solution)/shard_map/ppermute | solution.py:542
  212.5 6.5 %collective-permute-start.16 = (f32[8,512]{1,0:T(8,128)S(1)}, f32[8,512]{1,0:T(8,128)S(1)}, u32[]{:S(2)}, u32[]{:S(2)}) collective-permute-start(f32[8,512]{1,0:T(8,128)S(1)} %get-tuple-element.80), channel_id=1, source_target_pairs={{0,4},{1,5},{2,6},{3,7},{4,0},{5,1},{6,2},{7,3},{8,12},{9,13},{10,... | collective-permute-start | bytes 49160 | tf_op jit(solution)/shard_map/ppermute | solution.py:542
  215.5 3.8 %collective-permute-start.17 = (f32[8,512]{1,0:T(8,128)S(1)}, f32[8,512]{1,0:T(8,128)S(1)}, u32[]{:S(2)}, u32[]{:S(2)}) collective-permute-start(f32[8,512]{1,0:T(8,128)S(1)} %get-tuple-element.80), channel_id=1, source_target_pairs={{0,6},{1,7},{2,4},{3,5},{4,2},{5,3},{6,0},{7,1},{8,14},{9,15},{10,... | collective-permute-start | bytes 49160 | tf_op jit(solution)/shard_map/ppermute | solution.py:542
  216.3 5.9 %copy-start.6 = (f32[768]{0:T(1024)S(1)}, f32[768]{0:T(1024)}, u32[]{:S(2)}) copy-start(f32[768]{0:T(1024)} %gain_ref.3) | copy-start | bytes 9220
  219.3 3.0 %collective-permute-start.19 = (f32[8,512]{1,0:T(8,128)S(1)}, f32[8,512]{1,0:T(8,128)S(1)}, u32[]{:S(2)}, u32[]{:S(2)}) collective-permute-start(f32[8,512]{1,0:T(8,128)S(1)} %add_add_fusion.square_ref), channel_id=1, source_target_pairs={{0,1},{1,0},{2,3},{3,2},{4,5},{5,4},{6,7},{7,6},{8,9},{9,8},{10,11... | collective-permute-start | bytes 49160 | tf_op jit(solution)/shard_map/ppermute | solution.py:542

commit v2 on v1

--- a/solution.py
+++ b/solution.py
@@ -102,7 +102,7 @@
         compiler_params=params(16),
         cost_estimate=cost(0.2),
         name="recur",
-    )(lh_query, lh_key, lh_value, lh_step.T)
+    )(lh_query, lh_key, lh_value, lh_step)
 
 
 def beside_kernel(key_ref, value_ref, out_ref):
@@ -157,26 +157,37 @@
     ref[HEADS * HD :, :] = value[1]
 
 
-def join_kernel(bit, mine_ref, own_ref, other_ref, out_ref):
-    own_first = (mine_ref[0] // bit) % 2 == 0
+def join_cores_kernel(mine_ref, own_ref, other_ref, out_ref):
     own, other = state_of(own_ref), state_of(other_ref)
-
-    def pick(one, two):
-        return [jnp.where(own_first, a, b) for a, b in zip(one[0], two[0])], jnp.where(own_first, one[1], two[1])
-
-    put_state(out_ref, follow(pick(own, other), pick(other, own)))
-
-
-def join(bit, mine, own, other):
-    return pl.pallas_call(
-        functools.partial(join_kernel, bit),
-        out_shape=jax.ShapeDtypeStruct((STATE_ROWS, HD), f32),
-        in_specs=[SMEM, VMEM, VMEM],
-        out_specs=VMEM,
+    put_state(out_ref, follow_in_order(mine_ref[0] % 2 == 0, own, other))
+
+
+def join_sides_kernel(mine_ref, own_ref, even_ref, odd_ref, out_ref, other_ref):
+    mine = mine_ref[0]
+    own, even, odd = state_of(own_ref), state_of(even_ref), state_of(odd_ref)
+    other = select(mine % 2 == 0, even, odd)
+    put_state(other_ref, other)
+    put_state(out_ref, follow_in_order((mine // 2) % 2 == 0, own, other))
+
+
+def select(wanted, one, two):
+    return [jnp.where(wanted, a, b) for a, b in zip(one[0], two[0])], jnp.where(wanted, one[1], two[1])
+
+
+def follow_in_order(own_first, own, other):
+    return follow(select(own_first, own, other), select(own_first, other, own))
+
+
+def join(kernel, outputs, mine, *messages):
+    return pl.pallas_call(
+        kernel,
+        out_shape=(jax.ShapeDtypeStruct((STATE_ROWS, HD), f32),) * outputs,
+        in_specs=[SMEM] + [VMEM] * len(messages),
+        out_specs=(VMEM,) * outputs,
         compiler_params=params(14),
         cost_estimate=cost(0.2),
         name="join",
-    )(mine, own, other)
+    )(mine, *messages)
 
 
 def hand_kernel(mine_ref, behind_ref, beyond_ref, out_ref):
@@ -212,6 +223,9 @@
     if last:
         out_ref, square_ref, sums, keys, values, top_ref, tops = refs
     else:
+        if first:
+            (passed_ref,) = take(1)
+            passed_ref[...] = query_ref[...]
         numerator_ref, counted_ref, top_ref, sums, keys, values = refs
 
     def highest_of(part):
@@ -358,6 +372,8 @@
             jax.ShapeDtypeStruct((ROWS, HD), f32),
             jax.ShapeDtypeStruct(top, bf16),
         )
+        if first:
+            out_shape = (jax.ShapeDtypeStruct((ROWS, HEADS * HD), bf16),) + out_shape
     return pl.pallas_call(
         functools.partial(attend_kernel, first, last, numbers_of, len(blocks), kept_numbers_of, len(kept)),
         out_shape=out_shape,
@@ -459,16 +475,17 @@
         array
         for array in (lh_query, lh_key, lh_value, att_query, att_key, att_value)
     ]
-    near_query = att_query
-    lh_query, lh_key, lh_value, att_key, att_value = [
+    lh_step = lh_step.T
+    att_query, lh_query, lh_key, lh_value, att_key, att_value = [
         pltpu.with_memory_space_constraint(array, pltpu.HBM)
-        for array in (lh_query, lh_key, lh_value, att_key, att_value)
+        for array in (att_query, lh_query, lh_key, lh_value, att_key, att_value)
     ]
     own = beside(att_key, att_value)
     across = move(own, [(i, i ^ 2) for i in every if i < 4 or i % 4 < 2])
     near = move(own, sibling)
     chip = stack(own, near)
     chip, lh_step = tied(chip, lh_step)
+    lh_step = pltpu.with_memory_space_constraint(lh_step, pltpu.HBM)
     behind = move(chip, last_plane)
 
     local, grow, message = recur(lh_query, lh_key, lh_value, lh_step)
@@ -476,6 +493,8 @@
     beyond = move(chip, plane_before)
     across_near = move(across, sibling)
     first = move(message, sibling)
+    (of_chip,) = join(join_cores_kernel, 1, place, message, first)
+    other_even = move(of_chip, [(i, j) for i, j in sideways if i % 2 == 0])
     behind_near = move(behind, sibling)
     level = move(behind, [(i, j) for i, j in sideways if (i % 2 == 0 and i >= 4) or i >= 12])
 
@@ -510,23 +529,25 @@
         return behind_numbers(mine) + beyond_numbers(mine)
 
     first_blocks = [near, across, across_near, behind, behind_near]
-    carry = attend(place, near_query, own, None, first_blocks, first_numbers)
-    carry, first, beyond, level = tied(carry, first, beyond, level)
-    of_chip = join(1, place, message, first)
-    other_chip = move(of_chip, sideways)
+    first_blocks, of_chip = tied(first_blocks, of_chip)
+    near_query, *carry = attend(place, att_query, own, None, first_blocks, first_numbers)
+    carry, other_even, beyond, level = tied(carry, other_even, beyond, level)
+    other_odd = move(other_even, [(i, j) for i, j in sibling if i % 2 == 0])
     level_beyond = move(beyond, [(i, j) for i, j in sideways if i % 2 == 1 and i >= 8])
     beyond_near = move(beyond, sibling)
     level_near = move(level, sibling)
     middle_blocks = [level, level_near, beyond, beyond_near]
-    middle_blocks, of_chip = tied(middle_blocks, of_chip)
-    carry = attend(place, near_query, own, carry, middle_blocks, middle_numbers)
-    carry, level_beyond, other_chip = tied(carry, level_beyond, other_chip)
-    level_beyond_near = move(level_beyond, sibling)
-    of_plane = join(2, place, of_chip, other_chip)
+    of_plane, other_chip = join(join_sides_kernel, 2, place, of_chip, other_even, other_odd)
     state_behind = move(of_plane, last_plane)
     state_beyond = move(of_plane, plane_before)
+    middle_blocks, of_plane = tied(middle_blocks, of_plane)
+    carry = attend(place, near_query, own, carry, middle_blocks, middle_numbers)
+    carry, level_beyond, state_behind, state_beyond = tied(carry, level_beyond, state_behind, state_beyond)
+    level_beyond_near = move(level_beyond, sibling)
+    kept = hand(place, state_behind, state_beyond)
+    handed = move(kept, sibling)
     last_blocks = [level_beyond, level_beyond_near]
-    last_blocks, of_plane = tied(last_blocks, of_plane)
+    last_blocks, kept = tied(last_blocks, kept)
     attention, squares = attend(
         place,
         near_query,
@@ -541,10 +562,8 @@
     def over(value, bit):
         return lax.ppermute(value, "tp", [(i, i ^ bit) for i in range(8)])
 
-    squares, state_behind, state_beyond = tied(squares, state_behind, state_beyond)
+    squares, handed = tied(squares, handed)
     others = [over(squares, bit) for bit in (2, 4, 6)]
-    kept = hand(place, state_behind, state_beyond)
-    handed = move(kept, sibling)
     linear = carry_in(place, lh_query, local, grow, kept, handed, other_chip, first, lh_gain)
     others, linear = tied(others, linear)
     squares = squares + others[0] + others[1] + others[2]

time: 227 us -> 225 us (level); the launches traced: 224 us -> 224 us
  starting transfers between devices: 24.1 us -> 26.6 us
    ppermute x16 -> x17, starting transfers between devices: 18.4 us -> 20.9 us  [move(): return lax.ppermute(value, 'ctx', pairs)]
    ppermute x16 -> x17, waiting for transfers between devices: 6.53 us -> 6.19 us  [move(): return lax.ppermute(value, 'ctx', pairs)]
  transfers between devices with their start and end apart: 20 -> 21, of which waited for: 6 -> 6; matrix products, arithmetic and copies ran while one was open for 0% -> 0% of each run, Pallas kernels for 83% -> 83%
where the time goes in v2:
time: 225 us; the launch traced here: 224 us
  Pallas kernels  188 us (84%)
  starting transfers between devices  26.6 us (12%)
  waiting for transfers between devices  7.73 us (3%)
    pallas_call x3, Pallas kernels, attend(): pl.pallas_call(functools.partial(attend_kernel, first, last, numbers_of,...  175 us
    ppermute x17, starting transfers between devices, move(): return lax.ppermute(value, 'ctx', pairs)  20.9 us
    ppermute x17, waiting for transfers between devices, move(): return lax.ppermute(value, 'ctx', pairs)  6.19 us
    pallas_call x1, Pallas kernels, recur(): pl.pallas_call(recur_kernel, out_shape=(jax.ShapeDtypeStruct((ROWS, HEADS...  5.82 us
    ppermute x4, starting transfers between devices, over(): return lax.ppermute(value, 'tp', [(i, i ^ bit) for i in range(8)])  5.71 us
  transfers between devices with their start and end apart: 21, of which 6 were waited for; matrix products, arithmetic and copies ran while one was open for 0% of the time, Pallas kernels for 83%

profile of v2, /device:TPU:101, one launch (start us, length us, event | category | flops | bytes accessed | tf_op | source)
XLA Modules:
  0.0 224.2 jit_solution(5525996396265363545)
XLA Ops:
  0.0 1.0 beside.1.one_ref.own_ref
  1.0 0.8 collective-permute-start
  1.8 1.2 collective-permute-done.two_ref.refs_0_.refs_5_
  2.9 0.8 stack.1
  3.8 1.3 collective-permute-start.2
  5.0 1.3 collective-permute-start.1
  6.3 5.8 %recur.1 = (f32[512,768]{1,0:T(8,128)S(1)}, f32[512,128]{1,0:T(8,128)S(1)}, f32[776,128]{1,0:T(8,128)}) custom-call(bf16[512,768]{1,0:T(8,128)(2,1)} %query_hbm.1, bf16[512,768]{1,0:T(8,128)(2,1)} %k_hbm.1, bf16[512,768]{1,0:T(8,128)(2,1)} %v_hbm.1, f32[6,512]{1,0:T(8,128)} %bitcast.2), custom_call_target="tpu_custom_call" | custom-call | flops 200000000 | bytes 200000 | tf_op jit(solution)/shard_map/recur/pallas_call | solution.py:91
  12.2 0.0 copy-start
  12.2 1.2 copy-done
  13.4 2.6 %collective-permute-done.1.refs_1_.refs_6_ = bf16[512,256]{1,0:T(8,128)(2,1)S(1)} collective-permute-done((bf16[512,256]{1,0:T(8,128)(2,1)S(1)}, bf16[512,256]{1,0:T(8,128)(2,1)S(1)}, u32[]{:S(2)}, u32[]{:S(2)}) %collective-permute-start.1) | collective-permute-done | bytes 262176 | tf_op jit(solution)/shard_map/ppermute | solution.py:463
  16.0 0.0 collective-permute-done.2.refs_3_.refs_8_
  16.0 1.2 collective-permute-start.5
  17.2 0.0 collective-permute-start.4
  17.2 2.4 %collective-permute-start.8 = (bf16[1024,256]{1,0:T(8,128)(2,1)S(1)}, bf16[1024,256]{1,0:T(8,128)(2,1)S(1)}, u32[]{:S(2)}, u32[]{:S(2)}) collective-permute-start(bf16[1024,256]{1,0:T(8,128)(2,1)S(1)} %collective-permute-done.2.refs_3_.refs_8_), channel_id=1, source_target_pairs={{32,48},{48,32},{64,80},{80,64},{96,112},{104,120},{112,96},{120,1... | collective-permute-start | bytes 1572872 | tf_op jit(solution)/shard_map/ppermute | solution.py:463
  19.6 1.3 collective-permute-start.7
  20.9 0.0 collective-permute-done.5.other_ref.core_ref
  20.9 1.1 join.2.own_ref
  22.0 0.7 collective-permute-start.6
  22.7 4.2 %collective-permute-start.3 = (bf16[512,256]{1,0:T(8,128)(2,1)S(1)}, bf16[512,256]{1,0:T(8,128)(2,1)S(1)}, u32[]{:S(2)}, u32[]{:S(2)}) collective-permute-start(bf16[512,256]{1,0:T(8,128)(2,1)S(1)} %collective-permute-done.1.refs_1_.refs_6_), channel_id=1, source_target_pairs={{0,8},{8,0},{16,24},{24,16},{32,40},{40,32},{48,56},{56,48},{64,72... | collective-permute-start | bytes 786440 | tf_op jit(solution)/shard_map/ppermute | solution.py:463
  26.9 1.2 collective-permute-done.3.refs_2_.refs_7_
  28.1 0.0 collective-permute-done.4.refs_4_.refs_9_
  28.1 16.9 %attend_first.1 = (bf16[512,768]{1,0:T(8,128)(2,1)S(1)}, f32[512,768]{1,0:T(8,128)S(1)}, f32[512,128]{1,0:T(8,128)S(1)}, bf16[32,128]{1,0:T(8,128)(2,1)S(1)}) custom-call(s32[1]{0:T(128)} %bitcast.mine_ref, bf16[512,768]{1,0:T(8,128)(2,1)} %query_ref.1, bf16[512,256]{1,0:T(8,128)(2,1)S(1)} %beside.1.one_ref.own_ref, ...), custom_call_target="tpu_custom_call" | custom-call | flops 200000000 | bytes 200000 | tf_op jit(solution)/shard_map/attend_first/pallas_call | solution.py:377
  44.9 0.0 collective-permute-done.8.refs_3_.refs_10_
  44.9 0.0 collective-permute-done.7.refs_5_.refs_12_
  45.0 0.0 collective-permute-done.6.even_ref
  45.0 1.3 collective-permute-start.11
  46.3 1.2 collective-permute-start.10
  47.5 0.1 collective-permute-start.9
  47.6 1.9 collective-permute-start.12
  49.5 0.0 collective-permute-done.11.odd_ref
  49.5 0.2 join.3
  49.7 1.3 collective-permute-start.13
  51.0 1.3 collective-permute-start.14
  52.3 0.0 collective-permute-done.10.refs_6_.refs_13_
  52.3 0.0 collective-permute-done.9.refs_4_.refs_11_
  52.3 12.4 %attend_middle.1 = (f32[512,768]{1,0:T(8,128)S(1)}, f32[512,128]{1,0:T(8,128)S(1)}, bf16[32,128]{1,0:T(8,128)(2,1)S(1)}) custom-call(s32[1]{0:T(128)} %bitcast.mine_ref, bf16[512,768]{1,0:T(8,128)(2,1)S(1)} %get-tuple-element.67.query_ref, bf16[512,256]{1,0:T(8,128)(2,1)S(1)} %beside.1.one_ref.own_ref, f32[512,768]{1,0:T(8,128)S(1)} %get-tuple-element.72.refs_0_, ...), custom_call_target="tpu_custom_call" | custom-call | flops 200000000 | bytes 200000 | tf_op jit(solution)/shard_map/attend_middle/pallas_call | solution.py:377
  64.8 0.0 collective-permute-done.12.refs_3_
  64.8 0.0 collective-permute-done.13.behind_ref
  64.8 0.0 collective-permute-done.14.beyond_ref
  64.8 0.1 collective-permute-start.15
  64.9 0.1 hand.1.kept_ref
  65.0 0.0 copy-start.1
  65.0 0.0 copy-start.3
  65.0 0.5 collective-permute-start.16
  65.5 1.2 collective-permute-done.15.refs_4_
  66.8 146.1 %attend_last.1 = (bf16[512,768]{1,0:T(8,128)(2,1)S(1)}, f32[8,512]{1,0:T(8,128)S(1)}) custom-call(s32[1]{0:T(128)} %bitcast.mine_ref, bf16[512,768]{1,0:T(8,128)(2,1)S(1)} %get-tuple-element.67.query_ref, bf16[512,256]{1,0:T(8,128)(2,1)S(1)} %beside.1.one_ref.own_ref, f32[512,768]{1,0:T(8,128)S(1)} %get-tuple-element.87.refs_0_, ...), custom_call_target="tpu_custom_call" | custom-call | flops 200000000 | bytes 200000 | tf_op jit(solution)/shard_map/attend_last/pallas_call | solution.py:377
  212.9 0.0 collective-permute-done.16.handed_ref
  212.9 0.0 collective-permute-start.17
  212.9 3.0 %collective-permute-start.18 = (f32[8,512]{1,0:T(8,128)S(1)}, f32[8,512]{1,0:T(8,128)S(1)}, u32[]{:S(2)}, u32[]{:S(2)}) collective-permute-start(f32[8,512]{1,0:T(8,128)S(1)} %get-tuple-element.97), channel_id=1, source_target_pairs={{0,4},{1,5},{2,6},{3,7},{4,0},{5,1},{6,2},{7,3},{8,12},{9,13},{10,... | collective-permute-start | bytes 49160 | tf_op jit(solution)/shard_map/ppermute | solution.py:563
  215.9 0.9 collective-permute-start.19
  216.8 0.0 copy-done.1
  216.8 0.0 copy-done.3
  216.8 0.0 copy-start.2
  216.8 2.5 %carry.1.linear_ref = f32[512,768]{1,0:T(8,128)S(1)} custom-call(s32[1]{0:T(128)} %bitcast.mine_ref, bf16[512,768]{1,0:T(8,128)(2,1)} %query_hbm.1, f32[512,768]{1,0:T(8,128)S(1)} %copy-done.1, f32[512,128]{1,0:T(8,128)S(1)} %get-tuple-element.99.grow_ref, f32[776,128]{1,0:T(8,128)S(1)} %hand.1.kept_ref, f32[776,128]{1,0:T(8,128)S(1)} %collective-permute-done.16.handed_ref, ...), custom_call_target="tpu_custom_call" | custom-call | flops 200000000 | bytes 200000 | tf_op jit(solution)/shard_map/carry/pallas_call | solution.py:435
  219.3 0.0 collective-permute-done.17
  219.3 0.0 collective-permute-done.18
  219.3 0.4 collective-permute-done.19
  219.7 1.8 collective-permute-start.20
  221.5 1.1 collective-permute-done.20.other_ref
  222.7 0.0 copy-done.2
  222.7 1.5 finish.1
  (1 shorter events, 0.0 us)
Async XLA Ops:
  1.0 1.9 collective-permute-start
  3.8 12.2 %collective-permute-start.2 = (bf16[1024,256]{1,0:T(8,128)(2,1)}, bf16[1024,256]{1,0:T(8,128)(2,1)S(1)}, u32[]{:S(2)}, u32[]{:S(2)}) collective-permute-start(bf16[1024,256]{1,0:T(8,128)(2,1)} %stack.1), channel_id=1, source_target_pairs={{0,32},{16,48},{32,64},{48,80},{64,96},{80,112},{8,104},{24,120},{... | collective-permute-start | bytes 1572872 | tf_op jit(solution)/shard_map/ppermute | solution.py:463
  5.0 10.9 %collective-permute-start.1 = (bf16[512,256]{1,0:T(8,128)(2,1)S(1)}, bf16[512,256]{1,0:T(8,128)(2,1)S(1)}, u32[]{:S(2)}, u32[]{:S(2)}) collective-permute-start(bf16[512,256]{1,0:T(8,128)(2,1)S(1)} %beside.1.one_ref.own_ref), channel_id=1, source_target_pairs={{0,16},{8,24},{16,0},{24,8},{32,48},{40,56},{64,80},{72,88},{96,11... | collective-permute-start | bytes 786440 | tf_op jit(solution)/shard_map/ppermute | solution.py:463
  12.2 1.2 copy-start
  16.0 4.9 %collective-permute-start.5 = (f32[776,128]{1,0:T(8,128)}, f32[776,128]{1,0:T(8,128)S(1)}, u32[]{:S(2)}, u32[]{:S(2)}) collective-permute-start(f32[776,128]{1,0:T(8,128)} %get-tuple-element.61.own_ref), channel_id=1, source_target_pairs={{0,8},{8,0},{16,24},{24,16},{32,40},{40,32},{48,56},{56,48},{64,72... | collective-permute-start | bytes 1191944 | tf_op jit(solution)/shard_map/ppermute | solution.py:463
  17.2 10.9 %collective-permute-start.4 = (bf16[1024,256]{1,0:T(8,128)(2,1)S(1)}, bf16[1024,256]{1,0:T(8,128)(2,1)S(1)}, u32[]{:S(2)}, u32[]{:S(2)}) collective-permute-start(bf16[1024,256]{1,0:T(8,128)(2,1)S(1)} %collective-permute-done.2.refs_3_.refs_8_), channel_id=1, source_target_pairs={{0,8},{8,0},{16,24},{24,16},{32,40},{40,32},{48,56},{56,48},{64,72... | collective-permute-start | bytes 1572872 | tf_op jit(solution)/shard_map/ppermute | solution.py:463
  17.2 27.8 %collective-permute-start.8 = (bf16[1024,256]{1,0:T(8,128)(2,1)S(1)}, bf16[1024,256]{1,0:T(8,128)(2,1)S(1)}, u32[]{:S(2)}, u32[]{:S(2)}) collective-permute-start(bf16[1024,256]{1,0:T(8,128)(2,1)S(1)} %collective-permute-done.2.refs_3_.refs_8_), channel_id=1, source_target_pairs={{32,48},{48,32},{64,80},{80,64},{96,112},{104,120},{112,96},{120,1... | collective-permute-start | bytes 1572872 | tf_op jit(solution)/shard_map/ppermute | solution.py:463
  19.6 25.3 %collective-permute-start.7 = (bf16[1024,256]{1,0:T(8,128)(2,1)}, bf16[1024,256]{1,0:T(8,128)(2,1)S(1)}, u32[]{:S(2)}, u32[]{:S(2)}) collective-permute-start(bf16[1024,256]{1,0:T(8,128)(2,1)} %stack.1), channel_id=1, source_target_pairs={{8,72},{24,88},{40,104},{56,120},{9,73},{25,89},{41,105},{57,121},... | collective-permute-start | bytes 1572872 | tf_op jit(solution)/shard_map/ppermute | solution.py:463
  22.0 23.0 %collective-permute-start.6 = (f32[776,128]{1,0:T(8,128)S(1)}, f32[776,128]{1,0:T(8,128)S(1)}, u32[]{:S(2)}, u32[]{:S(2)}) collective-permute-start(f32[776,128]{1,0:T(8,128)S(1)} %join.2.own_ref), channel_id=1, source_target_pairs={{0,16},{16,0},{32,48},{48,32},{64,80},{80,64},{96,112},{112,96},{1... | collective-permute-start | bytes 1191944 | tf_op jit(solution)/shard_map/ppermute | solution.py:463
  22.7 5.4 %collective-permute-start.3 = (bf16[512,256]{1,0:T(8,128)(2,1)S(1)}, bf16[512,256]{1,0:T(8,128)(2,1)S(1)}, u32[]{:S(2)}, u32[]{:S(2)}) collective-permute-start(bf16[512,256]{1,0:T(8,128)(2,1)S(1)} %collective-permute-done.1.refs_1_.refs_6_), channel_id=1, source_target_pairs={{0,8},{8,0},{16,24},{24,16},{32,40},{40,32},{48,56},{56,48},{64,72... | collective-permute-start | bytes 786440 | tf_op jit(solution)/shard_map/ppermute | solution.py:463
  45.0 4.5 %collective-permute-start.11 = (f32[776,128]{1,0:T(8,128)S(1)}, f32[776,128]{1,0:T(8,128)S(1)}, u32[]{:S(2)}, u32[]{:S(2)}) collective-permute-start(f32[776,128]{1,0:T(8,128)S(1)} %collective-permute-done.6.even_ref), channel_id=1, source_target_pairs={{0,8},{16,24},{32,40},{48,56},{64,72},{80,88},{96,104},{112,120},{... | collective-permute-start | bytes 1191944 | tf_op jit(solution)/shard_map/ppermute | solution.py:463
  46.3 6.0 %collective-permute-start.10 = (bf16[1024,256]{1,0:T(8,128)(2,1)S(1)}, bf16[1024,256]{1,0:T(8,128)(2,1)S(1)}, u32[]{:S(2)}, u32[]{:S(2)}) collective-permute-start(bf16[1024,256]{1,0:T(8,128)(2,1)S(1)} %collective-permute-done.7.refs_5_.refs_12_), channel_id=1, source_target_pairs={{0,8},{8,0},{16,24},{24,16},{32,40},{40,32},{48,56},{56,48},{64,72... | collective-permute-start | bytes 1572872 | tf_op jit(solution)/shard_map/ppermute | solution.py:463
  47.5 4.8 %collective-permute-start.9 = (bf16[1024,256]{1,0:T(8,128)(2,1)S(1)}, bf16[1024,256]{1,0:T(8,128)(2,1)S(1)}, u32[]{:S(2)}, u32[]{:S(2)}) collective-permute-start(bf16[1024,256]{1,0:T(8,128)(2,1)S(1)} %collective-permute-done.8.refs_3_.refs_10_), channel_id=1, source_target_pairs={{0,8},{8,0},{16,24},{24,16},{32,40},{40,32},{48,56},{56,48},{64,72... | collective-permute-start | bytes 1572872 | tf_op jit(solution)/shard_map/ppermute | solution.py:463
  47.6 17.2 %collective-permute-start.12 = (bf16[1024,256]{1,0:T(8,128)(2,1)S(1)}, bf16[1024,256]{1,0:T(8,128)(2,1)S(1)}, u32[]{:S(2)}, u32[]{:S(2)}) collective-permute-start(bf16[1024,256]{1,0:T(8,128)(2,1)S(1)} %collective-permute-done.7.refs_5_.refs_12_), channel_id=1, source_target_pairs={{72,88},{88,72},{104,120},{120,104},{73,89},{89,73},{105,121},{121... | collective-permute-start | bytes 1572872 | tf_op jit(solution)/shard_map/ppermute | solution.py:463
  49.7 15.1 %collective-permute-start.13 = (f32[776,128]{1,0:T(8,128)S(1)}, f32[776,128]{1,0:T(8,128)S(1)}, u32[]{:S(2)}, u32[]{:S(2)}) collective-permute-start(f32[776,128]{1,0:T(8,128)S(1)} %get-tuple-element.79), channel_id=1, source_target_pairs={{0,32},{16,48},{32,64},{48,80},{64,96},{80,112},{8,104},{24,120},{... | collective-permute-start | bytes 1191944 | tf_op jit(solution)/shard_map/ppermute | solution.py:463
  51.0 13.8 %collective-permute-start.14 = (f32[776,128]{1,0:T(8,128)S(1)}, f32[776,128]{1,0:T(8,128)S(1)}, u32[]{:S(2)}, u32[]{:S(2)}) collective-permute-start(f32[776,128]{1,0:T(8,128)S(1)} %get-tuple-element.79), channel_id=1, source_target_pairs={{8,72},{24,88},{40,104},{56,120},{9,73},{25,89},{41,105},{57,121},... | collective-permute-start | bytes 1191944 | tf_op jit(solution)/shard_map/ppermute | solution.py:463
  64.8 2.0 collective-permute-start.15
  65.0 151.8 %copy-start.1 = (f32[512,768]{1,0:T(8,128)S(1)}, f32[512,768]{1,0:T(8,128)}, u32[]{:S(2)}) copy-start(f32[512,768]{1,0:T(8,128)} %copy-done) | copy-start | bytes 4718596
  65.0 151.8 %copy-start.3 = (f32[768]{0:T(1024)S(1)}, f32[768]{0:T(1024)}, u32[]{:S(2)}) copy-start(f32[768]{0:T(1024)} %gain_ref.2) | copy-start | bytes 9220
  65.0 147.9 %collective-permute-start.16 = (f32[776,128]{1,0:T(8,128)S(1)}, f32[776,128]{1,0:T(8,128)S(1)}, u32[]{:S(2)}, u32[]{:S(2)}) collective-permute-start(f32[776,128]{1,0:T(8,128)S(1)} %hand.1.kept_ref), channel_id=1, source_target_pairs={{0,8},{8,0},{16,24},{24,16},{32,40},{40,32},{48,56},{56,48},{64,72... | collective-permute-start | bytes 1191944 | tf_op jit(solution)/shard_map/ppermute | solution.py:463
  212.9 6.4 %collective-permute-start.17 = (f32[8,512]{1,0:T(8,128)S(1)}, f32[8,512]{1,0:T(8,128)S(1)}, u32[]{:S(2)}, u32[]{:S(2)}) collective-permute-start(f32[8,512]{1,0:T(8,128)S(1)} %get-tuple-element.97), channel_id=1, source_target_pairs={{0,2},{1,3},{2,0},{3,1},{4,6},{5,7},{6,4},{7,5},{8,10},{9,11},{10,... | collective-permute-start | bytes 49160 | tf_op jit(solution)/shard_map/ppermute | solution.py:563
  212.9 6.4 %collective-permute-start.18 = (f32[8,512]{1,0:T(8,128)S(1)}, f32[8,512]{1,0:T(8,128)S(1)}, u32[]{:S(2)}, u32[]{:S(2)}) collective-permute-start(f32[8,512]{1,0:T(8,128)S(1)} %get-tuple-element.97), channel_id=1, source_target_pairs={{0,4},{1,5},{2,6},{3,7},{4,0},{5,1},{6,2},{7,3},{8,12},{9,13},{10,... | collective-permute-start | bytes 49160 | tf_op jit(solution)/shard_map/ppermute | solution.py:563
  215.9 3.8 %collective-permute-start.19 = (f32[8,512]{1,0:T(8,128)S(1)}, f32[8,512]{1,0:T(8,128)S(1)}, u32[]{:S(2)}, u32[]{:S(2)}) collective-permute-start(f32[8,512]{1,0:T(8,128)S(1)} %get-tuple-element.97), channel_id=1, source_target_pairs={{0,6},{1,7},{2,4},{3,5},{4,2},{5,3},{6,0},{7,1},{8,14},{9,15},{10,... | collective-permute-start | bytes 49160 | tf_op jit(solution)/shard_map/ppermute | solution.py:563
  216.8 5.9 %copy-start.2 = (f32[768]{0:T(1024)S(1)}, f32[768]{0:T(1024)}, u32[]{:S(2)}) copy-start(f32[768]{0:T(1024)} %gain_ref.3) | copy-start | bytes 9220
  219.7 3.0 %collective-permute-start.20 = (f32[8,512]{1,0:T(8,128)S(1)}, f32[8,512]{1,0:T(8,128)S(1)}, u32[]{:S(2)}, u32[]{:S(2)}) collective-permute-start(f32[8,512]{1,0:T(8,128)S(1)} %add_add_fusion.square_ref), channel_id=1, source_target_pairs={{0,1},{1,0},{2,3},{3,2},{4,5},{5,4},{6,7},{7,6},{8,9},{9,8},{10,11... | collective-permute-start | bytes 49160 | tf_op jit(solution)/shard_map/ppermute | solution.py:563

commit v3 on v2

--- a/solution.py
+++ b/solution.py
@@ -276,13 +276,14 @@
         visit(n * 2 * ROWS, 2 * ROWS)
         return 0
 
-    lax.fori_loop(0, filled // 2, pair, 0)
+    if not first:
+        lax.fori_loop(0, filled // 2, pair, 0)
 
     if first:
 
-        @pl.when(filled % 2 == 1)
+        @pl.when(filled > 0)
         def _():
-            visit((filled - 1) * ROWS, ROWS)
+            visit(0, ROWS)
 
         at_row = lax.broadcasted_iota(jnp.int32, (TILE, TILE), 0)
         at_column = lax.broadcasted_iota(jnp.int32, (TILE, TILE), 1)
@@ -489,15 +490,6 @@
     behind = move(chip, last_plane)
 
     local, grow, message = recur(lh_query, lh_key, lh_value, lh_step)
-    chip, across, behind, message = tied(chip, across, behind, message)
-    beyond = move(chip, plane_before)
-    across_near = move(across, sibling)
-    first = move(message, sibling)
-    (of_chip,) = join(join_cores_kernel, 1, place, message, first)
-    other_even = move(of_chip, [(i, j) for i, j in sideways if i % 2 == 0])
-    behind_near = move(behind, sibling)
-    level = move(behind, [(i, j) for i, j in sideways if (i % 2 == 0 and i >= 4) or i >= 12])
-
     def where(number, wanted):
         return jnp.where(wanted, number, NEVER)
 
@@ -520,6 +512,23 @@
         number = where(even - 8, plane >= 2)
         return [where(number, core == 1), where(number, core == 0)]
 
+    def near_numbers(mine):
+        return [where(mine - 1, mine % 2 == 1)]
+
+    def across_numbers(mine):
+        _, side, _, even = parts(mine)
+        return [where(even - 2, side == 1)] * 2
+
+    def behind_numbers(mine):
+        _, _, core, _ = parts(mine)
+        zero, one = brought(mine, 0), brought(mine, 1)
+        return [jnp.where(core == 0, zero, one), jnp.where(core == 0, one, zero)]
+
+    def beyond_numbers(mine):
+        plane, _, core, even = parts(mine)
+        number = where(even - 8, plane >= 2)
+        return [where(number, core == 1), where(number, core == 0)]
+
     def first_numbers(mine):
         _, side, core, even = parts(mine)
         near_numbers = [where(mine - 1, core == 1)] + [where(even - 2, side == 1)] * 2
@@ -528,25 +537,39 @@
     def middle_numbers(mine):
         return behind_numbers(mine) + beyond_numbers(mine)
 
-    first_blocks = [near, across, across_near, behind, behind_near]
-    first_blocks, of_chip = tied(first_blocks, of_chip)
-    near_query, *carry = attend(place, att_query, own, None, first_blocks, first_numbers)
-    carry, other_even, beyond, level = tied(carry, other_even, beyond, level)
+    def last_numbers(mine):
+        return across_numbers(mine) + beyond_numbers(mine)
+
+    near_query, *carry = attend(place, att_query, own, None, [near], near_numbers)
+    carry, message, across = tied(carry, message, across)
+    first = move(message, sibling)
+    (of_chip,) = join(join_cores_kernel, 1, place, message, first)
+    other_even = move(of_chip, [(i, j) for i, j in sideways if i % 2 == 0])
+
+    chip, behind, of_chip = tied(chip, behind, of_chip)
+    behind_near = move(behind, sibling)
+    level = move(behind, [(i, j) for i, j in sideways if (i % 2 == 0 and i >= 4) or i >= 12])
+    beyond = move(chip, plane_before)
+    carry = attend(place, near_query, own, carry, [behind, behind_near], behind_numbers)
+
+    carry, other_even, across, beyond, level = tied(carry, other_even, across, beyond, level)
     other_odd = move(other_even, [(i, j) for i, j in sibling if i % 2 == 0])
     level_beyond = move(beyond, [(i, j) for i, j in sideways if i % 2 == 1 and i >= 8])
+    across_near = move(across, sibling)
     beyond_near = move(beyond, sibling)
     level_near = move(level, sibling)
-    middle_blocks = [level, level_near, beyond, beyond_near]
     of_plane, other_chip = join(join_sides_kernel, 2, place, of_chip, other_even, other_odd)
     state_behind = move(of_plane, last_plane)
     state_beyond = move(of_plane, plane_before)
+    middle_blocks = [level, level_near, beyond, beyond_near]
     middle_blocks, of_plane = tied(middle_blocks, of_plane)
     carry = attend(place, near_query, own, carry, middle_blocks, middle_numbers)
+
     carry, level_beyond, state_behind, state_beyond = tied(carry, level_beyond, state_behind, state_beyond)
     level_beyond_near = move(level_beyond, sibling)
     kept = hand(place, state_behind, state_beyond)
     handed = move(kept, sibling)
-    last_blocks = [level_beyond, level_beyond_near]
+    last_blocks = [across, across_near, level_beyond, level_beyond_near]
     last_blocks, kept = tied(last_blocks, kept)
     attention, squares = attend(
         place,
@@ -554,9 +577,9 @@
         own,
         carry,
         last_blocks,
-        beyond_numbers,
-        first_blocks + middle_blocks,
-        lambda mine: first_numbers(mine) + middle_numbers(mine),
+        last_numbers,
+        [near, behind, behind_near] + middle_blocks,
+        lambda mine: near_numbers(mine) + behind_numbers(mine) + middle_numbers(mine),
     )
 
     def over(value, bit):

time: 225 us -> 227 us (level)
  starting transfers between devices: 26.6 us -> 171 us
  Pallas kernels: 188 us -> 46.2 us
    ppermute x4, starting transfers between devices: 5.71 us -> 145 us  [over(): return lax.ppermute(value, 'tp', [(i, i ^ bit) for i in range(8)])]
    pallas_call x3 -> x4, Pallas kernels: 175 us -> 35.8 us  [attend(): pl.pallas_call(functools.partial(attend_kernel, first, last, numbers_of,...]
    ppermute x17, starting transfers between devices: 20.9 us -> 25.4 us  [move(): return lax.ppermute(value, 'ctx', pairs)]
  transfers between devices with their start and end apart: 21 -> 21, of which waited for: 6 -> 5; matrix products, arithmetic and copies ran while one was open for 0% -> 0% of each run, Pallas kernels for 83% -> 19%
where the time goes in v3:
time: 227 us
  starting transfers between devices  171 us (75%)
  Pallas kernels  46.2 us (20%)
  waiting for transfers between devices  9.75 us (4%)
    ppermute x4, starting transfers between devices, over(): return lax.ppermute(value, 'tp', [(i, i ^ bit) for i in range(8)])  145 us
    pallas_call x4, Pallas kernels, attend(): pl.pallas_call(functools.partial(attend_kernel, first, last, numbers_of,...  35.8 us
    ppermute x17, starting transfers between devices, move(): return lax.ppermute(value, 'ctx', pairs)  25.4 us
    ppermute x17, waiting for transfers between devices, move(): return lax.ppermute(value, 'ctx', pairs)  6.8 us
    pallas_call x1, Pallas kernels, recur(): pl.pallas_call(recur_kernel, out_shape=(jax.ShapeDtypeStruct((ROWS, HEADS...  5.03 us
  transfers between devices with their start and end apart: 21, of which 5 were waited for; matrix products, arithmetic and copies ran while one was open for 0% of the time, Pallas kernels for 19%

profile of v3, /device:TPU:101, one launch (start us, length us, event | category | flops | bytes accessed | tf_op | source)
XLA Modules:
  0.0 227.1 jit_solution(16772168654575698291)
XLA Ops:
  0.0 1.0 beside.1.own_ref.one_ref
  1.0 0.8 collective-permute-start
  1.8 1.3 collective-permute-start.1
  3.1 0.0 collective-permute-done.refs_0_.two_ref.refs_7_
  3.1 1.3 collective-permute-start.2
  4.4 5.0 %recur.1 = (f32[512,768]{1,0:T(8,128)S(1)}, f32[512,128]{1,0:T(8,128)S(1)}, f32[776,128]{1,0:T(8,128)S(1)}) custom-call(bf16[512,768]{1,0:T(8,128)(2,1)} %query_hbm.1, bf16[512,768]{1,0:T(8,128)(2,1)} %k_hbm.1, bf16[512,768]{1,0:T(8,128)(2,1)} %v_hbm.1, f32[6,512]{1,0:T(8,128)} %bitcast.2), custom_call_target="tpu_custom_call" | custom-call | flops 200000000 | bytes 200000 | tf_op jit(solution)/shard_map/recur/pallas_call | solution.py:91
  9.5 5.3 %attend_first.1 = (bf16[512,768]{1,0:T(8,128)(2,1)S(1)}, f32[512,768]{1,0:T(8,128)S(1)}, f32[512,128]{1,0:T(8,128)S(1)}, bf16[32,128]{1,0:T(8,128)(2,1)S(1)}) custom-call(s32[1]{0:T(128)} %bitcast.mine_ref, bf16[512,768]{1,0:T(8,128)(2,1)} %query_ref.1, bf16[512,256]{1,0:T(8,128)(2,1)S(1)} %beside.1.own_ref.one_ref, ...), custom_call_target="tpu_custom_call" | custom-call | flops 200000000 | bytes 200000 | tf_op jit(solution)/shard_map/attend_first/pallas_call | solution.py:378
  14.8 0.0 collective-permute-done.1.refs_3_
  14.8 0.1 collective-permute-start.3
  14.9 1.7 collective-permute-done.3.other_ref.core_ref
  16.6 0.1 join.2.own_ref
  16.7 0.0 collective-permute-done.2.refs_3_.refs_8_
  16.7 0.2 collective-permute-start.4
  16.9 1.3 collective-permute-start.6
  18.2 5.5 %collective-permute-start.7 = (bf16[1024,256]{1,0:T(8,128)(2,1)S(1)}, bf16[1024,256]{1,0:T(8,128)(2,1)S(1)}, u32[]{:S(2)}, u32[]{:S(2)}) collective-permute-start(bf16[1024,256]{1,0:T(8,128)(2,1)S(1)} %collective-permute-done.2.refs_3_.refs_8_), channel_id=1, source_target_pairs={{32,48},{48,32},{64,80},{80,64},{96,112},{104,120},{112,96},{120,1... | collective-permute-start | bytes 1572872 | tf_op jit(solution)/shard_map/ppermute | solution.py:464
  23.7 0.7 collective-permute-start.5
  24.4 0.0 collective-permute-done.4.refs_4_.refs_9_
  24.4 8.8 %attend_middle.2 = (f32[512,768]{1,0:T(8,128)S(1)}, f32[512,128]{1,0:T(8,128)S(1)}, bf16[32,128]{1,0:T(8,128)(2,1)S(1)}) custom-call(s32[1]{0:T(128)} %bitcast.mine_ref, bf16[512,768]{1,0:T(8,128)(2,1)S(1)} %get-tuple-element.60.query_ref, bf16[512,256]{1,0:T(8,128)(2,1)S(1)} %beside.1.own_ref.one_ref, f32[512,768]{1,0:T(8,128)S(1)} %get-tuple-element.66.refs_0_, ...), custom_call_target="tpu_custom_call" | custom-call | flops 200000000 | bytes 200000 | tf_op jit(solution)/shard_map/attend_middle/pallas_call | solution.py:378
  33.2 0.0 collective-permute-done.5.even_ref
  33.2 0.0 collective-permute-done.6.refs_5_.refs_12_
  33.2 3.0 %collective-permute-done.7.refs_3_.refs_10_ = bf16[1024,256]{1,0:T(8,128)(2,1)S(1)} collective-permute-done((bf16[1024,256]{1,0:T(8,128)(2,1)S(1)}, bf16[1024,256]{1,0:T(8,128)(2,1)S(1)}, u32[]{:S(2)}, u32[]{:S(2)}) %collective-permute-start.7) | collective-permute-done | bytes 524320 | tf_op jit(solution)/shard_map/ppermute | solution.py:464
  36.1 1.3 collective-permute-start.10
  37.4 4.7 %collective-permute-start.8 = (bf16[1024,256]{1,0:T(8,128)(2,1)S(1)}, bf16[1024,256]{1,0:T(8,128)(2,1)S(1)}, u32[]{:S(2)}, u32[]{:S(2)}) collective-permute-start(bf16[1024,256]{1,0:T(8,128)(2,1)S(1)} %collective-permute-done.7.refs_3_.refs_10_), channel_id=1, source_target_pairs={{0,8},{8,0},{16,24},{24,16},{32,40},{40,32},{48,56},{56,48},{64,72... | collective-permute-start | bytes 1572872 | tf_op jit(solution)/shard_map/ppermute | solution.py:464
  42.2 0.1 collective-permute-start.9
  42.2 4.9 %collective-permute-start.11 = (bf16[1024,256]{1,0:T(8,128)(2,1)S(1)}, bf16[1024,256]{1,0:T(8,128)(2,1)S(1)}, u32[]{:S(2)}, u32[]{:S(2)}) collective-permute-start(bf16[1024,256]{1,0:T(8,128)(2,1)S(1)} %collective-permute-done.6.refs_5_.refs_12_), channel_id=1, source_target_pairs={{72,88},{88,72},{104,120},{120,104},{73,89},{89,73},{105,121},{121... | collective-permute-start | bytes 1572872 | tf_op jit(solution)/shard_map/ppermute | solution.py:464
  47.2 0.0 collective-permute-done.10.odd_ref
  47.2 0.2 join.3
  47.3 1.3 collective-permute-start.12
  48.6 1.3 collective-permute-start.13
  49.9 0.0 collective-permute-done.8.refs_4_.refs_11_
  49.9 0.0 collective-permute-done.9.refs_6_.refs_13_
  49.9 12.4 %attend_middle.3 = (f32[512,768]{1,0:T(8,128)S(1)}, f32[512,128]{1,0:T(8,128)S(1)}, bf16[32,128]{1,0:T(8,128)(2,1)S(1)}) custom-call(s32[1]{0:T(128)} %bitcast.mine_ref, bf16[512,768]{1,0:T(8,128)(2,1)S(1)} %get-tuple-element.60.query_ref, bf16[512,256]{1,0:T(8,128)(2,1)S(1)} %beside.1.own_ref.one_ref, f32[512,768]{1,0:T(8,128)S(1)} %get-tuple-element.77.refs_0_, ...), custom_call_target="tpu_custom_call" | custom-call | flops 200000000 | bytes 200000 | tf_op jit(solution)/shard_map/attend_middle/pallas_call | solution.py:378
  62.4 0.0 collective-permute-done.11.refs_5_
  62.4 0.0 collective-permute-done.12.behind_ref
  62.4 0.0 collective-permute-done.13.beyond_ref
  62.4 0.1 collective-permute-start.15
  62.5 0.1 hand.1.kept_ref
  62.6 0.0 copy-start.1
  62.6 0.6 collective-permute-start.16
  63.2 0.1 collective-permute-start.14
  63.3 2.1 collective-permute-done.14.refs_4_
  65.4 0.0 collective-permute-done.15.refs_6_
  65.4 9.2 %attend_last.1 = (bf16[512,768]{1,0:T(8,128)(2,1)S(1)}, f32[8,512]{1,0:T(8,128)S(1)}) custom-call(s32[1]{0:T(128)} %bitcast.mine_ref, bf16[512,768]{1,0:T(8,128)(2,1)S(1)} %get-tuple-element.60.query_ref, bf16[512,256]{1,0:T(8,128)(2,1)S(1)} %beside.1.own_ref.one_ref, f32[512,768]{1,0:T(8,128)S(1)} %get-tuple-element.92.refs_0_, ...), custom_call_target="tpu_custom_call" | custom-call | flops 200000000 | bytes 200000 | tf_op jit(solution)/shard_map/attend_last/pallas_call | solution.py:378
  74.6 0.0 collective-permute-done.16.handed_ref
  74.6 141.9 %collective-permute-start.17 = (f32[8,512]{1,0:T(8,128)S(1)}, f32[8,512]{1,0:T(8,128)S(1)}, u32[]{:S(2)}, u32[]{:S(2)}) collective-permute-start(f32[8,512]{1,0:T(8,128)S(1)} %get-tuple-element.105), channel_id=1, source_target_pairs={{0,2},{1,3},{2,0},{3,1},{4,6},{5,7},{6,4},{7,5},{8,10},{9,11},{10,... | collective-permute-start | bytes 49160 | tf_op jit(solution)/shard_map/ppermute | solution.py:586
  216.5 2.6 %collective-permute-start.18 = (f32[8,512]{1,0:T(8,128)S(1)}, f32[8,512]{1,0:T(8,128)S(1)}, u32[]{:S(2)}, u32[]{:S(2)}) collective-permute-start(f32[8,512]{1,0:T(8,128)S(1)} %get-tuple-element.105), channel_id=1, source_target_pairs={{0,4},{1,5},{2,6},{3,7},{4,0},{5,1},{6,2},{7,3},{8,12},{9,13},{10,... | collective-permute-start | bytes 49160 | tf_op jit(solution)/shard_map/ppermute | solution.py:586
  219.1 0.0 collective-permute-start.19
  219.2 0.0 copy-done.1
  219.2 0.0 copy-start
  219.2 2.5 %carry.1.linear_ref = f32[512,768]{1,0:T(8,128)S(1)} custom-call(s32[1]{0:T(128)} %bitcast.mine_ref, bf16[512,768]{1,0:T(8,128)(2,1)} %query_hbm.1, f32[512,768]{1,0:T(8,128)S(1)} %get-tuple-element.106.local_ref, f32[512,128]{1,0:T(8,128)S(1)} %get-tuple-element.107.grow_ref, f32[776,128]{1,0:T(8,128)S(1)} %hand.1.kept_ref, ...), custom_call_target="tpu_custom_call" | custom-call | flops 200000000 | bytes 200000 | tf_op jit(solution)/shard_map/carry/pallas_call | solution.py:436
  221.6 0.0 collective-permute-done.17
  221.7 0.0 collective-permute-done.18
  221.7 1.3 collective-permute-done.19
  223.0 0.9 collective-permute-start.20
  223.9 1.7 collective-permute-done.20.other_ref
  225.5 0.0 copy-done
  225.5 1.5 finish.1
  (2 shorter events, 0.0 us)
Async XLA Ops:
  1.0 2.0 collective-permute-start
  1.8 13.0 %collective-permute-start.1 = (bf16[512,256]{1,0:T(8,128)(2,1)S(1)}, bf16[512,256]{1,0:T(8,128)(2,1)S(1)}, u32[]{:S(2)}, u32[]{:S(2)}) collective-permute-start(bf16[512,256]{1,0:T(8,128)(2,1)S(1)} %beside.1.own_ref.one_ref), channel_id=1, source_target_pairs={{0,16},{8,24},{16,0},{24,8},{32,48},{40,56},{64,80},{72,88},{96,11... | collective-permute-start | bytes 786440 | tf_op jit(solution)/shard_map/ppermute | solution.py:464
  3.1 13.5 %collective-permute-start.2 = (bf16[1024,256]{1,0:T(8,128)(2,1)S(1)}, bf16[1024,256]{1,0:T(8,128)(2,1)S(1)}, u32[]{:S(2)}, u32[]{:S(2)}) collective-permute-start(bf16[1024,256]{1,0:T(8,128)(2,1)S(1)} %stack.1), channel_id=1, source_target_pairs={{0,32},{16,48},{32,64},{48,80},{64,96},{80,112},{8,104},{24,120},{... | collective-permute-start | bytes 1572872 | tf_op jit(solution)/shard_map/ppermute | solution.py:464
  14.8 1.8 collective-permute-start.3
  16.7 7.7 %collective-permute-start.4 = (bf16[1024,256]{1,0:T(8,128)(2,1)S(1)}, bf16[1024,256]{1,0:T(8,128)(2,1)S(1)}, u32[]{:S(2)}, u32[]{:S(2)}) collective-permute-start(bf16[1024,256]{1,0:T(8,128)(2,1)S(1)} %collective-permute-done.2.refs_3_.refs_8_), channel_id=1, source_target_pairs={{0,8},{8,0},{16,24},{24,16},{32,40},{40,32},{48,56},{56,48},{64,72... | collective-permute-start | bytes 1572872 | tf_op jit(solution)/shard_map/ppermute | solution.py:464
  16.9 16.3 %collective-permute-start.6 = (bf16[1024,256]{1,0:T(8,128)(2,1)S(1)}, bf16[1024,256]{1,0:T(8,128)(2,1)S(1)}, u32[]{:S(2)}, u32[]{:S(2)}) collective-permute-start(bf16[1024,256]{1,0:T(8,128)(2,1)S(1)} %stack.1), channel_id=1, source_target_pairs={{8,72},{24,88},{40,104},{56,120},{9,73},{25,89},{41,105},{57,121},... | collective-permute-start | bytes 1572872 | tf_op jit(solution)/shard_map/ppermute | solution.py:464
  18.2 18.0 %collective-permute-start.7 = (bf16[1024,256]{1,0:T(8,128)(2,1)S(1)}, bf16[1024,256]{1,0:T(8,128)(2,1)S(1)}, u32[]{:S(2)}, u32[]{:S(2)}) collective-permute-start(bf16[1024,256]{1,0:T(8,128)(2,1)S(1)} %collective-permute-done.2.refs_3_.refs_8_), channel_id=1, source_target_pairs={{32,48},{48,32},{64,80},{80,64},{96,112},{104,120},{112,96},{120,1... | collective-permute-start | bytes 1572872 | tf_op jit(solution)/shard_map/ppermute | solution.py:464
  23.7 9.5 %collective-permute-start.5 = (f32[776,128]{1,0:T(8,128)S(1)}, f32[776,128]{1,0:T(8,128)S(1)}, u32[]{:S(2)}, u32[]{:S(2)}) collective-permute-start(f32[776,128]{1,0:T(8,128)S(1)} %join.2.own_ref), channel_id=1, source_target_pairs={{0,16},{16,0},{32,48},{48,32},{64,80},{80,64},{96,112},{112,96},{1... | collective-permute-start | bytes 1191944 | tf_op jit(solution)/shard_map/ppermute | solution.py:464
  36.1 11.0 %collective-permute-start.10 = (f32[776,128]{1,0:T(8,128)S(1)}, f32[776,128]{1,0:T(8,128)S(1)}, u32[]{:S(2)}, u32[]{:S(2)}) collective-permute-start(f32[776,128]{1,0:T(8,128)S(1)} %collective-permute-done.5.even_ref), channel_id=1, source_target_pairs={{0,8},{16,24},{32,40},{48,56},{64,72},{80,88},{96,104},{112,120},{... | collective-permute-start | bytes 1191944 | tf_op jit(solution)/shard_map/ppermute | solution.py:464
  37.4 12.5 %collective-permute-start.8 = (bf16[1024,256]{1,0:T(8,128)(2,1)S(1)}, bf16[1024,256]{1,0:T(8,128)(2,1)S(1)}, u32[]{:S(2)}, u32[]{:S(2)}) collective-permute-start(bf16[1024,256]{1,0:T(8,128)(2,1)S(1)} %collective-permute-done.7.refs_3_.refs_10_), channel_id=1, source_target_pairs={{0,8},{8,0},{16,24},{24,16},{32,40},{40,32},{48,56},{56,48},{64,72... | collective-permute-start | bytes 1572872 | tf_op jit(solution)/shard_map/ppermute | solution.py:464
  42.2 7.8 %collective-permute-start.9 = (bf16[1024,256]{1,0:T(8,128)(2,1)S(1)}, bf16[1024,256]{1,0:T(8,128)(2,1)S(1)}, u32[]{:S(2)}, u32[]{:S(2)}) collective-permute-start(bf16[1024,256]{1,0:T(8,128)(2,1)S(1)} %collective-permute-done.6.refs_5_.refs_12_), channel_id=1, source_target_pairs={{0,8},{8,0},{16,24},{24,16},{32,40},{40,32},{48,56},{56,48},{64,72... | collective-permute-start | bytes 1572872 | tf_op jit(solution)/shard_map/ppermute | solution.py:464
  42.2 20.2 %collective-permute-start.11 = (bf16[1024,256]{1,0:T(8,128)(2,1)S(1)}, bf16[1024,256]{1,0:T(8,128)(2,1)S(1)}, u32[]{:S(2)}, u32[]{:S(2)}) collective-permute-start(bf16[1024,256]{1,0:T(8,128)(2,1)S(1)} %collective-permute-done.6.refs_5_.refs_12_), channel_id=1, source_target_pairs={{72,88},{88,72},{104,120},{120,104},{73,89},{89,73},{105,121},{121... | collective-permute-start | bytes 1572872 | tf_op jit(solution)/shard_map/ppermute | solution.py:464
  47.3 15.1 %collective-permute-start.12 = (f32[776,128]{1,0:T(8,128)S(1)}, f32[776,128]{1,0:T(8,128)S(1)}, u32[]{:S(2)}, u32[]{:S(2)}) collective-permute-start(f32[776,128]{1,0:T(8,128)S(1)} %get-tuple-element.84), channel_id=1, source_target_pairs={{0,32},{16,48},{32,64},{48,80},{64,96},{80,112},{8,104},{24,120},{... | collective-permute-start | bytes 1191944 | tf_op jit(solution)/shard_map/ppermute | solution.py:464
  48.6 13.8 %collective-permute-start.13 = (f32[776,128]{1,0:T(8,128)S(1)}, f32[776,128]{1,0:T(8,128)S(1)}, u32[]{:S(2)}, u32[]{:S(2)}) collective-permute-start(f32[776,128]{1,0:T(8,128)S(1)} %get-tuple-element.84), channel_id=1, source_target_pairs={{8,72},{24,88},{40,104},{56,120},{9,73},{25,89},{41,105},{57,121},... | collective-permute-start | bytes 1191944 | tf_op jit(solution)/shard_map/ppermute | solution.py:464
  62.4 2.9 %collective-permute-start.15 = (bf16[1024,256]{1,0:T(8,128)(2,1)S(1)}, bf16[1024,256]{1,0:T(8,128)(2,1)S(1)}, u32[]{:S(2)}, u32[]{:S(2)}) collective-permute-start(bf16[1024,256]{1,0:T(8,128)(2,1)S(1)} %collective-permute-done.11.refs_5_), channel_id=1, source_target_pairs={{0,8},{8,0},{16,24},{24,16},{32,40},{40,32},{48,56},{56,48},{64,72... | collective-permute-start | bytes 1572872 | tf_op jit(solution)/shard_map/ppermute | solution.py:464
  62.6 156.5 %copy-start.1 = (f32[768]{0:T(1024)S(1)}, f32[768]{0:T(1024)}, u32[]{:S(2)}) copy-start(f32[768]{0:T(1024)} %gain_ref.2) | copy-start | bytes 9220
  62.6 12.0 %collective-permute-start.16 = (f32[776,128]{1,0:T(8,128)S(1)}, f32[776,128]{1,0:T(8,128)S(1)}, u32[]{:S(2)}, u32[]{:S(2)}) collective-permute-start(f32[776,128]{1,0:T(8,128)S(1)} %hand.1.kept_ref), channel_id=1, source_target_pairs={{0,8},{8,0},{16,24},{24,16},{32,40},{40,32},{48,56},{56,48},{64,72... | collective-permute-start | bytes 1191944 | tf_op jit(solution)/shard_map/ppermute | solution.py:464
  63.2 2.2 collective-permute-start.14
  74.6 147.0 %collective-permute-start.17 = (f32[8,512]{1,0:T(8,128)S(1)}, f32[8,512]{1,0:T(8,128)S(1)}, u32[]{:S(2)}, u32[]{:S(2)}) collective-permute-start(f32[8,512]{1,0:T(8,128)S(1)} %get-tuple-element.105), channel_id=1, source_target_pairs={{0,2},{1,3},{2,0},{3,1},{4,6},{5,7},{6,4},{7,5},{8,10},{9,11},{10,... | collective-permute-start | bytes 49160 | tf_op jit(solution)/shard_map/ppermute | solution.py:586
  216.5 5.1 %collective-permute-start.18 = (f32[8,512]{1,0:T(8,128)S(1)}, f32[8,512]{1,0:T(8,128)S(1)}, u32[]{:S(2)}, u32[]{:S(2)}) collective-permute-start(f32[8,512]{1,0:T(8,128)S(1)} %get-tuple-element.105), channel_id=1, source_target_pairs={{0,4},{1,5},{2,6},{3,7},{4,0},{5,1},{6,2},{7,3},{8,12},{9,13},{10,... | collective-permute-start | bytes 49160 | tf_op jit(solution)/shard_map/ppermute | solution.py:586
  219.1 3.8 %collective-permute-start.19 = (f32[8,512]{1,0:T(8,128)S(1)}, f32[8,512]{1,0:T(8,128)S(1)}, u32[]{:S(2)}, u32[]{:S(2)}) collective-permute-start(f32[8,512]{1,0:T(8,128)S(1)} %get-tuple-element.105), channel_id=1, source_target_pairs={{0,6},{1,7},{2,4},{3,5},{4,2},{5,3},{6,0},{7,1},{8,14},{9,15},{10,... | collective-permute-start | bytes 49160 | tf_op jit(solution)/shard_map/ppermute | solution.py:586
  219.2 6.4 %copy-start = (f32[768]{0:T(1024)S(1)}, f32[768]{0:T(1024)}, u32[]{:S(2)}) copy-start(f32[768]{0:T(1024)} %gain_ref.3) | copy-start | bytes 9220
  223.0 2.6 %collective-permute-start.20 = (f32[8,512]{1,0:T(8,128)S(1)}, f32[8,512]{1,0:T(8,128)S(1)}, u32[]{:S(2)}, u32[]{:S(2)}) collective-permute-start(f32[8,512]{1,0:T(8,128)S(1)} %add_add_fusion.square_ref), channel_id=1, source_target_pairs={{0,1},{1,0},{2,3},{3,2},{4,5},{5,4},{6,7},{7,6},{8,9},{9,8},{10,11... | collective-permute-start | bytes 49160 | tf_op jit(solution)/shard_map/ppermute | solution.py:586

commit v4 on v3

--- a/solution.py
+++ b/solution.py
@@ -121,20 +121,23 @@
     )(key, value)
 
 
-def stack_kernel(one_ref, two_ref, out_ref):
-    out_ref[:ROWS, :] = one_ref[...]
-    out_ref[ROWS:, :] = two_ref[...]
-
-
-def stack(one, two):
+def stack_kernel(*refs):
+    *parts, out_ref = refs
+    at = 0
+    for part in parts:
+        out_ref[at : at + part.shape[0], :] = part[...]
+        at += part.shape[0]
+
+
+def stack(*parts):
     return pl.pallas_call(
         stack_kernel,
-        out_shape=jax.ShapeDtypeStruct((2 * ROWS, 2 * HD), bf16),
-        in_specs=[VMEM, VMEM],
+        out_shape=jax.ShapeDtypeStruct((sum(part.shape[0] for part in parts), 2 * HD), bf16),
+        in_specs=[VMEM] * len(parts),
         out_specs=VMEM,
         compiler_params=params(14),
         name="stack",
-    )(one, two)
+    )(*parts)
 
 
 def follow(early, late):
@@ -209,7 +212,7 @@
     )(mine, behind, beyond)
 
 
-def attend_kernel(first, last, numbers_of, buffers, kept_numbers_of, kept, mine_ref, query_ref, own_ref, *refs):
+def attend_kernel(first, last, numbers_of, pieces, kept_numbers_of, kept, mine_ref, query_ref, own_ref, *refs):
     mine = mine_ref[0]
     refs = list(refs)
 
@@ -218,8 +221,8 @@
 
     if not first:
         carry_ref, count_ref, top_in_ref = take(3)
-    block_refs = take(buffers)
-    kept_refs = take(kept)
+    block_refs = [(ref, *piece) for ref, piece in zip(take(len(pieces)), pieces)]
+    kept_refs = [(ref, *piece) for ref, piece in zip(take(len(kept)), kept)]
     if last:
         out_ref, square_ref, sums, keys, values, top_ref, tops = refs
     else:
@@ -233,17 +236,17 @@
 
     def fill(blocks, numbers):
         filled = jnp.int32(0)
-        for block, number in zip(blocks, numbers):
-            rows = block.shape[0]
+        for (block, start, rows), number in zip(blocks, numbers):
             takes = number < mine
             place = filled
 
             @pl.when(takes)
             def _():
                 at = pl.ds(pl.multiple_of(place * ROWS, ROWS), rows)
-                keys[at, :] = block[:, :HD]
-                values[at, :HD] = block[:, HD:]
-                top_ref[16:32, :] = jnp.maximum(top_ref[16:32, :], highest_of(block[:, :HD]))
+                block_keys = block[start : start + rows, :HD]
+                keys[at, :] = block_keys
+                values[at, :HD] = block[start : start + rows, HD:]
+                top_ref[16:32, :] = jnp.maximum(top_ref[16:32, :], highest_of(block_keys))
 
             filled = filled + jnp.where(takes, rows // ROWS, 0)
         return filled
@@ -352,9 +355,8 @@
 def attend(mine, query, own, carry, blocks, numbers_of, kept=None, kept_numbers_of=None):
     first, last = carry is None, kept is not None
     kept = kept or []
-    size = sum(block.shape[0] for block in blocks)
-    size = 16 * ROWS if last else size
-    operands = [query, own] + list(carry or []) + list(blocks) + kept
+    size = 16 * ROWS if last else sum(rows for _, _, rows in blocks)
+    operands = [query, own] + list(carry or []) + [block for block, _, _ in blocks + kept]
     top = (32, HD)
     scratch = [
         pltpu.VMEM((HEADS, ROWS, 2 * HD), f32),
@@ -376,7 +378,15 @@
         if first:
             out_shape = (jax.ShapeDtypeStruct((ROWS, HEADS * HD), bf16),) + out_shape
     return pl.pallas_call(
-        functools.partial(attend_kernel, first, last, numbers_of, len(blocks), kept_numbers_of, len(kept)),
+        functools.partial(
+            attend_kernel,
+            first,
+            last,
+            numbers_of,
+            [block[1:] for block in blocks],
+            kept_numbers_of,
+            [block[1:] for block in kept],
+        ),
         out_shape=out_shape,
         in_specs=[SMEM] + [VMEM] * len(operands),
         out_specs=(VMEM,) * len(out_shape),
@@ -466,6 +476,8 @@
     every = range(16)
     sibling = [(i, i ^ 1) for i in every]
     sideways = [(i, i ^ 2) for i in every]
+    onward = [(i, i + 4) for i in every if i % 2 == 0 and i < 12] + [(i, i + 8) for i in every if i % 2 == 1 and i < 8]
+    wrapping = [(i, i + 12) for i in range(4)]
     last_plane = [(i, i + 4) for i in every if i % 2 == 0 and i < 12] + [(i, i + 12) for i in (1, 3)]
     plane_before = [(i, i + 8) for i in every if i % 2 == 1 and i < 8]
 
@@ -482,113 +494,99 @@
         for array in (att_query, lh_query, lh_key, lh_value, att_key, att_value)
     ]
     own = beside(att_key, att_value)
-    across = move(own, [(i, i ^ 2) for i in every if i < 4 or i % 4 < 2])
+    across = move(own, [(i, j) for i, j in sideways if i < 4 or i % 4 < 2])
+    wrapped = move(own, wrapping)
     near = move(own, sibling)
     chip = stack(own, near)
     chip, lh_step = tied(chip, lh_step)
     lh_step = pltpu.with_memory_space_constraint(lh_step, pltpu.HBM)
-    behind = move(chip, last_plane)
+    ring = move(chip, onward)
 
     local, grow, message = recur(lh_query, lh_key, lh_value, lh_step)
+
     def where(number, wanted):
         return jnp.where(wanted, number, NEVER)
 
     def parts(mine):
         return mine // 4, (mine // 2) % 2, mine % 2, mine - mine % 2
 
-    def brought(mine, core):
-        plane, _, _, even = parts(mine)
-        if core == 0:
-            return where(even - 4, plane >= 1)
-        return where(even - 12, plane == 3)
-
-    def behind_numbers(mine):
-        _, _, core, _ = parts(mine)
-        zero, one = brought(mine, 0), brought(mine, 1)
-        return [jnp.where(core == 0, zero, one), jnp.where(core == 0, one, zero)]
-
-    def beyond_numbers(mine):
-        plane, _, core, even = parts(mine)
-        number = where(even - 8, plane >= 2)
-        return [where(number, core == 1), where(number, core == 0)]
-
     def near_numbers(mine):
         return [where(mine - 1, mine % 2 == 1)]
+
+    def ring_numbers(mine):
+        plane, _, core, even = parts(mine)
+        one, two = where(even - 4, plane >= 1), where(even - 8, plane >= 2)
+        return [jnp.where(core == 0, one, two), jnp.where(core == 0, two, one)]
+
+    def wrapped_numbers(mine):
+        plane, _, _, even = parts(mine)
+        return [where(even - 12, plane == 3)] * 2
 
     def across_numbers(mine):
         _, side, _, even = parts(mine)
         return [where(even - 2, side == 1)] * 2
 
-    def behind_numbers(mine):
-        _, _, core, _ = parts(mine)
-        zero, one = brought(mine, 0), brought(mine, 1)
-        return [jnp.where(core == 0, zero, one), jnp.where(core == 0, one, zero)]
-
-    def beyond_numbers(mine):
-        plane, _, core, even = parts(mine)
-        number = where(even - 8, plane >= 2)
-        return [where(number, core == 1), where(number, core == 0)]
-
-    def first_numbers(mine):
-        _, side, core, even = parts(mine)
-        near_numbers = [where(mine - 1, core == 1)] + [where(even - 2, side == 1)] * 2
-        return near_numbers + behind_numbers(mine)
-
     def middle_numbers(mine):
-        return behind_numbers(mine) + beyond_numbers(mine)
+        return ring_numbers(mine) + wrapped_numbers(mine)
 
     def last_numbers(mine):
-        return across_numbers(mine) + beyond_numbers(mine)
-
-    near_query, *carry = attend(place, att_query, own, None, [near], near_numbers)
-    carry, message, across = tied(carry, message, across)
+        return ring_numbers(mine) + across_numbers(mine) + wrapped_numbers(mine)
+
+    first_pieces = [(near, 0, ROWS)]
+    near_query, *carry = attend(place, att_query, own, None, first_pieces, near_numbers)
+    carry, message, across, wrapped = tied(carry, message, across, wrapped)
     first = move(message, sibling)
+    wrapped_side = move(across, wrapping)
     (of_chip,) = join(join_cores_kernel, 1, place, message, first)
+    ring, of_chip = tied(ring, of_chip)
+    level = move(ring, [(i, j) for i, j in sideways if (i % 2 == 0 and i >= 4) or i >= 8])
     other_even = move(of_chip, [(i, j) for i, j in sideways if i % 2 == 0])
-
-    chip, behind, of_chip = tied(chip, behind, of_chip)
-    behind_near = move(behind, sibling)
-    level = move(behind, [(i, j) for i, j in sideways if (i % 2 == 0 and i >= 4) or i >= 12])
-    beyond = move(chip, plane_before)
-    carry = attend(place, near_query, own, carry, [behind, behind_near], behind_numbers)
-
-    carry, other_even, across, beyond, level = tied(carry, other_even, across, beyond, level)
+    bundle = stack(ring, wrapped)
+    bundle_near = move(bundle, sibling)
+    middle_pieces = [
+        (ring, 0, 2 * ROWS),
+        (bundle_near, 0, 2 * ROWS),
+        (wrapped, 0, ROWS),
+        (bundle_near, 2 * ROWS, ROWS),
+    ]
+    carry = attend(place, near_query, own, carry, middle_pieces, middle_numbers)
+
+    carry, other_even, across, wrapped_side, level = tied(carry, other_even, across, wrapped_side, level)
     other_odd = move(other_even, [(i, j) for i, j in sibling if i % 2 == 0])
-    level_beyond = move(beyond, [(i, j) for i, j in sideways if i % 2 == 1 and i >= 8])
-    across_near = move(across, sibling)
-    beyond_near = move(beyond, sibling)
     level_near = move(level, sibling)
+    rest = stack(across, wrapped_side)
+    rest_near = move(rest, sibling)
     of_plane, other_chip = join(join_sides_kernel, 2, place, of_chip, other_even, other_odd)
     state_behind = move(of_plane, last_plane)
     state_beyond = move(of_plane, plane_before)
-    middle_blocks = [level, level_near, beyond, beyond_near]
-    middle_blocks, of_plane = tied(middle_blocks, of_plane)
-    carry = attend(place, near_query, own, carry, middle_blocks, middle_numbers)
-
-    carry, level_beyond, state_behind, state_beyond = tied(carry, level_beyond, state_behind, state_beyond)
-    level_beyond_near = move(level_beyond, sibling)
-    kept = hand(place, state_behind, state_beyond)
-    handed = move(kept, sibling)
-    last_blocks = [across, across_near, level_beyond, level_beyond_near]
-    last_blocks, kept = tied(last_blocks, kept)
+    last_pieces = [
+        (level, 0, 2 * ROWS),
+        (level_near, 0, 2 * ROWS),
+        (across, 0, ROWS),
+        (rest_near, 0, ROWS),
+        (wrapped_side, 0, ROWS),
+        (rest_near, ROWS, ROWS),
+    ]
+    carry, of_plane = tied(carry, of_plane)
     attention, squares = attend(
         place,
         near_query,
         own,
         carry,
-        last_blocks,
+        last_pieces,
         last_numbers,
-        [near, behind, behind_near] + middle_blocks,
-        lambda mine: near_numbers(mine) + behind_numbers(mine) + middle_numbers(mine),
+        first_pieces + middle_pieces,
+        lambda mine: near_numbers(mine) + middle_numbers(mine),
     )
 
     def over(value, bit):
         return lax.ppermute(value, "tp", [(i, i ^ bit) for i in range(8)])
 
-    squares, handed = tied(squares, handed)
     others = [over(squares, bit) for bit in (2, 4, 6)]
+    others, state_behind, state_beyond = tied(others, state_behind, state_beyond)
+    kept = hand(place, state_behind, state_beyond)
+    handed = move(kept, sibling)
     linear = carry_in(place, lh_query, local, grow, kept, handed, other_chip, first, lh_gain)
-    others, linear = tied(others, linear)
     squares = squares + others[0] + others[1] + others[2]
     features = HEADS * HD * lax.axis_size("tp")
     return finish(float(features), attention, squares, over(squares, 1), linear, att_gain)

time: 227 us -> 221 us (0.974)
  starting transfers between devices: 171 us -> 25 us
  Pallas kernels: 46.2 us -> 185 us
    ppermute x4, starting transfers between devices: 145 us -> 4.92 us  [over(): return lax.ppermute(value, 'tp', [(i, i ^ bit) for i in range(8)])]
    pallas_call x4 -> x3, Pallas kernels: 35.8 us -> 175 us  [attend(): pl.pallas_call(functools.partial(attend_kernel, first, last, numbers_of,...]
    ppermute x17 -> x15, starting transfers between devices: 25.4 us -> 20.1 us  [move(): return lax.ppermute(value, 'ctx', pairs)]
    ppermute x17 -> x15, waiting for transfers between devices: 6.8 us -> 6.69 us  [move(): return lax.ppermute(value, 'ctx', pairs)]
  transfers between devices with their start and end apart: 21 -> 19, of which waited for: 5 -> 6; matrix products, arithmetic and copies ran while one was open for 0% -> 0% of each run, Pallas kernels for 19% -> 83%
where the time goes in v4:
time: 221 us
  Pallas kernels  185 us (84%)
  starting transfers between devices  25 us (11%)
  waiting for transfers between devices  10.5 us (5%)
    pallas_call x3, Pallas kernels, attend(): pl.pallas_call(functools.partial(attend_kernel, first, last, numbers_of,...  175 us
    ppermute x15, starting transfers between devices, move(): return lax.ppermute(value, 'ctx', pairs)  20.1 us
    ppermute x15, waiting for transfers between devices, move(): return lax.ppermute(value, 'ctx', pairs)  6.69 us
    pallas_call x1, Pallas kernels, recur(): pl.pallas_call(recur_kernel, out_shape=(jax.ShapeDtypeStruct((ROWS, HEADS...  5.04 us
    ppermute x4, starting transfers between devices, over(): return lax.ppermute(value, 'tp', [(i, i ^ bit) for i in range(8)])  4.92 us
  transfers between devices with their start and end apart: 19, of which 6 were waited for; matrix products, arithmetic and copies ran while one was open for 0% of the time, Pallas kernels for 83%

profile of v4, /device:TPU:101, one launch (start us, length us, event | category | flops | bytes accessed | tf_op | source)
XLA Modules:
  0.0 221.0 jit_solution(4739054263184017828)
XLA Ops:
  0.0 1.0 beside.1.own_ref.refs_0_
  1.0 0.8 collective-permute-start
  1.8 1.3 collective-permute-start.1
  3.1 1.3 collective-permute-start.2
  4.4 0.0 collective-permute-done.refs_0_.refs_1_.refs_9_
  4.4 1.3 collective-permute-start.3
  5.7 5.0 %recur.1 = (f32[512,768]{1,0:T(8,128)S(1)}, f32[512,128]{1,0:T(8,128)S(1)}, f32[776,128]{1,0:T(8,128)S(1)}) custom-call(bf16[512,768]{1,0:T(8,128)(2,1)} %query_hbm.1, bf16[512,768]{1,0:T(8,128)(2,1)} %k_hbm.1, bf16[512,768]{1,0:T(8,128)(2,1)} %v_hbm.1, f32[6,512]{1,0:T(8,128)} %bitcast.2), custom_call_target="tpu_custom_call" | custom-call | flops 200000000 | bytes 200000 | tf_op jit(solution)/shard_map/recur/pallas_call | solution.py:91
  10.8 5.3 %attend_first.1 = (bf16[512,768]{1,0:T(8,128)(2,1)S(1)}, f32[512,768]{1,0:T(8,128)S(1)}, f32[512,128]{1,0:T(8,128)S(1)}, bf16[32,128]{1,0:T(8,128)(2,1)S(1)}) custom-call(s32[1]{0:T(128)} %bitcast.mine_ref, bf16[512,768]{1,0:T(8,128)(2,1)} %query_ref.1, bf16[512,256]{1,0:T(8,128)(2,1)S(1)} %beside.1.own_ref.refs_0_, ...), custom_call_target="tpu_custom_call" | custom-call | flops 200000000 | bytes 200000 | tf_op jit(solution)/shard_map/attend_first/pallas_call | solution.py:380
  16.0 0.0 collective-permute-done.1.refs_0_.refs_5_
  16.0 3.6 %collective-permute-done.2.refs_1_.refs_5_.refs_12_ = bf16[512,256]{1,0:T(8,128)(2,1)S(1)} collective-permute-done((bf16[512,256]{1,0:T(8,128)(2,1)S(1)}, bf16[512,256]{1,0:T(8,128)(2,1)S(1)}, u32[]{:S(2)}, u32[]{:S(2)}) %collective-permute-start.2) | collective-permute-done | bytes 262176 | tf_op jit(solution)/shard_map/ppermute | solution.py:474
  19.7 0.8 collective-permute-start.4
  20.5 1.4 collective-permute-done.4.other_ref.core_ref
  21.9 0.1 join.2.own_ref
  21.9 0.0 collective-permute-done.3.refs_0_.refs_3_.refs_10_
  21.9 0.1 stack.4
  22.0 0.5 collective-permute-start.5
  22.5 5.5 %collective-permute-start.8 = (bf16[1024,256]{1,0:T(8,128)(2,1)S(1)}, bf16[1024,256]{1,0:T(8,128)(2,1)S(1)}, u32[]{:S(2)}, u32[]{:S(2)}) collective-permute-start(bf16[1024,256]{1,0:T(8,128)(2,1)S(1)} %collective-permute-done.3.refs_0_.refs_3_.refs_10_), channel_id=1, source_target_pairs={{32,48},{48,32},{64,80},{72,88},{80,64},{88,72},{96,112},{104,120}... | collective-permute-start | bytes 1572872 | tf_op jit(solution)/shard_map/ppermute | solution.py:474
  28.0 0.7 collective-permute-start.6
  28.7 1.3 collective-permute-start.7
  30.0 0.0 collective-permute-done.5.refs_4_.refs_6_.refs_11_.refs_13_
  30.0 12.5 %attend_middle.1 = (f32[512,768]{1,0:T(8,128)S(1)}, f32[512,128]{1,0:T(8,128)S(1)}, bf16[32,128]{1,0:T(8,128)(2,1)S(1)}) custom-call(s32[1]{0:T(128)} %bitcast.mine_ref, bf16[512,768]{1,0:T(8,128)(2,1)S(1)} %get-tuple-element.44.query_ref, bf16[512,256]{1,0:T(8,128)(2,1)S(1)} %beside.1.own_ref.refs_0_, f32[512,768]{1,0:T(8,128)S(1)} %get-tuple-element.50.refs_0_, ...), custom_call_target="tpu_custom_call" | custom-call | flops 200000000 | bytes 200000 | tf_op jit(solution)/shard_map/attend_middle/pallas_call | solution.py:380
  42.5 0.0 collective-permute-done.7.refs_1_.refs_7_
  42.5 0.0 collective-permute-done.6.even_ref
  42.5 0.0 collective-permute-done.8.refs_3_
  42.5 1.3 collective-permute-start.9
  43.8 2.7 %collective-permute-start.11 = (bf16[1024,256]{1,0:T(8,128)(2,1)S(1)}, bf16[1024,256]{1,0:T(8,128)(2,1)S(1)}, u32[]{:S(2)}, u32[]{:S(2)}) collective-permute-start(bf16[1024,256]{1,0:T(8,128)(2,1)S(1)} %stack.5), channel_id=1, source_target_pairs={{0,8},{8,0},{16,24},{24,16},{32,40},{40,32},{48,56},{56,48},{64,72... | collective-permute-start | bytes 1572872 | tf_op jit(solution)/shard_map/ppermute | solution.py:474
  46.5 0.1 collective-permute-start.10
  46.6 1.0 collective-permute-done.9.odd_ref
  47.6 0.1 join.3
  47.7 0.0 copy-start.1
  47.7 1.3 collective-permute-start.15
  49.0 1.3 collective-permute-start.16
  50.3 0.0 collective-permute-done.11.refs_6_.refs_8_
  50.3 0.0 collective-permute-done.10.refs_4_
  50.4 156.9 %attend_last.1 = (bf16[512,768]{1,0:T(8,128)(2,1)S(1)}, f32[8,512]{1,0:T(8,128)S(1)}) custom-call(s32[1]{0:T(128)} %bitcast.mine_ref, bf16[512,768]{1,0:T(8,128)(2,1)S(1)} %get-tuple-element.44.query_ref, bf16[512,256]{1,0:T(8,128)(2,1)S(1)} %beside.1.own_ref.refs_0_, f32[512,768]{1,0:T(8,128)S(1)} %get-tuple-element.67.refs_0_, ...), custom_call_target="tpu_custom_call" | custom-call | flops 200000000 | bytes 200000 | tf_op jit(solution)/shard_map/attend_last/pallas_call | solution.py:380
  207.3 1.3 collective-permute-start.12
  208.6 2.6 %collective-permute-start.13 = (f32[8,512]{1,0:T(8,128)S(1)}, f32[8,512]{1,0:T(8,128)S(1)}, u32[]{:S(2)}, u32[]{:S(2)}) collective-permute-start(f32[8,512]{1,0:T(8,128)S(1)} %get-tuple-element.74), channel_id=1, source_target_pairs={{0,4},{1,5},{2,6},{3,7},{4,0},{5,1},{6,2},{7,3},{8,12},{9,13},{10,... | collective-permute-start | bytes 49160 | tf_op jit(solution)/shard_map/ppermute | solution.py:583
  211.2 0.0 collective-permute-start.14
  211.2 0.0 collective-permute-done.12
  211.2 1.5 collective-permute-done.13
  212.7 2.3 %collective-permute-done.14 = f32[8,512]{1,0:T(8,128)S(1)} collective-permute-done((f32[8,512]{1,0:T(8,128)S(1)}, f32[8,512]{1,0:T(8,128)S(1)}, u32[]{:S(2)}, u32[]{:S(2)}) %collective-permute-start.14) | collective-permute-done | bytes 16416 | tf_op jit(solution)/shard_map/ppermute | solution.py:583
  215.0 0.0 collective-permute-done.15.behind_ref
  215.0 0.0 collective-permute-done.16.beyond_ref
  215.0 0.1 hand.1.kept_ref
  215.1 0.1 collective-permute-start.18
  215.2 1.0 collective-permute-start.17
  216.2 0.7 collective-permute-done.18.handed_ref
  216.9 0.0 copy-done.1
  216.9 0.0 copy-start
  216.9 2.5 %carry.1.linear_ref = f32[512,768]{1,0:T(8,128)S(1)} custom-call(s32[1]{0:T(128)} %bitcast.mine_ref, bf16[512,768]{1,0:T(8,128)(2,1)} %query_hbm.1, f32[512,768]{1,0:T(8,128)S(1)} %get-tuple-element.78.local_ref, f32[512,128]{1,0:T(8,128)S(1)} %get-tuple-element.79.grow_ref, f32[776,128]{1,0:T(8,128)S(1)} %hand.1.kept_ref, ...), custom_call_target="tpu_custom_call" | custom-call | flops 200000000 | bytes 200000 | tf_op jit(solution)/shard_map/carry/pallas_call | solution.py:446
  219.4 0.0 collective-permute-done.17.other_ref
  219.4 0.0 copy-done
  219.5 1.5 finish.1
  (3 shorter events, 0.1 us)
Async XLA Ops:
  1.0 3.3 %collective-permute-start = (bf16[512,256]{1,0:T(8,128)(2,1)S(1)}, bf16[512,256]{1,0:T(8,128)(2,1)S(1)}, u32[]{:S(2)}, u32[]{:S(2)}) collective-permute-start(bf16[512,256]{1,0:T(8,128)(2,1)S(1)} %beside.1.own_ref.refs_0_), channel_id=1, source_target_pairs={{0,8},{8,0},{16,24},{24,16},{32,40},{40,32},{48,56},{56,48},{64,72... | collective-permute-start | bytes 786440 | tf_op jit(solution)/shard_map/ppermute | solution.py:474
  1.8 14.3 %collective-permute-start.1 = (bf16[512,256]{1,0:T(8,128)(2,1)S(1)}, bf16[512,256]{1,0:T(8,128)(2,1)S(1)}, u32[]{:S(2)}, u32[]{:S(2)}) collective-permute-start(bf16[512,256]{1,0:T(8,128)(2,1)S(1)} %beside.1.own_ref.refs_0_), channel_id=1, source_target_pairs={{0,16},{8,24},{16,0},{24,8},{32,48},{40,56},{64,80},{72,88},{96,11... | collective-permute-start | bytes 786440 | tf_op jit(solution)/shard_map/ppermute | solution.py:474
  3.1 16.6 %collective-permute-start.2 = (bf16[512,256]{1,0:T(8,128)(2,1)S(1)}, bf16[512,256]{1,0:T(8,128)(2,1)S(1)}, u32[]{:S(2)}, u32[]{:S(2)}) collective-permute-start(bf16[512,256]{1,0:T(8,128)(2,1)S(1)} %beside.1.own_ref.refs_0_), channel_id=1, source_target_pairs={{0,96},{8,104},{16,112},{24,120},{1,97},{9,105},{17,113},{25,121},... | collective-permute-start | bytes 786440 | tf_op jit(solution)/shard_map/ppermute | solution.py:474
  4.4 17.5 %collective-permute-start.3 = (bf16[1024,256]{1,0:T(8,128)(2,1)S(1)}, bf16[1024,256]{1,0:T(8,128)(2,1)S(1)}, u32[]{:S(2)}, u32[]{:S(2)}) collective-permute-start(bf16[1024,256]{1,0:T(8,128)(2,1)S(1)} %stack.3), channel_id=1, source_target_pairs={{0,32},{16,48},{32,64},{48,80},{64,96},{80,112},{8,72},{24,88},{40... | collective-permute-start | bytes 1572872 | tf_op jit(solution)/shard_map/ppermute | solution.py:474
  19.7 2.2 collective-permute-start.4
  22.0 8.0 %collective-permute-start.5 = (bf16[1536,256]{1,0:T(8,128)(2,1)S(1)}, bf16[1536,256]{1,0:T(8,128)(2,1)S(1)}, u32[]{:S(2)}, u32[]{:S(2)}) collective-permute-start(bf16[1536,256]{1,0:T(8,128)(2,1)S(1)} %stack.4), channel_id=1, source_target_pairs={{0,8},{8,0},{16,24},{24,16},{32,40},{40,32},{48,56},{56,48},{64,72... | collective-permute-start | bytes 2359304 | tf_op jit(solution)/shard_map/ppermute | solution.py:474
  22.5 20.0 %collective-permute-start.8 = (bf16[1024,256]{1,0:T(8,128)(2,1)S(1)}, bf16[1024,256]{1,0:T(8,128)(2,1)S(1)}, u32[]{:S(2)}, u32[]{:S(2)}) collective-permute-start(bf16[1024,256]{1,0:T(8,128)(2,1)S(1)} %collective-permute-done.3.refs_0_.refs_3_.refs_10_), channel_id=1, source_target_pairs={{32,48},{48,32},{64,80},{72,88},{80,64},{88,72},{96,112},{104,120}... | collective-permute-start | bytes 1572872 | tf_op jit(solution)/shard_map/ppermute | solution.py:474
  28.0 14.5 %collective-permute-start.6 = (f32[776,128]{1,0:T(8,128)S(1)}, f32[776,128]{1,0:T(8,128)S(1)}, u32[]{:S(2)}, u32[]{:S(2)}) collective-permute-start(f32[776,128]{1,0:T(8,128)S(1)} %join.2.own_ref), channel_id=1, source_target_pairs={{0,16},{16,0},{32,48},{48,32},{64,80},{80,64},{96,112},{112,96},{1... | collective-permute-start | bytes 1191944 | tf_op jit(solution)/shard_map/ppermute | solution.py:474
  28.7 13.8 %collective-permute-start.7 = (bf16[512,256]{1,0:T(8,128)(2,1)S(1)}, bf16[512,256]{1,0:T(8,128)(2,1)S(1)}, u32[]{:S(2)}, u32[]{:S(2)}) collective-permute-start(bf16[512,256]{1,0:T(8,128)(2,1)S(1)} %collective-permute-done.1.refs_0_.refs_5_), channel_id=1, source_target_pairs={{0,96},{8,104},{16,112},{24,120},{1,97},{9,105},{17,113},{25,121},... | collective-permute-start | bytes 786440 | tf_op jit(solution)/shard_map/ppermute | solution.py:474
  42.5 5.1 %collective-permute-start.9 = (f32[776,128]{1,0:T(8,128)S(1)}, f32[776,128]{1,0:T(8,128)S(1)}, u32[]{:S(2)}, u32[]{:S(2)}) collective-permute-start(f32[776,128]{1,0:T(8,128)S(1)} %collective-permute-done.6.even_ref), channel_id=1, source_target_pairs={{0,8},{16,24},{32,40},{48,56},{64,72},{80,88},{96,104},{112,120},{... | collective-permute-start | bytes 1191944 | tf_op jit(solution)/shard_map/ppermute | solution.py:474
  43.8 6.5 %collective-permute-start.11 = (bf16[1024,256]{1,0:T(8,128)(2,1)S(1)}, bf16[1024,256]{1,0:T(8,128)(2,1)S(1)}, u32[]{:S(2)}, u32[]{:S(2)}) collective-permute-start(bf16[1024,256]{1,0:T(8,128)(2,1)S(1)} %stack.5), channel_id=1, source_target_pairs={{0,8},{8,0},{16,24},{24,16},{32,40},{40,32},{48,56},{56,48},{64,72... | collective-permute-start | bytes 1572872 | tf_op jit(solution)/shard_map/ppermute | solution.py:474
  46.5 3.8 %collective-permute-start.10 = (bf16[1024,256]{1,0:T(8,128)(2,1)S(1)}, bf16[1024,256]{1,0:T(8,128)(2,1)S(1)}, u32[]{:S(2)}, u32[]{:S(2)}) collective-permute-start(bf16[1024,256]{1,0:T(8,128)(2,1)S(1)} %collective-permute-done.8.refs_3_), channel_id=1, source_target_pairs={{0,8},{8,0},{16,24},{24,16},{32,40},{40,32},{48,56},{56,48},{64,72... | collective-permute-start | bytes 1572872 | tf_op jit(solution)/shard_map/ppermute | solution.py:474
  47.7 169.2 %copy-start.1 = (f32[768]{0:T(1024)S(1)}, f32[768]{0:T(1024)}, u32[]{:S(2)}) copy-start(f32[768]{0:T(1024)} %gain_ref.2) | copy-start | bytes 9220
  47.7 167.3 %collective-permute-start.15 = (f32[776,128]{1,0:T(8,128)S(1)}, f32[776,128]{1,0:T(8,128)S(1)}, u32[]{:S(2)}, u32[]{:S(2)}) collective-permute-start(f32[776,128]{1,0:T(8,128)S(1)} %get-tuple-element.66), channel_id=1, source_target_pairs={{0,32},{16,48},{32,64},{48,80},{64,96},{80,112},{8,104},{24,120},{... | collective-permute-start | bytes 1191944 | tf_op jit(solution)/shard_map/ppermute | solution.py:474
  49.0 166.0 %collective-permute-start.16 = (f32[776,128]{1,0:T(8,128)S(1)}, f32[776,128]{1,0:T(8,128)S(1)}, u32[]{:S(2)}, u32[]{:S(2)}) collective-permute-start(f32[776,128]{1,0:T(8,128)S(1)} %get-tuple-element.66), channel_id=1, source_target_pairs={{8,72},{24,88},{40,104},{56,120},{9,73},{25,89},{41,105},{57,121},... | collective-permute-start | bytes 1191944 | tf_op jit(solution)/shard_map/ppermute | solution.py:474
  207.3 3.9 %collective-permute-start.12 = (f32[8,512]{1,0:T(8,128)S(1)}, f32[8,512]{1,0:T(8,128)S(1)}, u32[]{:S(2)}, u32[]{:S(2)}) collective-permute-start(f32[8,512]{1,0:T(8,128)S(1)} %get-tuple-element.74), channel_id=1, source_target_pairs={{0,2},{1,3},{2,0},{3,1},{4,6},{5,7},{6,4},{7,5},{8,10},{9,11},{10,... | collective-permute-start | bytes 49160 | tf_op jit(solution)/shard_map/ppermute | solution.py:583
  208.6 4.1 %collective-permute-start.13 = (f32[8,512]{1,0:T(8,128)S(1)}, f32[8,512]{1,0:T(8,128)S(1)}, u32[]{:S(2)}, u32[]{:S(2)}) collective-permute-start(f32[8,512]{1,0:T(8,128)S(1)} %get-tuple-element.74), channel_id=1, source_target_pairs={{0,4},{1,5},{2,6},{3,7},{4,0},{5,1},{6,2},{7,3},{8,12},{9,13},{10,... | collective-permute-start | bytes 49160 | tf_op jit(solution)/shard_map/ppermute | solution.py:583
  211.2 3.8 %collective-permute-start.14 = (f32[8,512]{1,0:T(8,128)S(1)}, f32[8,512]{1,0:T(8,128)S(1)}, u32[]{:S(2)}, u32[]{:S(2)}) collective-permute-start(f32[8,512]{1,0:T(8,128)S(1)} %get-tuple-element.74), channel_id=1, source_target_pairs={{0,6},{1,7},{2,4},{3,5},{4,2},{5,3},{6,0},{7,1},{8,14},{9,15},{10,... | collective-permute-start | bytes 49160 | tf_op jit(solution)/shard_map/ppermute | solution.py:583
  215.1 1.8 collective-permute-start.18
  215.2 4.2 %collective-permute-start.17 = (f32[8,512]{1,0:T(8,128)S(1)}, f32[8,512]{1,0:T(8,128)S(1)}, u32[]{:S(2)}, u32[]{:S(2)}) collective-permute-start(f32[8,512]{1,0:T(8,128)S(1)} %add_add_fusion.square_ref), channel_id=1, source_target_pairs={{0,1},{1,0},{2,3},{3,2},{4,5},{5,4},{6,7},{7,6},{8,9},{9,8},{10,11... | collective-permute-start | bytes 49160 | tf_op jit(solution)/shard_map/ppermute | solution.py:583
  216.9 2.5 %copy-start = (f32[768]{0:T(1024)S(1)}, f32[768]{0:T(1024)}, u32[]{:S(2)}) copy-start(f32[768]{0:T(1024)} %gain_ref.3) | copy-start | bytes 9220

commit v5 on v4

--- a/solution.py
+++ b/solution.py
@@ -18,6 +18,8 @@
 SCORE_SCALE = LOG2E / math.sqrt(HD)
 SAFE_EXPONENT = 100.0
 STATE_ROWS = HEADS * HD + 8
+HALF = HEADS // 2
+BLOCKS = 2 * ROWS
 NEVER = 1 << 20
 
 VMEM = pl.BlockSpec(memory_space=pltpu.VMEM)
@@ -160,19 +162,6 @@
     ref[HEADS * HD :, :] = value[1]
 
 
-def join_cores_kernel(mine_ref, own_ref, other_ref, out_ref):
-    own, other = state_of(own_ref), state_of(other_ref)
-    put_state(out_ref, follow_in_order(mine_ref[0] % 2 == 0, own, other))
-
-
-def join_sides_kernel(mine_ref, own_ref, even_ref, odd_ref, out_ref, other_ref):
-    mine = mine_ref[0]
-    own, even, odd = state_of(own_ref), state_of(even_ref), state_of(odd_ref)
-    other = select(mine % 2 == 0, even, odd)
-    put_state(other_ref, other)
-    put_state(out_ref, follow_in_order((mine // 2) % 2 == 0, own, other))
-
-
 def select(wanted, one, two):
     return [jnp.where(wanted, a, b) for a, b in zip(one[0], two[0])], jnp.where(wanted, one[1], two[1])
 
@@ -181,16 +170,67 @@
     return follow(select(own_first, own, other), select(own_first, other, own))
 
 
-def join(kernel, outputs, mine, *messages):
-    return pl.pallas_call(
-        kernel,
-        out_shape=(jax.ShapeDtypeStruct((STATE_ROWS, HD), f32),) * outputs,
-        in_specs=[SMEM] + [VMEM] * len(messages),
-        out_specs=(VMEM,) * outputs,
+def split(value):
+    upper = value.astype(bf16)
+    return jnp.concatenate([upper, (value - upper.astype(f32)).astype(bf16)], 1)
+
+
+def merge(both):
+    return both[:, :HD].astype(f32) + both[:, HD:].astype(f32)
+
+
+def join_cores_kernel(mine_ref, own_ref, other_ref, blocks_ref, out_ref, message_ref):
+    even = mine_ref[0] % 2 == 0
+    joined = follow_in_order(even, state_of(own_ref), state_of(other_ref))
+    put_state(out_ref, joined)
+    message_ref[:BLOCKS, :] = blocks_ref[...]
+    for h in range(HALF):
+        at = BLOCKS + h * HD
+        message_ref[at : at + HD, :] = split(jnp.where(even, joined[0][h], joined[0][HALF + h]))
+    logs = jnp.concatenate([joined[1], jnp.zeros((8, HD), f32)], 0)
+    message_ref[BLOCKS + HALF * HD :, :] = split(logs)
+
+
+def join_cores(mine, own, other, blocks):
+    return pl.pallas_call(
+        join_cores_kernel,
+        out_shape=(
+            jax.ShapeDtypeStruct((STATE_ROWS, HD), f32),
+            jax.ShapeDtypeStruct((BLOCKS + HALF * HD + 16, 2 * HD), bf16),
+        ),
+        in_specs=[SMEM] + [VMEM] * 3,
+        out_specs=(VMEM,) * 2,
         compiler_params=params(14),
         cost_estimate=cost(0.2),
-        name="join",
-    )(mine, *messages)
+        name="join_cores",
+    )(mine, own, other, blocks)
+
+
+def join_sides_kernel(mine_ref, own_ref, level_ref, level_near_ref, out_ref, other_ref):
+    mine = mine_ref[0]
+    even = mine % 2 == 0
+    states = [None] * HEADS
+    for h in range(HALF):
+        at = slice(BLOCKS + h * HD, BLOCKS + (h + 1) * HD)
+        here, there = merge(level_ref[at, :]), merge(level_near_ref[at, :])
+        states[h] = jnp.where(even, here, there)
+        states[HALF + h] = jnp.where(even, there, here)
+    logs = merge(level_ref[BLOCKS + HALF * HD :, :])[:8, :]
+    other = states, logs
+    put_state(other_ref, other)
+    put_state(out_ref, follow_in_order((mine // 2) % 2 == 0, state_of(own_ref), other))
+
+
+def join_sides(mine, own, level, level_near):
+    return pl.pallas_call(
+        join_sides_kernel,
+        out_shape=(jax.ShapeDtypeStruct((STATE_ROWS, HD), f32),) * 2,
+        in_specs=[SMEM] + [VMEM] * 3,
+        out_specs=(VMEM,) * 2,
+        compiler_params=params(14),
+        cost_estimate=cost(0.2),
+        name="join_sides",
+    )(mine, own, level, level_near)
 
 
 def hand_kernel(mine_ref, behind_ref, beyond_ref, out_ref):
@@ -534,13 +574,12 @@
 
     first_pieces = [(near, 0, ROWS)]
     near_query, *carry = attend(place, att_query, own, None, first_pieces, near_numbers)
-    carry, message, across, wrapped = tied(carry, message, across, wrapped)
     first = move(message, sibling)
+    carry, first = tied(carry, first)
+    of_chip, leveled = join_cores(place, message, first, ring)
+    level = move(leveled, sideways)
+    of_chip, wrapped, across = tied(of_chip, wrapped, across)
     wrapped_side = move(across, wrapping)
-    (of_chip,) = join(join_cores_kernel, 1, place, message, first)
-    ring, of_chip = tied(ring, of_chip)
-    level = move(ring, [(i, j) for i, j in sideways if (i % 2 == 0 and i >= 4) or i >= 8])
-    other_even = move(of_chip, [(i, j) for i, j in sideways if i % 2 == 0])
     bundle = stack(ring, wrapped)
     bundle_near = move(bundle, sibling)
     middle_pieces = [
@@ -551,12 +590,11 @@
     ]
     carry = attend(place, near_query, own, carry, middle_pieces, middle_numbers)
 
-    carry, other_even, across, wrapped_side, level = tied(carry, other_even, across, wrapped_side, level)
-    other_odd = move(other_even, [(i, j) for i, j in sibling if i % 2 == 0])
+    carry, across, wrapped_side, level = tied(carry, across, wrapped_side, level)
     level_near = move(level, sibling)
     rest = stack(across, wrapped_side)
     rest_near = move(rest, sibling)
-    of_plane, other_chip = join(join_sides_kernel, 2, place, of_chip, other_even, other_odd)
+    of_plane, other_chip = join_sides(place, of_chip, level, level_near)
     state_behind = move(of_plane, last_plane)
     state_beyond = move(of_plane, plane_before)
     last_pieces = [
@@ -582,11 +620,12 @@
     def over(value, bit):
         return lax.ppermute(value, "tp", [(i, i ^ bit) for i in range(8)])
 
+    squares, state_behind, state_beyond = tied(squares, state_behind, state_beyond)
     others = [over(squares, bit) for bit in (2, 4, 6)]
-    others, state_behind, state_beyond = tied(others, state_behind, state_beyond)
     kept = hand(place, state_behind, state_beyond)
     handed = move(kept, sibling)
     linear = carry_in(place, lh_query, local, grow, kept, handed, other_chip, first, lh_gain)
+    others, linear = tied(others, linear)
     squares = squares + others[0] + others[1] + others[2]
     features = HEADS * HD * lax.axis_size("tp")
     return finish(float(features), attention, squares, over(squares, 1), linear, att_gain)

time: 221 us -> 222 us (level); the launches traced: 221 us -> 219 us
  starting transfers between devices: 25 us -> 19.6 us
  Pallas kernels: 185 us -> 188 us
    ppermute x15 -> x13, starting transfers between devices: 20.1 us -> 14.5 us  [move(): return lax.ppermute(value, 'ctx', pairs)]
    ppermute x15 -> x13, waiting for transfers between devices: 6.69 us -> 8.74 us  [move(): return lax.ppermute(value, 'ctx', pairs)]
  transfers between devices with their start and end apart: 19 -> 17, of which waited for: 6 -> 7; matrix products, arithmetic and copies ran while one was open for 0% -> 0% of each run, Pallas kernels for 83% -> 84%
where the time goes in v5:
time: 222 us; the launch traced here: 219 us
  Pallas kernels  188 us (85%)
  starting transfers between devices  19.6 us (9%)
  waiting for transfers between devices  10.8 us (5%)
    pallas_call x3, Pallas kernels, attend(): pl.pallas_call(functools.partial(attend_kernel, first, last, numbers_of,...  175 us
    ppermute x13, starting transfers between devices, move(): return lax.ppermute(value, 'ctx', pairs)  14.5 us
    ppermute x13, waiting for transfers between devices, move(): return lax.ppermute(value, 'ctx', pairs)  8.74 us
    pallas_call x1, Pallas kernels, recur(): pl.pallas_call(recur_kernel, out_shape=(jax.ShapeDtypeStruct((ROWS, HEADS...  5.79 us
    ppermute x4, starting transfers between devices, over(): return lax.ppermute(value, 'tp', [(i, i ^ bit) for i in range(8)])  5.11 us
  transfers between devices with their start and end apart: 17, of which 7 were waited for; matrix products, arithmetic and copies ran while one was open for 0% of the time, Pallas kernels for 84%

profile of v5, /device:TPU:101, one launch (start us, length us, event | category | flops | bytes accessed | tf_op | source)
XLA Modules:
  0.0 219.1 jit_solution(16905517266505673710)
XLA Ops:
  0.0 1.0 beside.1.own_ref.refs_0_
  1.0 0.8 collective-permute-start
  1.8 1.2 collective-permute-done.refs_0_.refs_1_.refs_9_
  2.9 0.8 stack.3
  3.8 1.3 collective-permute-start.2
  5.0 5.8 %recur.1 = (f32[512,768]{1,0:T(8,128)S(1)}, f32[512,128]{1,0:T(8,128)S(1)}, f32[776,128]{1,0:T(8,128)}) custom-call(bf16[512,768]{1,0:T(8,128)(2,1)} %query_hbm.1, bf16[512,768]{1,0:T(8,128)(2,1)} %k_hbm.1, bf16[512,768]{1,0:T(8,128)(2,1)} %v_hbm.1, f32[6,512]{1,0:T(8,128)} %bitcast.2), custom_call_target="tpu_custom_call" | custom-call | flops 200000000 | bytes 200000 | tf_op jit(solution)/shard_map/recur/pallas_call | solution.py:93
  10.8 0.0 copy-start
  10.8 0.7 copy-done
  11.5 0.4 collective-permute-start.1
  11.9 1.3 collective-permute-start.4
  13.2 1.3 collective-permute-start.3
  14.5 5.3 %attend_first.1 = (bf16[512,768]{1,0:T(8,128)(2,1)S(1)}, f32[512,768]{1,0:T(8,128)S(1)}, f32[512,128]{1,0:T(8,128)S(1)}, bf16[32,128]{1,0:T(8,128)(2,1)S(1)}) custom-call(s32[1]{0:T(128)} %bitcast.mine_ref, bf16[512,768]{1,0:T(8,128)(2,1)} %query_ref.1, bf16[512,256]{1,0:T(8,128)(2,1)S(1)} %beside.1.own_ref.refs_0_, ...), custom_call_target="tpu_custom_call" | custom-call | flops 200000000 | bytes 200000 | tf_op jit(solution)/shard_map/attend_first/pallas_call | solution.py:420
  19.8 0.0 collective-permute-done.1.other_ref.core_ref
  19.8 0.0 collective-permute-done.2.blocks_ref.refs_0_.refs_3_.refs_10_
  19.8 1.1 join_cores.1
  20.9 2.1 collective-permute-done.4.refs_0_.refs_5_
  23.1 0.9 collective-permute-done.3.refs_1_.refs_5_.refs_12_
  24.0 0.1 stack.4
  24.1 1.4 collective-permute-start.5
  25.5 3.3 %collective-permute-start.7 = (bf16[1424,256]{1,0:T(8,128)(2,1)S(1)}, bf16[1424,256]{1,0:T(8,128)(2,1)S(1)}, u32[]{:S(2)}, u32[]{:S(2)}) collective-permute-start(bf16[1424,256]{1,0:T(8,128)(2,1)S(1)} %get-tuple-element.63), channel_id=1, source_target_pairs={{0,16},{8,24},{16,0},{24,8},{32,48},{40,56},{48,32},{56,40},{64,80... | collective-permute-start | bytes 2187272 | tf_op jit(solution)/shard_map/ppermute | solution.py:514
  28.8 1.3 collective-permute-start.6
  30.1 0.0 collective-permute-done.5.refs_4_.refs_6_.refs_11_.refs_13_
  30.1 12.5 %attend_middle.1 = (f32[512,768]{1,0:T(8,128)S(1)}, f32[512,128]{1,0:T(8,128)S(1)}, bf16[32,128]{1,0:T(8,128)(2,1)S(1)}) custom-call(s32[1]{0:T(128)} %bitcast.mine_ref, bf16[512,768]{1,0:T(8,128)(2,1)S(1)} %get-tuple-element.46.query_ref, bf16[512,256]{1,0:T(8,128)(2,1)S(1)} %beside.1.own_ref.refs_0_, f32[512,768]{1,0:T(8,128)S(1)} %get-tuple-element.52.refs_0_, ...), custom_call_target="tpu_custom_call" | custom-call | flops 200000000 | bytes 200000 | tf_op jit(solution)/shard_map/attend_middle/pallas_call | solution.py:420
  42.6 0.0 collective-permute-done.6.refs_1_.refs_7_
  42.6 2.8 %collective-permute-done.7.level_ref.refs_3_ = bf16[1424,256]{1,0:T(8,128)(2,1)S(1)} collective-permute-done((bf16[1424,256]{1,0:T(8,128)(2,1)S(1)}, bf16[1424,256]{1,0:T(8,128)(2,1)S(1)}, u32[]{:S(2)}, u32[]{:S(2)}) %collective-permute-start.7) | collective-permute-done | bytes 729120 | tf_op jit(solution)/shard_map/ppermute | solution.py:514
  45.3 0.7 collective-permute-start.8
  46.1 0.1 collective-permute-start.9
  46.2 1.7 collective-permute-done.8.level_near_ref.refs_4_
  47.9 0.2 join_sides.1
  48.0 0.0 copy-start.1
  48.0 0.0 copy-start.3
  48.0 1.4 collective-permute-start.11
  49.5 1.3 collective-permute-start.10
  50.8 0.0 collective-permute-done.9.refs_6_.refs_8_
  50.8 156.9 %attend_last.1 = (bf16[512,768]{1,0:T(8,128)(2,1)S(1)}, f32[8,512]{1,0:T(8,128)S(1)}) custom-call(s32[1]{0:T(128)} %bitcast.mine_ref, bf16[512,768]{1,0:T(8,128)(2,1)S(1)} %get-tuple-element.46.query_ref, bf16[512,256]{1,0:T(8,128)(2,1)S(1)} %beside.1.own_ref.refs_0_, f32[512,768]{1,0:T(8,128)S(1)} %get-tuple-element.70.refs_0_, ...), custom_call_target="tpu_custom_call" | custom-call | flops 200000000 | bytes 200000 | tf_op jit(solution)/shard_map/attend_last/pallas_call | solution.py:420
  207.7 0.0 collective-permute-done.11.beyond_ref
  207.7 0.0 collective-permute-done.10.behind_ref
  207.7 0.1 hand.1.kept_ref
  207.8 0.1 collective-permute-start.15
  207.9 2.8 %collective-permute-start.14 = (f32[8,512]{1,0:T(8,128)S(1)}, f32[8,512]{1,0:T(8,128)S(1)}, u32[]{:S(2)}, u32[]{:S(2)}) collective-permute-start(f32[8,512]{1,0:T(8,128)S(1)} %get-tuple-element.77), channel_id=1, source_target_pairs={{0,6},{1,7},{2,4},{3,5},{4,2},{5,3},{6,0},{7,1},{8,14},{9,15},{10,... | collective-permute-start | bytes 49160 | tf_op jit(solution)/shard_map/ppermute | solution.py:621
  210.7 0.3 collective-permute-start.13
  211.1 0.3 collective-permute-start.12
  211.4 0.0 collective-permute-done.15.handed_ref
  211.4 0.0 copy-done.1
  211.4 0.0 copy-done.3
  211.4 0.0 copy-start.2
  211.4 2.5 %carry.1.linear_ref = f32[512,768]{1,0:T(8,128)S(1)} custom-call(s32[1]{0:T(128)} %bitcast.mine_ref, bf16[512,768]{1,0:T(8,128)(2,1)} %query_hbm.1, f32[512,768]{1,0:T(8,128)S(1)} %get-tuple-element.78.local_ref, f32[512,128]{1,0:T(8,128)S(1)} %copy-done.1, f32[776,128]{1,0:T(8,128)S(1)} %hand.1.kept_ref, f32[776,128]{1,0:T(8,128)S(1)} %collective-permute-done.15.handed_ref, ...), custom_call_target="tpu_custom_call" | custom-call | flops 200000000 | bytes 200000 | tf_op jit(solution)/shard_map/carry/pallas_call | solution.py:486
  213.9 0.0 collective-permute-done.14
  213.9 0.9 collective-permute-done.13
  214.8 0.0 collective-permute-done.12
  214.8 1.6 collective-permute-start.16
  216.5 1.1 collective-permute-done.16.other_ref
  217.6 0.0 copy-done.2
  217.6 1.5 finish.1
  (2 shorter events, 0.0 us)
Async XLA Ops:
  1.0 1.9 collective-permute-start
  3.8 16.0 %collective-permute-start.2 = (bf16[1024,256]{1,0:T(8,128)(2,1)}, bf16[1024,256]{1,0:T(8,128)(2,1)S(1)}, u32[]{:S(2)}, u32[]{:S(2)}) collective-permute-start(bf16[1024,256]{1,0:T(8,128)(2,1)} %stack.3), channel_id=1, source_target_pairs={{0,32},{16,48},{32,64},{48,80},{64,96},{80,112},{8,72},{24,88},{40... | collective-permute-start | bytes 1572872 | tf_op jit(solution)/shard_map/ppermute | solution.py:514
  10.8 0.7 copy-start
  11.5 8.2 %collective-permute-start.1 = (f32[776,128]{1,0:T(8,128)}, f32[776,128]{1,0:T(8,128)S(1)}, u32[]{:S(2)}, u32[]{:S(2)}) collective-permute-start(f32[776,128]{1,0:T(8,128)} %get-tuple-element.51.own_ref), channel_id=1, source_target_pairs={{0,8},{8,0},{16,24},{24,16},{32,40},{40,32},{48,56},{56,48},{64,72... | collective-permute-start | bytes 1191944 | tf_op jit(solution)/shard_map/ppermute | solution.py:514
  11.9 11.2 %collective-permute-start.4 = (bf16[512,256]{1,0:T(8,128)(2,1)S(1)}, bf16[512,256]{1,0:T(8,128)(2,1)S(1)}, u32[]{:S(2)}, u32[]{:S(2)}) collective-permute-start(bf16[512,256]{1,0:T(8,128)(2,1)S(1)} %beside.1.own_ref.refs_0_), channel_id=1, source_target_pairs={{0,16},{8,24},{16,0},{24,8},{32,48},{40,56},{64,80},{72,88},{96,11... | collective-permute-start | bytes 786440 | tf_op jit(solution)/shard_map/ppermute | solution.py:514
  13.2 10.8 %collective-permute-start.3 = (bf16[512,256]{1,0:T(8,128)(2,1)S(1)}, bf16[512,256]{1,0:T(8,128)(2,1)S(1)}, u32[]{:S(2)}, u32[]{:S(2)}) collective-permute-start(bf16[512,256]{1,0:T(8,128)(2,1)S(1)} %beside.1.own_ref.refs_0_), channel_id=1, source_target_pairs={{0,96},{8,104},{16,112},{24,120},{1,97},{9,105},{17,113},{25,121},... | collective-permute-start | bytes 786440 | tf_op jit(solution)/shard_map/ppermute | solution.py:514
  24.1 6.0 %collective-permute-start.5 = (bf16[1536,256]{1,0:T(8,128)(2,1)S(1)}, bf16[1536,256]{1,0:T(8,128)(2,1)S(1)}, u32[]{:S(2)}, u32[]{:S(2)}) collective-permute-start(bf16[1536,256]{1,0:T(8,128)(2,1)S(1)} %stack.4), channel_id=1, source_target_pairs={{0,8},{8,0},{16,24},{24,16},{32,40},{40,32},{48,56},{56,48},{64,72... | collective-permute-start | bytes 2359304 | tf_op jit(solution)/shard_map/ppermute | solution.py:514
  25.5 19.8 %collective-permute-start.7 = (bf16[1424,256]{1,0:T(8,128)(2,1)S(1)}, bf16[1424,256]{1,0:T(8,128)(2,1)S(1)}, u32[]{:S(2)}, u32[]{:S(2)}) collective-permute-start(bf16[1424,256]{1,0:T(8,128)(2,1)S(1)} %get-tuple-element.63), channel_id=1, source_target_pairs={{0,16},{8,24},{16,0},{24,8},{32,48},{40,56},{48,32},{56,40},{64,80... | collective-permute-start | bytes 2187272 | tf_op jit(solution)/shard_map/ppermute | solution.py:514
  28.8 13.8 %collective-permute-start.6 = (bf16[512,256]{1,0:T(8,128)(2,1)S(1)}, bf16[512,256]{1,0:T(8,128)(2,1)S(1)}, u32[]{:S(2)}, u32[]{:S(2)}) collective-permute-start(bf16[512,256]{1,0:T(8,128)(2,1)S(1)} %collective-permute-done.4.refs_0_.refs_5_), channel_id=1, source_target_pairs={{0,96},{8,104},{16,112},{24,120},{1,97},{9,105},{17,113},{25,121},... | collective-permute-start | bytes 786440 | tf_op jit(solution)/shard_map/ppermute | solution.py:514
  45.3 2.5 %collective-permute-start.8 = (bf16[1424,256]{1,0:T(8,128)(2,1)S(1)}, bf16[1424,256]{1,0:T(8,128)(2,1)S(1)}, u32[]{:S(2)}, u32[]{:S(2)}) collective-permute-start(bf16[1424,256]{1,0:T(8,128)(2,1)S(1)} %collective-permute-done.7.level_ref.refs_3_), channel_id=1, source_target_pairs={{0,8},{8,0},{16,24},{24,16},{32,40},{40,32},{48,56},{56,48},{64,72... | collective-permute-start | bytes 2187272 | tf_op jit(solution)/shard_map/ppermute | solution.py:514
  46.1 4.7 %collective-permute-start.9 = (bf16[1024,256]{1,0:T(8,128)(2,1)S(1)}, bf16[1024,256]{1,0:T(8,128)(2,1)S(1)}, u32[]{:S(2)}, u32[]{:S(2)}) collective-permute-start(bf16[1024,256]{1,0:T(8,128)(2,1)S(1)} %stack.5), channel_id=1, source_target_pairs={{0,8},{8,0},{16,24},{24,16},{32,40},{40,32},{48,56},{56,48},{64,72... | collective-permute-start | bytes 1572872 | tf_op jit(solution)/shard_map/ppermute | solution.py:514
  48.0 163.4 %copy-start.1 = (f32[512,128]{1,0:T(8,128)S(1)}, f32[512,128]{1,0:T(8,128)}, u32[]{:S(2)}) copy-start(f32[512,128]{1,0:T(8,128)} %copy-done) | copy-start | bytes 786436
  48.0 163.4 %copy-start.3 = (f32[768]{0:T(1024)S(1)}, f32[768]{0:T(1024)}, u32[]{:S(2)}) copy-start(f32[768]{0:T(1024)} %gain_ref.2) | copy-start | bytes 9220
  48.0 159.7 %collective-permute-start.11 = (f32[776,128]{1,0:T(8,128)S(1)}, f32[776,128]{1,0:T(8,128)S(1)}, u32[]{:S(2)}, u32[]{:S(2)}) collective-permute-start(f32[776,128]{1,0:T(8,128)S(1)} %get-tuple-element.69), channel_id=1, source_target_pairs={{8,72},{24,88},{40,104},{56,120},{9,73},{25,89},{41,105},{57,121},... | collective-permute-start | bytes 1191944 | tf_op jit(solution)/shard_map/ppermute | solution.py:514
  49.5 158.2 %collective-permute-start.10 = (f32[776,128]{1,0:T(8,128)S(1)}, f32[776,128]{1,0:T(8,128)S(1)}, u32[]{:S(2)}, u32[]{:S(2)}) collective-permute-start(f32[776,128]{1,0:T(8,128)S(1)} %get-tuple-element.69), channel_id=1, source_target_pairs={{0,32},{16,48},{32,64},{48,80},{64,96},{80,112},{8,104},{24,120},{... | collective-permute-start | bytes 1191944 | tf_op jit(solution)/shard_map/ppermute | solution.py:514
  207.8 3.6 %collective-permute-start.15 = (f32[776,128]{1,0:T(8,128)S(1)}, f32[776,128]{1,0:T(8,128)S(1)}, u32[]{:S(2)}, u32[]{:S(2)}) collective-permute-start(f32[776,128]{1,0:T(8,128)S(1)} %hand.1.kept_ref), channel_id=1, source_target_pairs={{0,8},{8,0},{16,24},{24,16},{32,40},{40,32},{48,56},{56,48},{64,72... | collective-permute-start | bytes 1191944 | tf_op jit(solution)/shard_map/ppermute | solution.py:514
  207.9 6.0 %collective-permute-start.14 = (f32[8,512]{1,0:T(8,128)S(1)}, f32[8,512]{1,0:T(8,128)S(1)}, u32[]{:S(2)}, u32[]{:S(2)}) collective-permute-start(f32[8,512]{1,0:T(8,128)S(1)} %get-tuple-element.77), channel_id=1, source_target_pairs={{0,6},{1,7},{2,4},{3,5},{4,2},{5,3},{6,0},{7,1},{8,14},{9,15},{10,... | collective-permute-start | bytes 49160 | tf_op jit(solution)/shard_map/ppermute | solution.py:621
  210.7 4.1 %collective-permute-start.13 = (f32[8,512]{1,0:T(8,128)S(1)}, f32[8,512]{1,0:T(8,128)S(1)}, u32[]{:S(2)}, u32[]{:S(2)}) collective-permute-start(f32[8,512]{1,0:T(8,128)S(1)} %get-tuple-element.77), channel_id=1, source_target_pairs={{0,4},{1,5},{2,6},{3,7},{4,0},{5,1},{6,2},{7,3},{8,12},{9,13},{10,... | collective-permute-start | bytes 49160 | tf_op jit(solution)/shard_map/ppermute | solution.py:621
  211.1 3.7 %collective-permute-start.12 = (f32[8,512]{1,0:T(8,128)S(1)}, f32[8,512]{1,0:T(8,128)S(1)}, u32[]{:S(2)}, u32[]{:S(2)}) collective-permute-start(f32[8,512]{1,0:T(8,128)S(1)} %get-tuple-element.77), channel_id=1, source_target_pairs={{0,2},{1,3},{2,0},{3,1},{4,6},{5,7},{6,4},{7,5},{8,10},{9,11},{10,... | collective-permute-start | bytes 49160 | tf_op jit(solution)/shard_map/ppermute | solution.py:621
  211.4 6.2 %copy-start.2 = (f32[768]{0:T(1024)S(1)}, f32[768]{0:T(1024)}, u32[]{:S(2)}) copy-start(f32[768]{0:T(1024)} %gain_ref.3) | copy-start | bytes 9220
  214.8 2.8 %collective-permute-start.16 = (f32[8,512]{1,0:T(8,128)S(1)}, f32[8,512]{1,0:T(8,128)S(1)}, u32[]{:S(2)}, u32[]{:S(2)}) collective-permute-start(f32[8,512]{1,0:T(8,128)S(1)} %add_add_fusion.square_ref), channel_id=1, source_target_pairs={{0,1},{1,0},{2,3},{3,2},{4,5},{5,4},{6,7},{7,6},{8,9},{9,8},{10,11... | collective-permute-start | bytes 49160 | tf_op jit(solution)/shard_map/ppermute | solution.py:621

commit v6 on v5

--- a/solution.py
+++ b/solution.py
@@ -574,11 +574,10 @@
 
     first_pieces = [(near, 0, ROWS)]
     near_query, *carry = attend(place, att_query, own, None, first_pieces, near_numbers)
+    carry, message, across, wrapped = tied(carry, message, across, wrapped)
     first = move(message, sibling)
-    carry, first = tied(carry, first)
     of_chip, leveled = join_cores(place, message, first, ring)
     level = move(leveled, sideways)
-    of_chip, wrapped, across = tied(of_chip, wrapped, across)
     wrapped_side = move(across, wrapping)
     bundle = stack(ring, wrapped)
     bundle_near = move(bundle, sibling)

time: 222 us -> 217 us (0.977)
  starting transfers between devices: 19.6 us -> 15.3 us
  Pallas kernels: 188 us -> 185 us
  waiting for transfers between devices: 10.8 us -> 13.1 us
    ppermute x13, starting transfers between devices: 14.5 us -> 11.7 us  [move(): return lax.ppermute(value, 'ctx', pairs)]
  transfers between devices with their start and end apart: 17 -> 17, of which waited for: 7 -> 6; matrix products, arithmetic and copies ran while one was open for 0% -> 0% of each run, Pallas kernels for 84% -> 85%
where the time goes in v6:
time: 217 us; the launch traced here: 214 us
  Pallas kernels  185 us (85%)
  starting transfers between devices  15.3 us (7%)
  waiting for transfers between devices  13.1 us (6%)
    pallas_call x3, Pallas kernels, attend(): pl.pallas_call(functools.partial(attend_kernel, first, last, numbers_of,...  175 us
    ppermute x13, starting transfers between devices, move(): return lax.ppermute(value, 'ctx', pairs)  11.7 us
    ppermute x13, waiting for transfers between devices, move(): return lax.ppermute(value, 'ctx', pairs)  9.62 us
    pallas_call x1, Pallas kernels, recur(): pl.pallas_call(recur_kernel, out_shape=(jax.ShapeDtypeStruct((ROWS, HEADS...  5.04 us
  transfers between devices with their start and end apart: 17, of which 6 were waited for; matrix products, arithmetic and copies ran while one was open for 0% of the time, Pallas kernels for 85%

profile of v6, /device:TPU:101, one launch (start us, length us, event | category | flops | bytes accessed | tf_op | source)
XLA Modules:
  0.0 213.9 jit_solution(154390636233460927)
XLA Ops:
  0.0 1.0 beside.1.own_ref.refs_0_
  1.0 0.8 collective-permute-start
  1.8 1.3 collective-permute-start.2
  3.1 1.3 collective-permute-start.1
  4.4 0.0 collective-permute-done.refs_0_.refs_1_.refs_9_
  4.4 1.3 collective-permute-start.3
  5.7 5.0 %recur.1 = (f32[512,768]{1,0:T(8,128)S(1)}, f32[512,128]{1,0:T(8,128)S(1)}, f32[776,128]{1,0:T(8,128)S(1)}) custom-call(bf16[512,768]{1,0:T(8,128)(2,1)} %query_hbm.1, bf16[512,768]{1,0:T(8,128)(2,1)} %k_hbm.1, bf16[512,768]{1,0:T(8,128)(2,1)} %v_hbm.1, f32[6,512]{1,0:T(8,128)} %bitcast.2), custom_call_target="tpu_custom_call" | custom-call | flops 200000000 | bytes 200000 | tf_op jit(solution)/shard_map/recur/pallas_call | solution.py:93
  10.8 5.3 %attend_first.1 = (bf16[512,768]{1,0:T(8,128)(2,1)S(1)}, f32[512,768]{1,0:T(8,128)S(1)}, f32[512,128]{1,0:T(8,128)S(1)}, bf16[32,128]{1,0:T(8,128)(2,1)S(1)}) custom-call(s32[1]{0:T(128)} %bitcast.mine_ref, bf16[512,768]{1,0:T(8,128)(2,1)} %query_ref.1, bf16[512,256]{1,0:T(8,128)(2,1)S(1)} %beside.1.own_ref.refs_0_, ...), custom_call_target="tpu_custom_call" | custom-call | flops 200000000 | bytes 200000 | tf_op jit(solution)/shard_map/attend_first/pallas_call | solution.py:420
  16.0 2.4 %collective-permute-done.2.refs_1_.refs_5_.refs_12_ = bf16[512,256]{1,0:T(8,128)(2,1)S(1)} collective-permute-done((bf16[512,256]{1,0:T(8,128)(2,1)S(1)}, bf16[512,256]{1,0:T(8,128)(2,1)S(1)}, u32[]{:S(2)}, u32[]{:S(2)}) %collective-permute-start.2) | collective-permute-done | bytes 262176 | tf_op jit(solution)/shard_map/ppermute | solution.py:514
  18.4 0.0 collective-permute-done.1.refs_0_.refs_5_
  18.4 0.8 collective-permute-start.6
  19.2 0.0 collective-permute-done.3.refs_0_.refs_3_.blocks_ref.refs_10_
  19.2 0.1 stack.4
  19.3 0.1 collective-permute-start.4
  19.4 1.2 collective-permute-done.6.other_ref.core_ref
  20.6 0.1 join_cores.1
  20.7 1.0 collective-permute-start.7
  21.7 1.3 collective-permute-start.5
  23.0 0.0 collective-permute-done.4.refs_4_.refs_6_.refs_11_.refs_13_
  23.0 12.5 %attend_middle.1 = (f32[512,768]{1,0:T(8,128)S(1)}, f32[512,128]{1,0:T(8,128)S(1)}, bf16[32,128]{1,0:T(8,128)(2,1)S(1)}) custom-call(s32[1]{0:T(128)} %bitcast.mine_ref, bf16[512,768]{1,0:T(8,128)(2,1)S(1)} %get-tuple-element.45.query_ref, bf16[512,256]{1,0:T(8,128)(2,1)S(1)} %beside.1.own_ref.refs_0_, f32[512,768]{1,0:T(8,128)S(1)} %get-tuple-element.51.refs_0_, ...), custom_call_target="tpu_custom_call" | custom-call | flops 200000000 | bytes 200000 | tf_op jit(solution)/shard_map/attend_middle/pallas_call | solution.py:420
  35.5 0.0 collective-permute-done.5.refs_1_.refs_7_
  35.5 4.3 %collective-permute-done.7.level_ref.refs_3_ = bf16[1424,256]{1,0:T(8,128)(2,1)S(1)} collective-permute-done((bf16[1424,256]{1,0:T(8,128)(2,1)S(1)}, bf16[1424,256]{1,0:T(8,128)(2,1)S(1)}, u32[]{:S(2)}, u32[]{:S(2)}) %collective-permute-start.7) | collective-permute-done | bytes 729120 | tf_op jit(solution)/shard_map/ppermute | solution.py:514
  39.8 1.2 collective-permute-start.8
  41.1 0.1 collective-permute-start.9
  41.2 1.7 collective-permute-done.8.level_near_ref.refs_4_
  42.9 0.2 join_sides.1
  43.0 0.0 copy-start.1
  43.0 1.3 collective-permute-start.11
  44.3 1.3 collective-permute-start.10
  45.6 0.0 collective-permute-done.9.refs_6_.refs_8_
  45.6 156.9 %attend_last.1 = (bf16[512,768]{1,0:T(8,128)(2,1)S(1)}, f32[8,512]{1,0:T(8,128)S(1)}) custom-call(s32[1]{0:T(128)} %bitcast.mine_ref, bf16[512,768]{1,0:T(8,128)(2,1)S(1)} %get-tuple-element.45.query_ref, bf16[512,256]{1,0:T(8,128)(2,1)S(1)} %beside.1.own_ref.refs_0_, f32[512,768]{1,0:T(8,128)S(1)} %get-tuple-element.68.refs_0_, ...), custom_call_target="tpu_custom_call" | custom-call | flops 200000000 | bytes 200000 | tf_op jit(solution)/shard_map/attend_last/pallas_call | solution.py:420
  202.6 0.0 collective-permute-done.11.beyond_ref
  202.6 0.0 collective-permute-done.10.behind_ref
  202.6 0.1 hand.1.kept_ref
  202.7 0.1 collective-permute-start.15
  202.8 2.8 %collective-permute-start.14 = (f32[8,512]{1,0:T(8,128)S(1)}, f32[8,512]{1,0:T(8,128)S(1)}, u32[]{:S(2)}, u32[]{:S(2)}) collective-permute-start(f32[8,512]{1,0:T(8,128)S(1)} %get-tuple-element.75), channel_id=1, source_target_pairs={{0,6},{1,7},{2,4},{3,5},{4,2},{5,3},{6,0},{7,1},{8,14},{9,15},{10,... | collective-permute-start | bytes 49160 | tf_op jit(solution)/shard_map/ppermute | solution.py:620
  205.6 0.3 collective-permute-start.13
  205.9 0.4 collective-permute-start.12
  206.3 0.0 collective-permute-done.15.handed_ref
  206.3 0.0 copy-done.1
  206.3 0.0 copy-start
  206.3 2.5 %carry.1.linear_ref = f32[512,768]{1,0:T(8,128)S(1)} custom-call(s32[1]{0:T(128)} %bitcast.mine_ref, bf16[512,768]{1,0:T(8,128)(2,1)} %query_hbm.1, f32[512,768]{1,0:T(8,128)S(1)} %get-tuple-element.76.local_ref, f32[512,128]{1,0:T(8,128)S(1)} %get-tuple-element.77.grow_ref, f32[776,128]{1,0:T(8,128)S(1)} %hand.1.kept_ref, ...), custom_call_target="tpu_custom_call" | custom-call | flops 200000000 | bytes 200000 | tf_op jit(solution)/shard_map/carry/pallas_call | solution.py:486
  208.8 0.0 collective-permute-done.14
  208.8 0.9 collective-permute-done.13
  209.7 0.0 collective-permute-done.12
  209.7 0.1 collective-permute-start.16
  209.8 2.6 %collective-permute-done.16.other_ref = f32[8,512]{1,0:T(8,128)S(1)} collective-permute-done((f32[8,512]{1,0:T(8,128)S(1)}, f32[8,512]{1,0:T(8,128)S(1)}, u32[]{:S(2)}, u32[]{:S(2)}) %collective-permute-start.16) | collective-permute-done | bytes 16416 | tf_op jit(solution)/shard_map/ppermute | solution.py:620
  212.4 0.0 copy-done
  212.4 1.5 finish.1
  (3 shorter events, 0.1 us)
Async XLA Ops:
  1.0 3.3 %collective-permute-start = (bf16[512,256]{1,0:T(8,128)(2,1)S(1)}, bf16[512,256]{1,0:T(8,128)(2,1)S(1)}, u32[]{:S(2)}, u32[]{:S(2)}) collective-permute-start(bf16[512,256]{1,0:T(8,128)(2,1)S(1)} %beside.1.own_ref.refs_0_), channel_id=1, source_target_pairs={{0,8},{8,0},{16,24},{24,16},{32,40},{40,32},{48,56},{56,48},{64,72... | collective-permute-start | bytes 786440 | tf_op jit(solution)/shard_map/ppermute | solution.py:514
  1.8 16.6 %collective-permute-start.2 = (bf16[512,256]{1,0:T(8,128)(2,1)S(1)}, bf16[512,256]{1,0:T(8,128)(2,1)S(1)}, u32[]{:S(2)}, u32[]{:S(2)}) collective-permute-start(bf16[512,256]{1,0:T(8,128)(2,1)S(1)} %beside.1.own_ref.refs_0_), channel_id=1, source_target_pairs={{0,96},{8,104},{16,112},{24,120},{1,97},{9,105},{17,113},{25,121},... | collective-permute-start | bytes 786440 | tf_op jit(solution)/shard_map/ppermute | solution.py:514
  3.1 15.3 %collective-permute-start.1 = (bf16[512,256]{1,0:T(8,128)(2,1)S(1)}, bf16[512,256]{1,0:T(8,128)(2,1)S(1)}, u32[]{:S(2)}, u32[]{:S(2)}) collective-permute-start(bf16[512,256]{1,0:T(8,128)(2,1)S(1)} %beside.1.own_ref.refs_0_), channel_id=1, source_target_pairs={{0,16},{8,24},{16,0},{24,8},{32,48},{40,56},{64,80},{72,88},{96,11... | collective-permute-start | bytes 786440 | tf_op jit(solution)/shard_map/ppermute | solution.py:514
  4.4 14.8 %collective-permute-start.3 = (bf16[1024,256]{1,0:T(8,128)(2,1)S(1)}, bf16[1024,256]{1,0:T(8,128)(2,1)S(1)}, u32[]{:S(2)}, u32[]{:S(2)}) collective-permute-start(bf16[1024,256]{1,0:T(8,128)(2,1)S(1)} %stack.3), channel_id=1, source_target_pairs={{0,32},{16,48},{32,64},{48,80},{64,96},{80,112},{8,72},{24,88},{40... | collective-permute-start | bytes 1572872 | tf_op jit(solution)/shard_map/ppermute | solution.py:514
  18.4 2.2 %collective-permute-start.6 = (f32[776,128]{1,0:T(8,128)S(1)}, f32[776,128]{1,0:T(8,128)S(1)}, u32[]{:S(2)}, u32[]{:S(2)}) collective-permute-start(f32[776,128]{1,0:T(8,128)S(1)} %get-tuple-element.60.own_ref), channel_id=1, source_target_pairs={{0,8},{8,0},{16,24},{24,16},{32,40},{40,32},{48,56},{56,48},{64,72... | collective-permute-start | bytes 1191944 | tf_op jit(solution)/shard_map/ppermute | solution.py:514
  19.3 3.7 %collective-permute-start.4 = (bf16[1536,256]{1,0:T(8,128)(2,1)S(1)}, bf16[1536,256]{1,0:T(8,128)(2,1)S(1)}, u32[]{:S(2)}, u32[]{:S(2)}) collective-permute-start(bf16[1536,256]{1,0:T(8,128)(2,1)S(1)} %stack.4), channel_id=1, source_target_pairs={{0,8},{8,0},{16,24},{24,16},{32,40},{40,32},{48,56},{56,48},{64,72... | collective-permute-start | bytes 2359304 | tf_op jit(solution)/shard_map/ppermute | solution.py:514
  20.7 19.1 %collective-permute-start.7 = (bf16[1424,256]{1,0:T(8,128)(2,1)S(1)}, bf16[1424,256]{1,0:T(8,128)(2,1)S(1)}, u32[]{:S(2)}, u32[]{:S(2)}) collective-permute-start(bf16[1424,256]{1,0:T(8,128)(2,1)S(1)} %get-tuple-element.61), channel_id=1, source_target_pairs={{0,16},{8,24},{16,0},{24,8},{32,48},{40,56},{48,32},{56,40},{64,80... | collective-permute-start | bytes 2187272 | tf_op jit(solution)/shard_map/ppermute | solution.py:514
  21.7 13.8 %collective-permute-start.5 = (bf16[512,256]{1,0:T(8,128)(2,1)S(1)}, bf16[512,256]{1,0:T(8,128)(2,1)S(1)}, u32[]{:S(2)}, u32[]{:S(2)}) collective-permute-start(bf16[512,256]{1,0:T(8,128)(2,1)S(1)} %collective-permute-done.1.refs_0_.refs_5_), channel_id=1, source_target_pairs={{0,96},{8,104},{16,112},{24,120},{1,97},{9,105},{17,113},{25,121},... | collective-permute-start | bytes 786440 | tf_op jit(solution)/shard_map/ppermute | solution.py:514
  39.8 3.0 %collective-permute-start.8 = (bf16[1424,256]{1,0:T(8,128)(2,1)S(1)}, bf16[1424,256]{1,0:T(8,128)(2,1)S(1)}, u32[]{:S(2)}, u32[]{:S(2)}) collective-permute-start(bf16[1424,256]{1,0:T(8,128)(2,1)S(1)} %collective-permute-done.7.level_ref.refs_3_), channel_id=1, source_target_pairs={{0,8},{8,0},{16,24},{24,16},{32,40},{40,32},{48,56},{56,48},{64,72... | collective-permute-start | bytes 2187272 | tf_op jit(solution)/shard_map/ppermute | solution.py:514
  41.1 4.6 %collective-permute-start.9 = (bf16[1024,256]{1,0:T(8,128)(2,1)S(1)}, bf16[1024,256]{1,0:T(8,128)(2,1)S(1)}, u32[]{:S(2)}, u32[]{:S(2)}) collective-permute-start(bf16[1024,256]{1,0:T(8,128)(2,1)S(1)} %stack.5), channel_id=1, source_target_pairs={{0,8},{8,0},{16,24},{24,16},{32,40},{40,32},{48,56},{56,48},{64,72... | collective-permute-start | bytes 1572872 | tf_op jit(solution)/shard_map/ppermute | solution.py:514
  43.0 163.2 %copy-start.1 = (f32[768]{0:T(1024)S(1)}, f32[768]{0:T(1024)}, u32[]{:S(2)}) copy-start(f32[768]{0:T(1024)} %gain_ref.2) | copy-start | bytes 9220
  43.0 159.6 %collective-permute-start.11 = (f32[776,128]{1,0:T(8,128)S(1)}, f32[776,128]{1,0:T(8,128)S(1)}, u32[]{:S(2)}, u32[]{:S(2)}) collective-permute-start(f32[776,128]{1,0:T(8,128)S(1)} %get-tuple-element.67), channel_id=1, source_target_pairs={{8,72},{24,88},{40,104},{56,120},{9,73},{25,89},{41,105},{57,121},... | collective-permute-start | bytes 1191944 | tf_op jit(solution)/shard_map/ppermute | solution.py:514
  44.3 158.3 %collective-permute-start.10 = (f32[776,128]{1,0:T(8,128)S(1)}, f32[776,128]{1,0:T(8,128)S(1)}, u32[]{:S(2)}, u32[]{:S(2)}) collective-permute-start(f32[776,128]{1,0:T(8,128)S(1)} %get-tuple-element.67), channel_id=1, source_target_pairs={{0,32},{16,48},{32,64},{48,80},{64,96},{80,112},{8,104},{24,120},{... | collective-permute-start | bytes 1191944 | tf_op jit(solution)/shard_map/ppermute | solution.py:514
  202.7 3.6 %collective-permute-start.15 = (f32[776,128]{1,0:T(8,128)S(1)}, f32[776,128]{1,0:T(8,128)S(1)}, u32[]{:S(2)}, u32[]{:S(2)}) collective-permute-start(f32[776,128]{1,0:T(8,128)S(1)} %hand.1.kept_ref), channel_id=1, source_target_pairs={{0,8},{8,0},{16,24},{24,16},{32,40},{40,32},{48,56},{56,48},{64,72... | collective-permute-start | bytes 1191944 | tf_op jit(solution)/shard_map/ppermute | solution.py:514
  202.8 6.0 %collective-permute-start.14 = (f32[8,512]{1,0:T(8,128)S(1)}, f32[8,512]{1,0:T(8,128)S(1)}, u32[]{:S(2)}, u32[]{:S(2)}) collective-permute-start(f32[8,512]{1,0:T(8,128)S(1)} %get-tuple-element.75), channel_id=1, source_target_pairs={{0,6},{1,7},{2,4},{3,5},{4,2},{5,3},{6,0},{7,1},{8,14},{9,15},{10,... | collective-permute-start | bytes 49160 | tf_op jit(solution)/shard_map/ppermute | solution.py:620
  205.6 4.1 %collective-permute-start.13 = (f32[8,512]{1,0:T(8,128)S(1)}, f32[8,512]{1,0:T(8,128)S(1)}, u32[]{:S(2)}, u32[]{:S(2)}) collective-permute-start(f32[8,512]{1,0:T(8,128)S(1)} %get-tuple-element.75), channel_id=1, source_target_pairs={{0,4},{1,5},{2,6},{3,7},{4,0},{5,1},{6,2},{7,3},{8,12},{9,13},{10,... | collective-permute-start | bytes 49160 | tf_op jit(solution)/shard_map/ppermute | solution.py:620
  205.9 3.8 %collective-permute-start.12 = (f32[8,512]{1,0:T(8,128)S(1)}, f32[8,512]{1,0:T(8,128)S(1)}, u32[]{:S(2)}, u32[]{:S(2)}) collective-permute-start(f32[8,512]{1,0:T(8,128)S(1)} %get-tuple-element.75), channel_id=1, source_target_pairs={{0,2},{1,3},{2,0},{3,1},{4,6},{5,7},{6,4},{7,5},{8,10},{9,11},{10,... | collective-permute-start | bytes 49160 | tf_op jit(solution)/shard_map/ppermute | solution.py:620
  206.3 6.1 %copy-start = (f32[768]{0:T(1024)S(1)}, f32[768]{0:T(1024)}, u32[]{:S(2)}) copy-start(f32[768]{0:T(1024)} %gain_ref.3) | copy-start | bytes 9220
  209.7 2.7 %collective-permute-start.16 = (f32[8,512]{1,0:T(8,128)S(1)}, f32[8,512]{1,0:T(8,128)S(1)}, u32[]{:S(2)}, u32[]{:S(2)}) collective-permute-start(f32[8,512]{1,0:T(8,128)S(1)} %add_add_fusion.square_ref), channel_id=1, source_target_pairs={{0,1},{1,0},{2,3},{3,2},{4,5},{5,4},{6,7},{7,6},{8,9},{9,8},{10,11... | collective-permute-start | bytes 49160 | tf_op jit(solution)/shard_map/ppermute | solution.py:620

commit v7 on v6

--- a/solution.py
+++ b/solution.py
@@ -18,8 +18,6 @@
 SCORE_SCALE = LOG2E / math.sqrt(HD)
 SAFE_EXPONENT = 100.0
 STATE_ROWS = HEADS * HD + 8
-HALF = HEADS // 2
-BLOCKS = 2 * ROWS
 NEVER = 1 << 20
 
 VMEM = pl.BlockSpec(memory_space=pltpu.VMEM)
@@ -183,12 +181,14 @@
     even = mine_ref[0] % 2 == 0
     joined = follow_in_order(even, state_of(own_ref), state_of(other_ref))
     put_state(out_ref, joined)
-    message_ref[:BLOCKS, :] = blocks_ref[...]
-    for h in range(HALF):
-        at = BLOCKS + h * HD
-        message_ref[at : at + HD, :] = split(jnp.where(even, joined[0][h], joined[0][HALF + h]))
-    logs = jnp.concatenate([joined[1], jnp.zeros((8, HD), f32)], 0)
-    message_ref[BLOCKS + HALF * HD :, :] = split(logs)
+    message_ref[...] = blocks_ref[...]
+
+    @pl.when(even)
+    def _():
+        for h in range(HEADS):
+            message_ref[head(h), :] = split(joined[0][h])
+        logs = jnp.concatenate([joined[1], jnp.zeros((8, HD), f32)], 0)
+        message_ref[HEADS * HD : HEADS * HD + 16, :] = split(logs)
 
 
 def join_cores(mine, own, other, blocks):
@@ -196,7 +196,7 @@
         join_cores_kernel,
         out_shape=(
             jax.ShapeDtypeStruct((STATE_ROWS, HD), f32),
-            jax.ShapeDtypeStruct((BLOCKS + HALF * HD + 16, 2 * HD), bf16),
+            jax.ShapeDtypeStruct((2 * ROWS, 2 * HD), bf16),
         ),
         in_specs=[SMEM] + [VMEM] * 3,
         out_specs=(VMEM,) * 2,
@@ -209,14 +209,12 @@
 def join_sides_kernel(mine_ref, own_ref, level_ref, level_near_ref, out_ref, other_ref):
     mine = mine_ref[0]
     even = mine % 2 == 0
-    states = [None] * HEADS
-    for h in range(HALF):
-        at = slice(BLOCKS + h * HD, BLOCKS + (h + 1) * HD)
-        here, there = merge(level_ref[at, :]), merge(level_near_ref[at, :])
-        states[h] = jnp.where(even, here, there)
-        states[HALF + h] = jnp.where(even, there, here)
-    logs = merge(level_ref[BLOCKS + HALF * HD :, :])[:8, :]
-    other = states, logs
+
+    def brought(ref):
+        logs = merge(ref[HEADS * HD : HEADS * HD + 16, :])[:8, :]
+        return [merge(ref[head(h), :]) for h in range(HEADS)], logs
+
+    other = select(even, brought(level_ref), brought(level_near_ref))
     put_state(other_ref, other)
     put_state(out_ref, follow_in_order((mine // 2) % 2 == 0, state_of(own_ref), other))
 
@@ -534,7 +532,7 @@
         for array in (att_query, lh_query, lh_key, lh_value, att_key, att_value)
     ]
     own = beside(att_key, att_value)
-    across = move(own, [(i, j) for i, j in sideways if i < 4 or i % 4 < 2])
+    across = move(own, [(i, j) for i, j in sideways if i < 12 or i % 4 < 2])
     wrapped = move(own, wrapping)
     near = move(own, sibling)
     chip = stack(own, near)
@@ -570,7 +568,10 @@
         return ring_numbers(mine) + wrapped_numbers(mine)
 
     def last_numbers(mine):
-        return ring_numbers(mine) + across_numbers(mine) + wrapped_numbers(mine)
+        plane, _, core, even = parts(mine)
+        beyond, behind = where(even - 8, plane >= 2), where(even - 4, plane >= 1)
+        level_numbers = [where(beyond, core == 1), where(beyond, core == 0)]
+        return level_numbers + across_numbers(mine) + wrapped_numbers(mine) + [behind] * 2
 
     first_pieces = [(near, 0, ROWS)]
     near_query, *carry = attend(place, att_query, own, None, first_pieces, near_numbers)
@@ -579,6 +580,7 @@
     of_chip, leveled = join_cores(place, message, first, ring)
     level = move(leveled, sideways)
     wrapped_side = move(across, wrapping)
+    behind_side = move(across, [(i, i + 4) for i in range(12)])
     bundle = stack(ring, wrapped)
     bundle_near = move(bundle, sibling)
     middle_pieces = [
@@ -589,9 +591,9 @@
     ]
     carry = attend(place, near_query, own, carry, middle_pieces, middle_numbers)
 
-    carry, across, wrapped_side, level = tied(carry, across, wrapped_side, level)
+    carry, across, wrapped_side, behind_side, level = tied(carry, across, wrapped_side, behind_side, level)
     level_near = move(level, sibling)
-    rest = stack(across, wrapped_side)
+    rest = stack(across, wrapped_side, behind_side)
     rest_near = move(rest, sibling)
     of_plane, other_chip = join_sides(place, of_chip, level, level_near)
     state_behind = move(of_plane, last_plane)
@@ -603,6 +605,8 @@
         (rest_near, 0, ROWS),
         (wrapped_side, 0, ROWS),
         (rest_near, ROWS, ROWS),
+        (behind_side, 0, ROWS),
+        (rest_near, 2 * ROWS, ROWS),
     ]
     carry, of_plane = tied(carry, of_plane)
     attention, squares = attend(

time: 217 us -> 216 us (level)
  waiting for transfers between devices: 13.1 us -> 8.37 us
  starting transfers between devices: 15.3 us -> 18.3 us
    ppermute x4, starting transfers between devices: 3.56 us -> 6.54 us  [over(): return lax.ppermute(value, 'tp', [(i, i ^ bit) for i in range(8)])]
    ppermute x13 -> x14, waiting for transfers between devices: 9.62 us -> 6.76 us  [move(): return lax.ppermute(value, 'ctx', pairs)]
    ppermute x13 -> x14, starting transfers between devices: 11.7 us -> 11.8 us  [move(): return lax.ppermute(value, 'ctx', pairs)]
  transfers between devices with their start and end apart: 17 -> 18, of which waited for: 6 -> 6; matrix products, arithmetic and copies ran while one was open for 0% -> 0% of each run, Pallas kernels for 85% -> 86%
where the time goes in v7:
time: 216 us; the launch traced here: 212 us
  Pallas kernels  185 us (86%)
  starting transfers between devices  18.3 us (8%)
  waiting for transfers between devices  8.37 us (4%)
    pallas_call x3, Pallas kernels, attend(): pl.pallas_call(functools.partial(attend_kernel, first, last, numbers_of,...  175 us
    ppermute x14, starting transfers between devices, move(): return lax.ppermute(value, 'ctx', pairs)  11.8 us
    ppermute x14, waiting for transfers between devices, move(): return lax.ppermute(value, 'ctx', pairs)  6.76 us
    ppermute x4, starting transfers between devices, over(): return lax.ppermute(value, 'tp', [(i, i ^ bit) for i in range(8)])  6.54 us
    pallas_call x1, Pallas kernels, recur(): pl.pallas_call(recur_kernel, out_shape=(jax.ShapeDtypeStruct((ROWS, HEADS...  5.04 us
  transfers between devices with their start and end apart: 18, of which 6 were waited for; matrix products, arithmetic and copies ran while one was open for 0% of the time, Pallas kernels for 86%

profile of v7, /device:TPU:101, one launch (start us, length us, event | category | flops | bytes accessed | tf_op | source)
XLA Modules:
  0.0 212.2 jit_solution(16331871249982506114)
XLA Ops:
  0.0 1.0 beside.1.own_ref.refs_0_
  1.0 0.8 collective-permute-start
  1.8 1.2 collective-permute-done.refs_0_.refs_1_.refs_11_
  3.0 1.3 collective-permute-start.3
  4.3 1.3 collective-permute-start.1
  5.6 1.3 collective-permute-start.2
  6.9 5.0 %recur.1 = (f32[512,768]{1,0:T(8,128)S(1)}, f32[512,128]{1,0:T(8,128)S(1)}, f32[776,128]{1,0:T(8,128)S(1)}) custom-call(bf16[512,768]{1,0:T(8,128)(2,1)} %query_hbm.1, bf16[512,768]{1,0:T(8,128)(2,1)} %k_hbm.1, bf16[512,768]{1,0:T(8,128)(2,1)} %v_hbm.1, f32[6,512]{1,0:T(8,128)} %bitcast.2), custom_call_target="tpu_custom_call" | custom-call | flops 200000000 | bytes 200000 | tf_op jit(solution)/shard_map/recur/pallas_call | solution.py:91
  11.9 5.3 %attend_first.1 = (bf16[512,768]{1,0:T(8,128)(2,1)S(1)}, f32[512,768]{1,0:T(8,128)S(1)}, f32[512,128]{1,0:T(8,128)S(1)}, bf16[32,128]{1,0:T(8,128)(2,1)S(1)}) custom-call(s32[1]{0:T(128)} %bitcast.mine_ref, bf16[512,768]{1,0:T(8,128)(2,1)} %query_ref.1, bf16[512,256]{1,0:T(8,128)(2,1)S(1)} %beside.1.own_ref.refs_0_, ...), custom_call_target="tpu_custom_call" | custom-call | flops 200000000 | bytes 200000 | tf_op jit(solution)/shard_map/attend_first/pallas_call | solution.py:418
  17.2 0.0 collective-permute-done.1.refs_0_.refs_5_
  17.2 3.1 %collective-permute-done.2.refs_1_.refs_5_.refs_14_ = bf16[512,256]{1,0:T(8,128)(2,1)S(1)} collective-permute-done((bf16[512,256]{1,0:T(8,128)(2,1)S(1)}, bf16[512,256]{1,0:T(8,128)(2,1)S(1)}, u32[]{:S(2)}, u32[]{:S(2)}) %collective-permute-start.2) | collective-permute-done | bytes 262176 | tf_op jit(solution)/shard_map/ppermute | solution.py:512
  20.3 0.4 collective-permute-start.7
  20.7 0.0 collective-permute-done.3.refs_0_.refs_3_.blocks_ref.refs_12_
  20.7 0.1 stack.4
  20.8 0.2 collective-permute-start.4
  21.0 1.1 collective-permute-done.7.other_ref.core_ref
  22.1 0.1 join_cores.1
  22.2 0.6 collective-permute-start.8
  22.8 1.3 collective-permute-start.5
  24.1 1.3 collective-permute-start.6
  25.4 0.0 collective-permute-done.4.refs_4_.refs_6_.refs_13_.refs_15_
  25.4 12.5 %attend_middle.1 = (f32[512,768]{1,0:T(8,128)S(1)}, f32[512,128]{1,0:T(8,128)S(1)}, bf16[32,128]{1,0:T(8,128)(2,1)S(1)}) custom-call(s32[1]{0:T(128)} %bitcast.mine_ref, bf16[512,768]{1,0:T(8,128)(2,1)S(1)} %get-tuple-element.46.query_ref, bf16[512,256]{1,0:T(8,128)(2,1)S(1)} %beside.1.own_ref.refs_0_, f32[512,768]{1,0:T(8,128)S(1)} %get-tuple-element.52.refs_0_, ...), custom_call_target="tpu_custom_call" | custom-call | flops 200000000 | bytes 200000 | tf_op jit(solution)/shard_map/attend_middle/pallas_call | solution.py:418
  37.9 0.0 collective-permute-done.5.refs_1_.refs_7_
  37.9 0.0 collective-permute-done.6.refs_2_.refs_9_
  37.9 0.0 collective-permute-done.8.level_ref.refs_3_
  37.9 0.5 collective-permute-start.9
  38.5 0.1 stack.5
  38.5 0.1 collective-permute-start.10
  38.7 1.4 collective-permute-done.9.level_near_ref.refs_4_
  40.0 0.2 join_sides.1
  40.2 0.0 copy-start.1
  40.2 1.3 collective-permute-start.11
  41.5 1.3 collective-permute-start.12
  42.8 0.0 collective-permute-done.10.refs_6_.refs_8_.refs_10_
  42.8 157.0 %attend_last.1 = (bf16[512,768]{1,0:T(8,128)(2,1)S(1)}, f32[8,512]{1,0:T(8,128)S(1)}) custom-call(s32[1]{0:T(128)} %bitcast.mine_ref, bf16[512,768]{1,0:T(8,128)(2,1)S(1)} %get-tuple-element.46.query_ref, bf16[512,256]{1,0:T(8,128)(2,1)S(1)} %beside.1.own_ref.refs_0_, f32[512,768]{1,0:T(8,128)S(1)} %get-tuple-element.69.refs_0_, ...), custom_call_target="tpu_custom_call" | custom-call | flops 200000000 | bytes 200000 | tf_op jit(solution)/shard_map/attend_last/pallas_call | solution.py:418
  199.8 0.0 collective-permute-done.11.behind_ref
  199.8 0.0 collective-permute-done.12.beyond_ref
  199.8 0.1 hand.1.kept_ref
  199.9 0.1 collective-permute-start.16
  200.0 1.4 collective-permute-start.13
  201.4 1.7 collective-permute-start.14
  203.1 0.9 collective-permute-start.15
  203.9 0.0 collective-permute-done.16.handed_ref
  203.9 0.0 copy-done.1
  203.9 0.0 copy-start
  203.9 2.5 %carry.1.linear_ref = f32[512,768]{1,0:T(8,128)S(1)} custom-call(s32[1]{0:T(128)} %bitcast.mine_ref, bf16[512,768]{1,0:T(8,128)(2,1)} %query_hbm.1, f32[512,768]{1,0:T(8,128)S(1)} %get-tuple-element.78.local_ref, f32[512,128]{1,0:T(8,128)S(1)} %get-tuple-element.79.grow_ref, f32[776,128]{1,0:T(8,128)S(1)} %hand.1.kept_ref, ...), custom_call_target="tpu_custom_call" | custom-call | flops 200000000 | bytes 200000 | tf_op jit(solution)/shard_map/carry/pallas_call | solution.py:484
  206.4 0.0 collective-permute-done.13
  206.4 0.0 collective-permute-done.14
  206.4 0.5 collective-permute-done.15
  206.9 2.6 %collective-permute-start.17 = (f32[8,512]{1,0:T(8,128)S(1)}, f32[8,512]{1,0:T(8,128)S(1)}, u32[]{:S(2)}, u32[]{:S(2)}) collective-permute-start(f32[8,512]{1,0:T(8,128)S(1)} %add_add_fusion.square_ref), channel_id=1, source_target_pairs={{0,1},{1,0},{2,3},{3,2},{4,5},{5,4},{6,7},{7,6},{8,9},{9,8},{10,11... | collective-permute-start | bytes 49160 | tf_op jit(solution)/shard_map/ppermute | solution.py:624
  209.5 1.1 collective-permute-done.17.other_ref
  210.7 0.0 copy-done
  210.7 1.5 finish.1
  (2 shorter events, 0.0 us)
Async XLA Ops:
  1.0 1.9 collective-permute-start
  3.0 17.7 %collective-permute-start.3 = (bf16[1024,256]{1,0:T(8,128)(2,1)S(1)}, bf16[1024,256]{1,0:T(8,128)(2,1)S(1)}, u32[]{:S(2)}, u32[]{:S(2)}) collective-permute-start(bf16[1024,256]{1,0:T(8,128)(2,1)S(1)} %stack.3), channel_id=1, source_target_pairs={{0,32},{16,48},{32,64},{48,80},{64,96},{80,112},{8,72},{24,88},{40... | collective-permute-start | bytes 1572872 | tf_op jit(solution)/shard_map/ppermute | solution.py:512
  4.3 12.9 %collective-permute-start.1 = (bf16[512,256]{1,0:T(8,128)(2,1)S(1)}, bf16[512,256]{1,0:T(8,128)(2,1)S(1)}, u32[]{:S(2)}, u32[]{:S(2)}) collective-permute-start(bf16[512,256]{1,0:T(8,128)(2,1)S(1)} %beside.1.own_ref.refs_0_), channel_id=1, source_target_pairs={{0,16},{8,24},{16,0},{24,8},{32,48},{40,56},{48,32},{56,40},{64,80... | collective-permute-start | bytes 786440 | tf_op jit(solution)/shard_map/ppermute | solution.py:512
  5.6 14.7 %collective-permute-start.2 = (bf16[512,256]{1,0:T(8,128)(2,1)S(1)}, bf16[512,256]{1,0:T(8,128)(2,1)S(1)}, u32[]{:S(2)}, u32[]{:S(2)}) collective-permute-start(bf16[512,256]{1,0:T(8,128)(2,1)S(1)} %beside.1.own_ref.refs_0_), channel_id=1, source_target_pairs={{0,96},{8,104},{16,112},{24,120},{1,97},{9,105},{17,113},{25,121},... | collective-permute-start | bytes 786440 | tf_op jit(solution)/shard_map/ppermute | solution.py:512
  20.3 1.8 collective-permute-start.7
  20.8 4.6 %collective-permute-start.4 = (bf16[1536,256]{1,0:T(8,128)(2,1)S(1)}, bf16[1536,256]{1,0:T(8,128)(2,1)S(1)}, u32[]{:S(2)}, u32[]{:S(2)}) collective-permute-start(bf16[1536,256]{1,0:T(8,128)(2,1)S(1)} %stack.4), channel_id=1, source_target_pairs={{0,8},{8,0},{16,24},{24,16},{32,40},{40,32},{48,56},{56,48},{64,72... | collective-permute-start | bytes 2359304 | tf_op jit(solution)/shard_map/ppermute | solution.py:512
  22.2 15.7 %collective-permute-start.8 = (bf16[1024,256]{1,0:T(8,128)(2,1)S(1)}, bf16[1024,256]{1,0:T(8,128)(2,1)S(1)}, u32[]{:S(2)}, u32[]{:S(2)}) collective-permute-start(bf16[1024,256]{1,0:T(8,128)(2,1)S(1)} %get-tuple-element.62), channel_id=1, source_target_pairs={{0,16},{8,24},{16,0},{24,8},{32,48},{40,56},{48,32},{56,40},{64,80... | collective-permute-start | bytes 1572872 | tf_op jit(solution)/shard_map/ppermute | solution.py:512
  22.8 15.1 %collective-permute-start.5 = (bf16[512,256]{1,0:T(8,128)(2,1)S(1)}, bf16[512,256]{1,0:T(8,128)(2,1)S(1)}, u32[]{:S(2)}, u32[]{:S(2)}) collective-permute-start(bf16[512,256]{1,0:T(8,128)(2,1)S(1)} %collective-permute-done.1.refs_0_.refs_5_), channel_id=1, source_target_pairs={{0,96},{8,104},{16,112},{24,120},{1,97},{9,105},{17,113},{25,121},... | collective-permute-start | bytes 786440 | tf_op jit(solution)/shard_map/ppermute | solution.py:512
  24.1 13.8 %collective-permute-start.6 = (bf16[512,256]{1,0:T(8,128)(2,1)S(1)}, bf16[512,256]{1,0:T(8,128)(2,1)S(1)}, u32[]{:S(2)}, u32[]{:S(2)}) collective-permute-start(bf16[512,256]{1,0:T(8,128)(2,1)S(1)} %collective-permute-done.1.refs_0_.refs_5_), channel_id=1, source_target_pairs={{0,32},{8,40},{16,48},{24,56},{32,64},{40,72},{48,80},{56,88},{64,... | collective-permute-start | bytes 786440 | tf_op jit(solution)/shard_map/ppermute | solution.py:512
  37.9 2.1 collective-permute-start.9
  38.5 4.3 %collective-permute-start.10 = (bf16[1536,256]{1,0:T(8,128)(2,1)S(1)}, bf16[1536,256]{1,0:T(8,128)(2,1)S(1)}, u32[]{:S(2)}, u32[]{:S(2)}) collective-permute-start(bf16[1536,256]{1,0:T(8,128)(2,1)S(1)} %stack.5), channel_id=1, source_target_pairs={{0,8},{8,0},{16,24},{24,16},{32,40},{40,32},{48,56},{56,48},{64,72... | collective-permute-start | bytes 2359304 | tf_op jit(solution)/shard_map/ppermute | solution.py:512
  40.2 163.7 %copy-start.1 = (f32[768]{0:T(1024)S(1)}, f32[768]{0:T(1024)}, u32[]{:S(2)}) copy-start(f32[768]{0:T(1024)} %gain_ref.2) | copy-start | bytes 9220
  40.2 159.6 %collective-permute-start.11 = (f32[776,128]{1,0:T(8,128)S(1)}, f32[776,128]{1,0:T(8,128)S(1)}, u32[]{:S(2)}, u32[]{:S(2)}) collective-permute-start(f32[776,128]{1,0:T(8,128)S(1)} %get-tuple-element.68), channel_id=1, source_target_pairs={{0,32},{16,48},{32,64},{48,80},{64,96},{80,112},{8,104},{24,120},{... | collective-permute-start | bytes 1191944 | tf_op jit(solution)/shard_map/ppermute | solution.py:512
  41.5 158.3 %collective-permute-start.12 = (f32[776,128]{1,0:T(8,128)S(1)}, f32[776,128]{1,0:T(8,128)S(1)}, u32[]{:S(2)}, u32[]{:S(2)}) collective-permute-start(f32[776,128]{1,0:T(8,128)S(1)} %get-tuple-element.68), channel_id=1, source_target_pairs={{8,72},{24,88},{40,104},{56,120},{9,73},{25,89},{41,105},{57,121},... | collective-permute-start | bytes 1191944 | tf_op jit(solution)/shard_map/ppermute | solution.py:512
  199.9 4.0 %collective-permute-start.16 = (f32[776,128]{1,0:T(8,128)S(1)}, f32[776,128]{1,0:T(8,128)S(1)}, u32[]{:S(2)}, u32[]{:S(2)}) collective-permute-start(f32[776,128]{1,0:T(8,128)S(1)} %hand.1.kept_ref), channel_id=1, source_target_pairs={{0,8},{8,0},{16,24},{24,16},{32,40},{40,32},{48,56},{56,48},{64,72... | collective-permute-start | bytes 1191944 | tf_op jit(solution)/shard_map/ppermute | solution.py:512
  200.0 6.4 %collective-permute-start.13 = (f32[8,512]{1,0:T(8,128)S(1)}, f32[8,512]{1,0:T(8,128)S(1)}, u32[]{:S(2)}, u32[]{:S(2)}) collective-permute-start(f32[8,512]{1,0:T(8,128)S(1)} %get-tuple-element.77), channel_id=1, source_target_pairs={{0,2},{1,3},{2,0},{3,1},{4,6},{5,7},{6,4},{7,5},{8,10},{9,11},{10,... | collective-permute-start | bytes 49160 | tf_op jit(solution)/shard_map/ppermute | solution.py:624
  201.4 5.1 %collective-permute-start.14 = (f32[8,512]{1,0:T(8,128)S(1)}, f32[8,512]{1,0:T(8,128)S(1)}, u32[]{:S(2)}, u32[]{:S(2)}) collective-permute-start(f32[8,512]{1,0:T(8,128)S(1)} %get-tuple-element.77), channel_id=1, source_target_pairs={{0,4},{1,5},{2,6},{3,7},{4,0},{5,1},{6,2},{7,3},{8,12},{9,13},{10,... | collective-permute-start | bytes 49160 | tf_op jit(solution)/shard_map/ppermute | solution.py:624
  203.1 3.8 %collective-permute-start.15 = (f32[8,512]{1,0:T(8,128)S(1)}, f32[8,512]{1,0:T(8,128)S(1)}, u32[]{:S(2)}, u32[]{:S(2)}) collective-permute-start(f32[8,512]{1,0:T(8,128)S(1)} %get-tuple-element.77), channel_id=1, source_target_pairs={{0,6},{1,7},{2,4},{3,5},{4,2},{5,3},{6,0},{7,1},{8,14},{9,15},{10,... | collective-permute-start | bytes 49160 | tf_op jit(solution)/shard_map/ppermute | solution.py:624
  203.9 6.7 %copy-start = (f32[768]{0:T(1024)S(1)}, f32[768]{0:T(1024)}, u32[]{:S(2)}) copy-start(f32[768]{0:T(1024)} %gain_ref.3) | copy-start | bytes 9220
  206.9 3.7 %collective-permute-start.17 = (f32[8,512]{1,0:T(8,128)S(1)}, f32[8,512]{1,0:T(8,128)S(1)}, u32[]{:S(2)}, u32[]{:S(2)}) collective-permute-start(f32[8,512]{1,0:T(8,128)S(1)} %add_add_fusion.square_ref), channel_id=1, source_target_pairs={{0,1},{1,0},{2,3},{3,2},{4,5},{5,4},{6,7},{7,6},{8,9},{9,8},{10,11... | collective-permute-start | bytes 49160 | tf_op jit(solution)/shard_map/ppermute | solution.py:624

commit v8 on v7

--- a/solution.py
+++ b/solution.py
@@ -575,7 +575,7 @@
 
     first_pieces = [(near, 0, ROWS)]
     near_query, *carry = attend(place, att_query, own, None, first_pieces, near_numbers)
-    carry, message, across, wrapped = tied(carry, message, across, wrapped)
+    carry, message, wrapped, across = tied(carry, message, wrapped, across)
     first = move(message, sibling)
     of_chip, leveled = join_cores(place, message, first, ring)
     level = move(leveled, sideways)

time: 216 us -> 215 us (level)
  Pallas kernels: 185 us -> 44.8 us
  starting transfers between devices: 18.3 us -> 157 us
    pallas_call x3, Pallas kernels: 175 us -> 34.3 us  [attend(): pl.pallas_call(functools.partial(attend_kernel, first, last, numbers_of,...]
    ppermute x14, starting transfers between devices: 11.8 us -> 143 us  [move(): return lax.ppermute(value, 'ctx', pairs)]
    ppermute x4, starting transfers between devices: 6.54 us -> 13.8 us  [over(): return lax.ppermute(value, 'tp', [(i, i ^ bit) for i in range(8)])]
  transfers between devices with their start and end apart: 18 -> 18, of which waited for: 6 -> 6; matrix products, arithmetic and copies ran while one was open for 0% -> 0% of each run, Pallas kernels for 86% -> 20%
where the time goes in v8:
time: 215 us; the launch traced here: 212 us
  starting transfers between devices  157 us (73%)
  Pallas kernels  44.8 us (21%)
  waiting for transfers between devices  9.79 us (5%)
    ppermute x14, starting transfers between devices, move(): return lax.ppermute(value, 'ctx', pairs)  143 us
    pallas_call x3, Pallas kernels, attend(): pl.pallas_call(functools.partial(attend_kernel, first, last, numbers_of,...  34.3 us
    ppermute x4, starting transfers between devices, over(): return lax.ppermute(value, 'tp', [(i, i ^ bit) for i in range(8)])  13.8 us
    ppermute x14, waiting for transfers between devices, move(): return lax.ppermute(value, 'ctx', pairs)  6.77 us
    pallas_call x1, Pallas kernels, recur(): pl.pallas_call(recur_kernel, out_shape=(jax.ShapeDtypeStruct((ROWS, HEADS...  5.04 us
  transfers between devices with their start and end apart: 18, of which 6 were waited for; matrix products, arithmetic and copies ran while one was open for 0% of the time, Pallas kernels for 20%

profile of v8, /device:TPU:101, one launch (start us, length us, event | category | flops | bytes accessed | tf_op | source)
XLA Modules:
  0.0 211.9 jit_solution(10871452147359048067)
XLA Ops:
  0.0 1.0 beside.1.own_ref.refs_0_
  1.0 0.8 collective-permute-start
  1.8 1.2 collective-permute-done.refs_0_.refs_1_.refs_11_
  3.0 1.3 collective-permute-start.3
  4.3 1.3 collective-permute-start.1
  5.6 1.3 collective-permute-start.2
  6.9 5.0 %recur.1 = (f32[512,768]{1,0:T(8,128)S(1)}, f32[512,128]{1,0:T(8,128)S(1)}, f32[776,128]{1,0:T(8,128)S(1)}) custom-call(bf16[512,768]{1,0:T(8,128)(2,1)} %query_hbm.1, bf16[512,768]{1,0:T(8,128)(2,1)} %k_hbm.1, bf16[512,768]{1,0:T(8,128)(2,1)} %v_hbm.1, f32[6,512]{1,0:T(8,128)} %bitcast.2), custom_call_target="tpu_custom_call" | custom-call | flops 200000000 | bytes 200000 | tf_op jit(solution)/shard_map/recur/pallas_call | solution.py:91
  11.9 5.3 %attend_first.1 = (bf16[512,768]{1,0:T(8,128)(2,1)S(1)}, f32[512,768]{1,0:T(8,128)S(1)}, f32[512,128]{1,0:T(8,128)S(1)}, bf16[32,128]{1,0:T(8,128)(2,1)S(1)}) custom-call(s32[1]{0:T(128)} %bitcast.mine_ref, bf16[512,768]{1,0:T(8,128)(2,1)} %query_ref.1, bf16[512,256]{1,0:T(8,128)(2,1)S(1)} %beside.1.own_ref.refs_0_, ...), custom_call_target="tpu_custom_call" | custom-call | flops 200000000 | bytes 200000 | tf_op jit(solution)/shard_map/attend_first/pallas_call | solution.py:418
  17.2 3.0 %collective-permute-done.1.refs_1_.refs_5_.refs_14_ = bf16[512,256]{1,0:T(8,128)(2,1)S(1)} collective-permute-done((bf16[512,256]{1,0:T(8,128)(2,1)S(1)}, bf16[512,256]{1,0:T(8,128)(2,1)S(1)}, u32[]{:S(2)}, u32[]{:S(2)}) %collective-permute-start.1) | collective-permute-done | bytes 262176 | tf_op jit(solution)/shard_map/ppermute | solution.py:512
  20.2 0.0 collective-permute-done.2.refs_0_.refs_5_
  20.2 0.5 collective-permute-start.7
  20.7 0.0 collective-permute-done.3.refs_0_.refs_3_.blocks_ref.refs_12_
  20.7 0.1 stack.4
  20.8 0.1 collective-permute-start.4
  20.9 1.2 collective-permute-done.7.other_ref.core_ref
  22.1 0.1 join_cores.1
  22.2 0.6 collective-permute-start.8
  22.8 1.3 collective-permute-start.5
  24.1 1.3 collective-permute-start.6
  25.4 0.0 collective-permute-done.4.refs_4_.refs_6_.refs_13_.refs_15_
  25.4 12.5 %attend_middle.1 = (f32[512,768]{1,0:T(8,128)S(1)}, f32[512,128]{1,0:T(8,128)S(1)}, bf16[32,128]{1,0:T(8,128)(2,1)S(1)}) custom-call(s32[1]{0:T(128)} %bitcast.mine_ref, bf16[512,768]{1,0:T(8,128)(2,1)S(1)} %get-tuple-element.46.query_ref, bf16[512,256]{1,0:T(8,128)(2,1)S(1)} %beside.1.own_ref.refs_0_, f32[512,768]{1,0:T(8,128)S(1)} %get-tuple-element.52.refs_0_, ...), custom_call_target="tpu_custom_call" | custom-call | flops 200000000 | bytes 200000 | tf_op jit(solution)/shard_map/attend_middle/pallas_call | solution.py:418
  37.9 0.0 collective-permute-done.5.refs_1_.refs_7_
  37.9 0.0 collective-permute-done.6.refs_2_.refs_9_
  37.9 0.0 collective-permute-done.8.level_ref.refs_3_
  37.9 0.5 collective-permute-start.9
  38.5 0.1 stack.5
  38.5 0.1 collective-permute-start.10
  38.7 1.4 collective-permute-done.9.level_near_ref.refs_4_
  40.0 0.2 join_sides.1
  40.2 0.0 copy-start.1
  40.2 1.3 collective-permute-start.11
  41.5 1.3 collective-permute-start.12
  42.8 0.0 collective-permute-done.10.refs_6_.refs_8_.refs_10_
  42.8 16.5 %attend_last.1 = (bf16[512,768]{1,0:T(8,128)(2,1)S(1)}, f32[8,512]{1,0:T(8,128)S(1)}) custom-call(s32[1]{0:T(128)} %bitcast.mine_ref, bf16[512,768]{1,0:T(8,128)(2,1)S(1)} %get-tuple-element.46.query_ref, bf16[512,256]{1,0:T(8,128)(2,1)S(1)} %beside.1.own_ref.refs_0_, f32[512,768]{1,0:T(8,128)S(1)} %get-tuple-element.69.refs_0_, ...), custom_call_target="tpu_custom_call" | custom-call | flops 200000000 | bytes 200000 | tf_op jit(solution)/shard_map/attend_last/pallas_call | solution.py:418
  59.3 0.0 collective-permute-done.11.behind_ref
  59.3 0.0 collective-permute-done.12.beyond_ref
  59.4 0.1 hand.1.kept_ref
  59.4 131.6 %collective-permute-start.16 = (f32[776,128]{1,0:T(8,128)S(1)}, f32[776,128]{1,0:T(8,128)S(1)}, u32[]{:S(2)}, u32[]{:S(2)}) collective-permute-start(f32[776,128]{1,0:T(8,128)S(1)} %hand.1.kept_ref), channel_id=1, source_target_pairs={{0,8},{8,0},{16,24},{24,16},{32,40},{40,32},{48,56},{56,48},{64,72... | collective-permute-start | bytes 1191944 | tf_op jit(solution)/shard_map/ppermute | solution.py:512
  191.0 10.4 %collective-permute-start.13 = (f32[8,512]{1,0:T(8,128)S(1)}, f32[8,512]{1,0:T(8,128)S(1)}, u32[]{:S(2)}, u32[]{:S(2)}) collective-permute-start(f32[8,512]{1,0:T(8,128)S(1)} %get-tuple-element.77), channel_id=1, source_target_pairs={{0,2},{1,3},{2,0},{3,1},{4,6},{5,7},{6,4},{7,5},{8,10},{9,11},{10,... | collective-permute-start | bytes 49160 | tf_op jit(solution)/shard_map/ppermute | solution.py:624
  201.4 2.6 %collective-permute-start.14 = (f32[8,512]{1,0:T(8,128)S(1)}, f32[8,512]{1,0:T(8,128)S(1)}, u32[]{:S(2)}, u32[]{:S(2)}) collective-permute-start(f32[8,512]{1,0:T(8,128)S(1)} %get-tuple-element.77), channel_id=1, source_target_pairs={{0,4},{1,5},{2,6},{3,7},{4,0},{5,1},{6,2},{7,3},{8,12},{9,13},{10,... | collective-permute-start | bytes 49160 | tf_op jit(solution)/shard_map/ppermute | solution.py:624
  204.0 0.0 collective-permute-start.15
  204.0 0.0 collective-permute-done.16.handed_ref
  204.0 0.0 copy-done.1
  204.0 0.0 copy-start
  204.0 2.5 %carry.1.linear_ref = f32[512,768]{1,0:T(8,128)S(1)} custom-call(s32[1]{0:T(128)} %bitcast.mine_ref, bf16[512,768]{1,0:T(8,128)(2,1)} %query_hbm.1, f32[512,768]{1,0:T(8,128)S(1)} %get-tuple-element.78.local_ref, f32[512,128]{1,0:T(8,128)S(1)} %get-tuple-element.79.grow_ref, f32[776,128]{1,0:T(8,128)S(1)} %hand.1.kept_ref, ...), custom_call_target="tpu_custom_call" | custom-call | flops 200000000 | bytes 200000 | tf_op jit(solution)/shard_map/carry/pallas_call | solution.py:484
  206.5 0.0 collective-permute-done.13
  206.5 0.0 collective-permute-done.14
  206.5 1.3 collective-permute-done.15
  207.8 0.9 collective-permute-start.17
  208.7 1.7 collective-permute-done.17.other_ref
  210.4 0.0 copy-done
  210.4 1.5 finish.1
  (2 shorter events, 0.0 us)
Async XLA Ops:
  1.0 1.9 collective-permute-start
  3.0 17.7 %collective-permute-start.3 = (bf16[1024,256]{1,0:T(8,128)(2,1)S(1)}, bf16[1024,256]{1,0:T(8,128)(2,1)S(1)}, u32[]{:S(2)}, u32[]{:S(2)}) collective-permute-start(bf16[1024,256]{1,0:T(8,128)(2,1)S(1)} %stack.3), channel_id=1, source_target_pairs={{0,32},{16,48},{32,64},{48,80},{64,96},{80,112},{8,72},{24,88},{40... | collective-permute-start | bytes 1572872 | tf_op jit(solution)/shard_map/ppermute | solution.py:512
  4.3 16.0 %collective-permute-start.1 = (bf16[512,256]{1,0:T(8,128)(2,1)S(1)}, bf16[512,256]{1,0:T(8,128)(2,1)S(1)}, u32[]{:S(2)}, u32[]{:S(2)}) collective-permute-start(bf16[512,256]{1,0:T(8,128)(2,1)S(1)} %beside.1.own_ref.refs_0_), channel_id=1, source_target_pairs={{0,96},{8,104},{16,112},{24,120},{1,97},{9,105},{17,113},{25,121},... | collective-permute-start | bytes 786440 | tf_op jit(solution)/shard_map/ppermute | solution.py:512
  5.6 14.7 %collective-permute-start.2 = (bf16[512,256]{1,0:T(8,128)(2,1)S(1)}, bf16[512,256]{1,0:T(8,128)(2,1)S(1)}, u32[]{:S(2)}, u32[]{:S(2)}) collective-permute-start(bf16[512,256]{1,0:T(8,128)(2,1)S(1)} %beside.1.own_ref.refs_0_), channel_id=1, source_target_pairs={{0,16},{8,24},{16,0},{24,8},{32,48},{40,56},{48,32},{56,40},{64,80... | collective-permute-start | bytes 786440 | tf_op jit(solution)/shard_map/ppermute | solution.py:512
  20.2 1.8 collective-permute-start.7
  20.8 4.6 %collective-permute-start.4 = (bf16[1536,256]{1,0:T(8,128)(2,1)S(1)}, bf16[1536,256]{1,0:T(8,128)(2,1)S(1)}, u32[]{:S(2)}, u32[]{:S(2)}) collective-permute-start(bf16[1536,256]{1,0:T(8,128)(2,1)S(1)} %stack.4), channel_id=1, source_target_pairs={{0,8},{8,0},{16,24},{24,16},{32,40},{40,32},{48,56},{56,48},{64,72... | collective-permute-start | bytes 2359304 | tf_op jit(solution)/shard_map/ppermute | solution.py:512
  22.2 15.7 %collective-permute-start.8 = (bf16[1024,256]{1,0:T(8,128)(2,1)S(1)}, bf16[1024,256]{1,0:T(8,128)(2,1)S(1)}, u32[]{:S(2)}, u32[]{:S(2)}) collective-permute-start(bf16[1024,256]{1,0:T(8,128)(2,1)S(1)} %get-tuple-element.62), channel_id=1, source_target_pairs={{0,16},{8,24},{16,0},{24,8},{32,48},{40,56},{48,32},{56,40},{64,80... | collective-permute-start | bytes 1572872 | tf_op jit(solution)/shard_map/ppermute | solution.py:512
  22.8 15.1 %collective-permute-start.5 = (bf16[512,256]{1,0:T(8,128)(2,1)S(1)}, bf16[512,256]{1,0:T(8,128)(2,1)S(1)}, u32[]{:S(2)}, u32[]{:S(2)}) collective-permute-start(bf16[512,256]{1,0:T(8,128)(2,1)S(1)} %collective-permute-done.2.refs_0_.refs_5_), channel_id=1, source_target_pairs={{0,96},{8,104},{16,112},{24,120},{1,97},{9,105},{17,113},{25,121},... | collective-permute-start | bytes 786440 | tf_op jit(solution)/shard_map/ppermute | solution.py:512
  24.1 13.8 %collective-permute-start.6 = (bf16[512,256]{1,0:T(8,128)(2,1)S(1)}, bf16[512,256]{1,0:T(8,128)(2,1)S(1)}, u32[]{:S(2)}, u32[]{:S(2)}) collective-permute-start(bf16[512,256]{1,0:T(8,128)(2,1)S(1)} %collective-permute-done.2.refs_0_.refs_5_), channel_id=1, source_target_pairs={{0,32},{8,40},{16,48},{24,56},{32,64},{40,72},{48,80},{56,88},{64,... | collective-permute-start | bytes 786440 | tf_op jit(solution)/shard_map/ppermute | solution.py:512
  37.9 2.1 collective-permute-start.9
  38.5 4.3 %collective-permute-start.10 = (bf16[1536,256]{1,0:T(8,128)(2,1)S(1)}, bf16[1536,256]{1,0:T(8,128)(2,1)S(1)}, u32[]{:S(2)}, u32[]{:S(2)}) collective-permute-start(bf16[1536,256]{1,0:T(8,128)(2,1)S(1)} %stack.5), channel_id=1, source_target_pairs={{0,8},{8,0},{16,24},{24,16},{32,40},{40,32},{48,56},{56,48},{64,72... | collective-permute-start | bytes 2359304 | tf_op jit(solution)/shard_map/ppermute | solution.py:512
  40.2 163.8 %copy-start.1 = (f32[768]{0:T(1024)S(1)}, f32[768]{0:T(1024)}, u32[]{:S(2)}) copy-start(f32[768]{0:T(1024)} %gain_ref.2) | copy-start | bytes 9220
  40.2 19.1 %collective-permute-start.11 = (f32[776,128]{1,0:T(8,128)S(1)}, f32[776,128]{1,0:T(8,128)S(1)}, u32[]{:S(2)}, u32[]{:S(2)}) collective-permute-start(f32[776,128]{1,0:T(8,128)S(1)} %get-tuple-element.68), channel_id=1, source_target_pairs={{0,32},{16,48},{32,64},{48,80},{64,96},{80,112},{8,104},{24,120},{... | collective-permute-start | bytes 1191944 | tf_op jit(solution)/shard_map/ppermute | solution.py:512
  41.5 17.8 %collective-permute-start.12 = (f32[776,128]{1,0:T(8,128)S(1)}, f32[776,128]{1,0:T(8,128)S(1)}, u32[]{:S(2)}, u32[]{:S(2)}) collective-permute-start(f32[776,128]{1,0:T(8,128)S(1)} %get-tuple-element.68), channel_id=1, source_target_pairs={{8,72},{24,88},{40,104},{56,120},{9,73},{25,89},{41,105},{57,121},... | collective-permute-start | bytes 1191944 | tf_op jit(solution)/shard_map/ppermute | solution.py:512
  59.4 144.5 %collective-permute-start.16 = (f32[776,128]{1,0:T(8,128)S(1)}, f32[776,128]{1,0:T(8,128)S(1)}, u32[]{:S(2)}, u32[]{:S(2)}) collective-permute-start(f32[776,128]{1,0:T(8,128)S(1)} %hand.1.kept_ref), channel_id=1, source_target_pairs={{0,8},{8,0},{16,24},{24,16},{32,40},{40,32},{48,56},{56,48},{64,72... | collective-permute-start | bytes 1191944 | tf_op jit(solution)/shard_map/ppermute | solution.py:512
  191.0 15.5 %collective-permute-start.13 = (f32[8,512]{1,0:T(8,128)S(1)}, f32[8,512]{1,0:T(8,128)S(1)}, u32[]{:S(2)}, u32[]{:S(2)}) collective-permute-start(f32[8,512]{1,0:T(8,128)S(1)} %get-tuple-element.77), channel_id=1, source_target_pairs={{0,2},{1,3},{2,0},{3,1},{4,6},{5,7},{6,4},{7,5},{8,10},{9,11},{10,... | collective-permute-start | bytes 49160 | tf_op jit(solution)/shard_map/ppermute | solution.py:624
  201.4 5.1 %collective-permute-start.14 = (f32[8,512]{1,0:T(8,128)S(1)}, f32[8,512]{1,0:T(8,128)S(1)}, u32[]{:S(2)}, u32[]{:S(2)}) collective-permute-start(f32[8,512]{1,0:T(8,128)S(1)} %get-tuple-element.77), channel_id=1, source_target_pairs={{0,4},{1,5},{2,6},{3,7},{4,0},{5,1},{6,2},{7,3},{8,12},{9,13},{10,... | collective-permute-start | bytes 49160 | tf_op jit(solution)/shard_map/ppermute | solution.py:624
  204.0 3.8 %collective-permute-start.15 = (f32[8,512]{1,0:T(8,128)S(1)}, f32[8,512]{1,0:T(8,128)S(1)}, u32[]{:S(2)}, u32[]{:S(2)}) collective-permute-start(f32[8,512]{1,0:T(8,128)S(1)} %get-tuple-element.77), channel_id=1, source_target_pairs={{0,6},{1,7},{2,4},{3,5},{4,2},{5,3},{6,0},{7,1},{8,14},{9,15},{10,... | collective-permute-start | bytes 49160 | tf_op jit(solution)/shard_map/ppermute | solution.py:624
  204.0 6.4 %copy-start = (f32[768]{0:T(1024)S(1)}, f32[768]{0:T(1024)}, u32[]{:S(2)}) copy-start(f32[768]{0:T(1024)} %gain_ref.3) | copy-start | bytes 9220
  207.8 2.6 %collective-permute-start.17 = (f32[8,512]{1,0:T(8,128)S(1)}, f32[8,512]{1,0:T(8,128)S(1)}, u32[]{:S(2)}, u32[]{:S(2)}) collective-permute-start(f32[8,512]{1,0:T(8,128)S(1)} %add_add_fusion.square_ref), channel_id=1, source_target_pairs={{0,1},{1,0},{2,3},{3,2},{4,5},{5,4},{6,7},{7,6},{8,9},{9,8},{10,11... | collective-permute-start | bytes 49160 | tf_op jit(solution)/shard_map/ppermute | solution.py:624

commit v9 on v8

--- a/solution.py
+++ b/solution.py
@@ -472,8 +472,12 @@
         out_ref[:, head(h)] = result * lax.rsqrt(square + EPS) * gain_ref[head(h)][None, :]
 
 
-def finish_kernel(features, attention_ref, square_ref, other_ref, linear_ref, gain_ref, out_ref):
-    factor = lax.rsqrt((square_ref[...] + other_ref[...]) / features + EPS)
+def finish_kernel(features, attention_ref, linear_ref, gain_ref, *refs):
+    *square_refs, out_ref = refs
+    total = square_refs[0][...]
+    for square_ref in square_refs[1:]:
+        total = total + square_ref[...]
+    factor = lax.rsqrt(total / features + EPS)
     factor = dot(factor, jnp.full((8, HD), 0.125, f32), ((0,), (0,)), highest)
     for h in range(HEADS):
         part = attention_ref[:, head(h)].astype(f32) * factor * gain_ref[head(h)][None, :]
@@ -624,14 +628,13 @@
         return lax.ppermute(value, "tp", [(i, i ^ bit) for i in range(8)])
 
     squares, state_behind, state_beyond = tied(squares, state_behind, state_beyond)
-    others = [over(squares, bit) for bit in (2, 4, 6)]
+    others = [over(squares, bit) for bit in range(1, 8)]
     kept = hand(place, state_behind, state_beyond)
     handed = move(kept, sibling)
     linear = carry_in(place, lh_query, local, grow, kept, handed, other_chip, first, lh_gain)
     others, linear = tied(others, linear)
-    squares = squares + others[0] + others[1] + others[2]
     features = HEADS * HD * lax.axis_size("tp")
-    return finish(float(features), attention, squares, over(squares, 1), linear, att_gain)
+    return finish(float(features), attention, linear, att_gain, squares, *others)
 
 
 def solution(mesh):

time: 215 us -> 219 us (1.019)
  Pallas kernels: 44.8 us -> 185 us
  starting transfers between devices: 157 us -> 21.6 us
    pallas_call x3, Pallas kernels: 34.3 us -> 175 us  [attend(): pl.pallas_call(functools.partial(attend_kernel, first, last, numbers_of,...]
    ppermute x14, starting transfers between devices: 143 us -> 11.8 us  [move(): return lax.ppermute(value, 'ctx', pairs)]
    ppermute x4 -> x7, starting transfers between devices: 13.8 us -> 9.89 us  [over(): return lax.ppermute(value, 'tp', [(i, i ^ bit) for i in range(8)])]
  transfers between devices with their start and end apart: 18 -> 21, of which waited for: 6 -> 5; matrix products, arithmetic and copies ran while one was open for 0% -> 0% of each run, Pallas kernels for 20% -> 84%
where the time goes in v9:
time: 219 us; the launch traced here: 216 us
  Pallas kernels  185 us (84%)
  starting transfers between devices  21.6 us (10%)
  waiting for transfers between devices  8.96 us (4%)
    pallas_call x3, Pallas kernels, attend(): pl.pallas_call(functools.partial(attend_kernel, first, last, numbers_of,...  175 us
    ppermute x14, starting transfers between devices, move(): return lax.ppermute(value, 'ctx', pairs)  11.8 us
    ppermute x7, starting transfers between devices, over(): return lax.ppermute(value, 'tp', [(i, i ^ bit) for i in range(8)])  9.89 us
    ppermute x14, waiting for transfers between devices, move(): return lax.ppermute(value, 'ctx', pairs)  6.77 us
    pallas_call x1, Pallas kernels, recur(): pl.pallas_call(recur_kernel, out_shape=(jax.ShapeDtypeStruct((ROWS, HEADS...  5.04 us
  transfers between devices with their start and end apart: 21, of which 5 were waited for; matrix products, arithmetic and copies ran while one was open for 0% of the time, Pallas kernels for 84%

profile of v9, /device:TPU:101, one launch (start us, length us, event | category | flops | bytes accessed | tf_op | source)
XLA Modules:
  0.0 216.1 jit_solution(17459613043502435323)
XLA Ops:
  0.0 1.0 beside.1.own_ref.refs_0_
  1.0 0.8 collective-permute-start
  1.8 1.2 collective-permute-done.refs_0_.refs_1_.refs_11_
  3.0 1.3 collective-permute-start.3
  4.3 1.3 collective-permute-start.1
  5.6 1.3 collective-permute-start.2
  6.9 5.0 %recur.1 = (f32[512,768]{1,0:T(8,128)S(1)}, f32[512,128]{1,0:T(8,128)S(1)}, f32[776,128]{1,0:T(8,128)S(1)}) custom-call(bf16[512,768]{1,0:T(8,128)(2,1)} %query_hbm.1, bf16[512,768]{1,0:T(8,128)(2,1)} %k_hbm.1, bf16[512,768]{1,0:T(8,128)(2,1)} %v_hbm.1, f32[6,512]{1,0:T(8,128)} %bitcast.2), custom_call_target="tpu_custom_call" | custom-call | flops 200000000 | bytes 200000 | tf_op jit(solution)/shard_map/recur/pallas_call | solution.py:91
  11.9 5.3 %attend_first.1 = (bf16[512,768]{1,0:T(8,128)(2,1)S(1)}, f32[512,768]{1,0:T(8,128)S(1)}, f32[512,128]{1,0:T(8,128)S(1)}, bf16[32,128]{1,0:T(8,128)(2,1)S(1)}) custom-call(s32[1]{0:T(128)} %bitcast.mine_ref, bf16[512,768]{1,0:T(8,128)(2,1)} %query_ref.1, bf16[512,256]{1,0:T(8,128)(2,1)S(1)} %beside.1.own_ref.refs_0_, ...), custom_call_target="tpu_custom_call" | custom-call | flops 200000000 | bytes 200000 | tf_op jit(solution)/shard_map/attend_first/pallas_call | solution.py:418
  17.2 3.0 %collective-permute-done.1.refs_1_.refs_5_.refs_14_ = bf16[512,256]{1,0:T(8,128)(2,1)S(1)} collective-permute-done((bf16[512,256]{1,0:T(8,128)(2,1)S(1)}, bf16[512,256]{1,0:T(8,128)(2,1)S(1)}, u32[]{:S(2)}, u32[]{:S(2)}) %collective-permute-start.1) | collective-permute-done | bytes 262176 | tf_op jit(solution)/shard_map/ppermute | solution.py:516
  20.2 0.0 collective-permute-done.2.refs_0_.refs_5_
  20.2 0.5 collective-permute-start.7
  20.7 0.0 collective-permute-done.3.refs_0_.refs_3_.blocks_ref.refs_12_
  20.7 0.1 stack.4
  20.8 0.1 collective-permute-start.4
  20.9 1.2 collective-permute-done.7.other_ref.core_ref
  22.1 0.1 join_cores.1
  22.2 0.6 collective-permute-start.8
  22.8 1.3 collective-permute-start.5
  24.1 1.3 collective-permute-start.6
  25.4 0.0 collective-permute-done.4.refs_4_.refs_6_.refs_13_.refs_15_
  25.4 12.5 %attend_middle.1 = (f32[512,768]{1,0:T(8,128)S(1)}, f32[512,128]{1,0:T(8,128)S(1)}, bf16[32,128]{1,0:T(8,128)(2,1)S(1)}) custom-call(s32[1]{0:T(128)} %bitcast.mine_ref, bf16[512,768]{1,0:T(8,128)(2,1)S(1)} %get-tuple-element.50.query_ref, bf16[512,256]{1,0:T(8,128)(2,1)S(1)} %beside.1.own_ref.refs_0_, f32[512,768]{1,0:T(8,128)S(1)} %get-tuple-element.56.refs_0_, ...), custom_call_target="tpu_custom_call" | custom-call | flops 200000000 | bytes 200000 | tf_op jit(solution)/shard_map/attend_middle/pallas_call | solution.py:418
  37.9 0.0 collective-permute-done.5.refs_1_.refs_7_
  37.9 0.0 collective-permute-done.6.refs_2_.refs_9_
  37.9 0.0 collective-permute-done.8.level_ref.refs_3_
  37.9 0.5 collective-permute-start.9
  38.5 0.1 stack.5
  38.5 0.1 collective-permute-start.10
  38.7 1.4 collective-permute-done.9.level_near_ref.refs_4_
  40.0 0.2 join_sides.1
  40.2 0.0 copy-start.1
  40.2 1.3 collective-permute-start.11
  41.5 1.3 collective-permute-start.12
  42.8 0.0 collective-permute-done.10.refs_6_.refs_8_.refs_10_
  42.8 157.0 %attend_last.1 = (bf16[512,768]{1,0:T(8,128)(2,1)S(1)}, f32[8,512]{1,0:T(8,128)S(1)}) custom-call(s32[1]{0:T(128)} %bitcast.mine_ref, bf16[512,768]{1,0:T(8,128)(2,1)S(1)} %get-tuple-element.50.query_ref, bf16[512,256]{1,0:T(8,128)(2,1)S(1)} %beside.1.own_ref.refs_0_, f32[512,768]{1,0:T(8,128)S(1)} %get-tuple-element.73.refs_0_, ...), custom_call_target="tpu_custom_call" | custom-call | flops 200000000 | bytes 200000 | tf_op jit(solution)/shard_map/attend_last/pallas_call | solution.py:418
  199.8 0.0 collective-permute-done.11.behind_ref
  199.8 0.0 collective-permute-done.12.beyond_ref
  199.8 0.1 hand.1.kept_ref
  199.9 0.1 collective-permute-start.20
  200.0 1.8 collective-permute-start.13
  201.8 1.3 collective-permute-start.14
  203.1 0.0 collective-permute-start.15
  203.1 2.6 %collective-permute-start.16 = (f32[8,512]{1,0:T(8,128)S(1)}, f32[8,512]{1,0:T(8,128)S(1)}, u32[]{:S(2)}, u32[]{:S(2)}) collective-permute-start(f32[8,512]{1,0:T(8,128)S(1)} %get-tuple-element.81.refs_0_), channel_id=1, source_target_pairs={{0,4},{1,5},{2,6},{3,7},{4,0},{5,1},{6,2},{7,3},{8,12},{9,13},{10,... | collective-permute-start | bytes 49160 | tf_op jit(solution)/shard_map/ppermute | solution.py:628
  205.7 0.0 collective-permute-done.13.refs_1_
  205.7 1.4 collective-permute-start.17
  207.2 0.0 collective-permute-done.14.refs_2_
  207.2 2.7 %collective-permute-start.18 = (f32[8,512]{1,0:T(8,128)S(1)}, f32[8,512]{1,0:T(8,128)S(1)}, u32[]{:S(2)}, u32[]{:S(2)}) collective-permute-start(f32[8,512]{1,0:T(8,128)S(1)} %get-tuple-element.81.refs_0_), channel_id=1, source_target_pairs={{0,6},{1,7},{2,4},{3,5},{4,2},{5,3},{6,0},{7,1},{8,14},{9,15},{10,... | collective-permute-start | bytes 49160 | tf_op jit(solution)/shard_map/ppermute | solution.py:628
  209.9 0.0 collective-permute-done.20.handed_ref
  209.9 0.0 collective-permute-start.19
  209.9 0.0 copy-done.1
  209.9 0.0 copy-start
  209.9 2.5 %carry.1.linear_ref = f32[512,768]{1,0:T(8,128)S(1)} custom-call(s32[1]{0:T(128)} %bitcast.mine_ref, bf16[512,768]{1,0:T(8,128)(2,1)} %query_hbm.1, f32[512,768]{1,0:T(8,128)S(1)} %get-tuple-element.82.local_ref, f32[512,128]{1,0:T(8,128)S(1)} %get-tuple-element.83.grow_ref, f32[776,128]{1,0:T(8,128)S(1)} %hand.1.kept_ref, ...), custom_call_target="tpu_custom_call" | custom-call | flops 200000000 | bytes 200000 | tf_op jit(solution)/shard_map/carry/pallas_call | solution.py:488
  212.4 0.0 collective-permute-done.15.refs_3_
  212.4 0.0 collective-permute-done.16.refs_4_
  212.4 0.0 collective-permute-done.17.refs_5_
  212.4 0.0 collective-permute-done.18.refs_6_
  212.4 2.2 %collective-permute-done.19.refs_7_ = f32[8,512]{1,0:T(8,128)S(1)} collective-permute-done((f32[8,512]{1,0:T(8,128)S(1)}, f32[8,512]{1,0:T(8,128)S(1)}, u32[]{:S(2)}, u32[]{:S(2)}) %collective-permute-start.19) | collective-permute-done | bytes 16416 | tf_op jit(solution)/shard_map/ppermute | solution.py:628
  214.6 0.0 copy-done
  214.6 1.5 finish.1
  (1 shorter events, 0.0 us)
Async XLA Ops:
  1.0 1.9 collective-permute-start
  3.0 17.7 %collective-permute-start.3 = (bf16[1024,256]{1,0:T(8,128)(2,1)S(1)}, bf16[1024,256]{1,0:T(8,128)(2,1)S(1)}, u32[]{:S(2)}, u32[]{:S(2)}) collective-permute-start(bf16[1024,256]{1,0:T(8,128)(2,1)S(1)} %stack.3), channel_id=1, source_target_pairs={{0,32},{16,48},{32,64},{48,80},{64,96},{80,112},{8,72},{24,88},{40... | collective-permute-start | bytes 1572872 | tf_op jit(solution)/shard_map/ppermute | solution.py:516
  4.3 16.0 %collective-permute-start.1 = (bf16[512,256]{1,0:T(8,128)(2,1)S(1)}, bf16[512,256]{1,0:T(8,128)(2,1)S(1)}, u32[]{:S(2)}, u32[]{:S(2)}) collective-permute-start(bf16[512,256]{1,0:T(8,128)(2,1)S(1)} %beside.1.own_ref.refs_0_), channel_id=1, source_target_pairs={{0,96},{8,104},{16,112},{24,120},{1,97},{9,105},{17,113},{25,121},... | collective-permute-start | bytes 786440 | tf_op jit(solution)/shard_map/ppermute | solution.py:516
  5.6 14.7 %collective-permute-start.2 = (bf16[512,256]{1,0:T(8,128)(2,1)S(1)}, bf16[512,256]{1,0:T(8,128)(2,1)S(1)}, u32[]{:S(2)}, u32[]{:S(2)}) collective-permute-start(bf16[512,256]{1,0:T(8,128)(2,1)S(1)} %beside.1.own_ref.refs_0_), channel_id=1, source_target_pairs={{0,16},{8,24},{16,0},{24,8},{32,48},{40,56},{48,32},{56,40},{64,80... | collective-permute-start | bytes 786440 | tf_op jit(solution)/shard_map/ppermute | solution.py:516
  20.2 1.8 collective-permute-start.7
  20.8 4.6 %collective-permute-start.4 = (bf16[1536,256]{1,0:T(8,128)(2,1)S(1)}, bf16[1536,256]{1,0:T(8,128)(2,1)S(1)}, u32[]{:S(2)}, u32[]{:S(2)}) collective-permute-start(bf16[1536,256]{1,0:T(8,128)(2,1)S(1)} %stack.4), channel_id=1, source_target_pairs={{0,8},{8,0},{16,24},{24,16},{32,40},{40,32},{48,56},{56,48},{64,72... | collective-permute-start | bytes 2359304 | tf_op jit(solution)/shard_map/ppermute | solution.py:516
  22.2 15.7 %collective-permute-start.8 = (bf16[1024,256]{1,0:T(8,128)(2,1)S(1)}, bf16[1024,256]{1,0:T(8,128)(2,1)S(1)}, u32[]{:S(2)}, u32[]{:S(2)}) collective-permute-start(bf16[1024,256]{1,0:T(8,128)(2,1)S(1)} %get-tuple-element.66), channel_id=1, source_target_pairs={{0,16},{8,24},{16,0},{24,8},{32,48},{40,56},{48,32},{56,40},{64,80... | collective-permute-start | bytes 1572872 | tf_op jit(solution)/shard_map/ppermute | solution.py:516
  22.8 15.1 %collective-permute-start.5 = (bf16[512,256]{1,0:T(8,128)(2,1)S(1)}, bf16[512,256]{1,0:T(8,128)(2,1)S(1)}, u32[]{:S(2)}, u32[]{:S(2)}) collective-permute-start(bf16[512,256]{1,0:T(8,128)(2,1)S(1)} %collective-permute-done.2.refs_0_.refs_5_), channel_id=1, source_target_pairs={{0,96},{8,104},{16,112},{24,120},{1,97},{9,105},{17,113},{25,121},... | collective-permute-start | bytes 786440 | tf_op jit(solution)/shard_map/ppermute | solution.py:516
  24.1 13.8 %collective-permute-start.6 = (bf16[512,256]{1,0:T(8,128)(2,1)S(1)}, bf16[512,256]{1,0:T(8,128)(2,1)S(1)}, u32[]{:S(2)}, u32[]{:S(2)}) collective-permute-start(bf16[512,256]{1,0:T(8,128)(2,1)S(1)} %collective-permute-done.2.refs_0_.refs_5_), channel_id=1, source_target_pairs={{0,32},{8,40},{16,48},{24,56},{32,64},{40,72},{48,80},{56,88},{64,... | collective-permute-start | bytes 786440 | tf_op jit(solution)/shard_map/ppermute | solution.py:516
  37.9 2.1 collective-permute-start.9
  38.5 4.3 %collective-permute-start.10 = (bf16[1536,256]{1,0:T(8,128)(2,1)S(1)}, bf16[1536,256]{1,0:T(8,128)(2,1)S(1)}, u32[]{:S(2)}, u32[]{:S(2)}) collective-permute-start(bf16[1536,256]{1,0:T(8,128)(2,1)S(1)} %stack.5), channel_id=1, source_target_pairs={{0,8},{8,0},{16,24},{24,16},{32,40},{40,32},{48,56},{56,48},{64,72... | collective-permute-start | bytes 2359304 | tf_op jit(solution)/shard_map/ppermute | solution.py:516
  40.2 169.7 %copy-start.1 = (f32[768]{0:T(1024)S(1)}, f32[768]{0:T(1024)}, u32[]{:S(2)}) copy-start(f32[768]{0:T(1024)} %gain_ref.2) | copy-start | bytes 9220
  40.2 159.6 %collective-permute-start.11 = (f32[776,128]{1,0:T(8,128)S(1)}, f32[776,128]{1,0:T(8,128)S(1)}, u32[]{:S(2)}, u32[]{:S(2)}) collective-permute-start(f32[776,128]{1,0:T(8,128)S(1)} %get-tuple-element.72), channel_id=1, source_target_pairs={{0,32},{16,48},{32,64},{48,80},{64,96},{80,112},{8,104},{24,120},{... | collective-permute-start | bytes 1191944 | tf_op jit(solution)/shard_map/ppermute | solution.py:516
  41.5 158.3 %collective-permute-start.12 = (f32[776,128]{1,0:T(8,128)S(1)}, f32[776,128]{1,0:T(8,128)S(1)}, u32[]{:S(2)}, u32[]{:S(2)}) collective-permute-start(f32[776,128]{1,0:T(8,128)S(1)} %get-tuple-element.72), channel_id=1, source_target_pairs={{8,72},{24,88},{40,104},{56,120},{9,73},{25,89},{41,105},{57,121},... | collective-permute-start | bytes 1191944 | tf_op jit(solution)/shard_map/ppermute | solution.py:516
  199.9 10.0 %collective-permute-start.20 = (f32[776,128]{1,0:T(8,128)S(1)}, f32[776,128]{1,0:T(8,128)S(1)}, u32[]{:S(2)}, u32[]{:S(2)}) collective-permute-start(f32[776,128]{1,0:T(8,128)S(1)} %hand.1.kept_ref), channel_id=1, source_target_pairs={{0,8},{8,0},{16,24},{24,16},{32,40},{40,32},{48,56},{56,48},{64,72... | collective-permute-start | bytes 1191944 | tf_op jit(solution)/shard_map/ppermute | solution.py:516
  200.0 5.7 %collective-permute-start.13 = (f32[8,512]{1,0:T(8,128)S(1)}, f32[8,512]{1,0:T(8,128)S(1)}, u32[]{:S(2)}, u32[]{:S(2)}) collective-permute-start(f32[8,512]{1,0:T(8,128)S(1)} %get-tuple-element.81.refs_0_), channel_id=1, source_target_pairs={{0,1},{1,0},{2,3},{3,2},{4,5},{5,4},{6,7},{7,6},{8,9},{9,8},{10,11... | collective-permute-start | bytes 49160 | tf_op jit(solution)/shard_map/ppermute | solution.py:628
  201.8 5.3 %collective-permute-start.14 = (f32[8,512]{1,0:T(8,128)S(1)}, f32[8,512]{1,0:T(8,128)S(1)}, u32[]{:S(2)}, u32[]{:S(2)}) collective-permute-start(f32[8,512]{1,0:T(8,128)S(1)} %get-tuple-element.81.refs_0_), channel_id=1, source_target_pairs={{0,2},{1,3},{2,0},{3,1},{4,6},{5,7},{6,4},{7,5},{8,10},{9,11},{10,... | collective-permute-start | bytes 49160 | tf_op jit(solution)/shard_map/ppermute | solution.py:628
  203.1 9.3 %collective-permute-start.15 = (f32[8,512]{1,0:T(8,128)S(1)}, f32[8,512]{1,0:T(8,128)S(1)}, u32[]{:S(2)}, u32[]{:S(2)}) collective-permute-start(f32[8,512]{1,0:T(8,128)S(1)} %get-tuple-element.81.refs_0_), channel_id=1, source_target_pairs={{0,3},{1,2},{2,1},{3,0},{4,7},{5,6},{6,5},{7,4},{8,11},{9,10},{10,... | collective-permute-start | bytes 49160 | tf_op jit(solution)/shard_map/ppermute | solution.py:628
  203.1 9.3 %collective-permute-start.16 = (f32[8,512]{1,0:T(8,128)S(1)}, f32[8,512]{1,0:T(8,128)S(1)}, u32[]{:S(2)}, u32[]{:S(2)}) collective-permute-start(f32[8,512]{1,0:T(8,128)S(1)} %get-tuple-element.81.refs_0_), channel_id=1, source_target_pairs={{0,4},{1,5},{2,6},{3,7},{4,0},{5,1},{6,2},{7,3},{8,12},{9,13},{10,... | collective-permute-start | bytes 49160 | tf_op jit(solution)/shard_map/ppermute | solution.py:628
  205.7 6.7 %collective-permute-start.17 = (f32[8,512]{1,0:T(8,128)S(1)}, f32[8,512]{1,0:T(8,128)S(1)}, u32[]{:S(2)}, u32[]{:S(2)}) collective-permute-start(f32[8,512]{1,0:T(8,128)S(1)} %get-tuple-element.81.refs_0_), channel_id=1, source_target_pairs={{0,5},{1,4},{2,7},{3,6},{4,1},{5,0},{6,3},{7,2},{8,13},{9,12},{10,... | collective-permute-start | bytes 49160 | tf_op jit(solution)/shard_map/ppermute | solution.py:628
  207.2 5.2 %collective-permute-start.18 = (f32[8,512]{1,0:T(8,128)S(1)}, f32[8,512]{1,0:T(8,128)S(1)}, u32[]{:S(2)}, u32[]{:S(2)}) collective-permute-start(f32[8,512]{1,0:T(8,128)S(1)} %get-tuple-element.81.refs_0_), channel_id=1, source_target_pairs={{0,6},{1,7},{2,4},{3,5},{4,2},{5,3},{6,0},{7,1},{8,14},{9,15},{10,... | collective-permute-start | bytes 49160 | tf_op jit(solution)/shard_map/ppermute | solution.py:628
  209.9 4.7 %collective-permute-start.19 = (f32[8,512]{1,0:T(8,128)S(1)}, f32[8,512]{1,0:T(8,128)S(1)}, u32[]{:S(2)}, u32[]{:S(2)}) collective-permute-start(f32[8,512]{1,0:T(8,128)S(1)} %get-tuple-element.81.refs_0_), channel_id=1, source_target_pairs={{0,7},{1,6},{2,5},{3,4},{4,3},{5,2},{6,1},{7,0},{8,15},{9,14},{10,... | collective-permute-start | bytes 49160 | tf_op jit(solution)/shard_map/ppermute | solution.py:628
  209.9 4.7 %copy-start = (f32[768]{0:T(1024)S(1)}, f32[768]{0:T(1024)}, u32[]{:S(2)}) copy-start(f32[768]{0:T(1024)} %gain_ref.3) | copy-start | bytes 9220

commit v10 on v8

--- a/solution.py
+++ b/solution.py
@@ -624,7 +624,7 @@
         return lax.ppermute(value, "tp", [(i, i ^ bit) for i in range(8)])
 
     squares, state_behind, state_beyond = tied(squares, state_behind, state_beyond)
-    others = [over(squares, bit) for bit in (2, 4, 6)]
+    others = [over(squares, bit) for bit in (4, 2, 6)]
     kept = hand(place, state_behind, state_beyond)
     handed = move(kept, sibling)
     linear = carry_in(place, lh_query, local, grow, kept, handed, other_chip, first, lh_gain)

time: 215 us -> 215 us (level)
  Pallas kernels: 44.8 us -> 185 us
  starting transfers between devices: 157 us -> 17.3 us
    pallas_call x3, Pallas kernels: 34.3 us -> 175 us  [attend(): pl.pallas_call(functools.partial(attend_kernel, first, last, numbers_of,...]
    ppermute x14, starting transfers between devices: 143 us -> 11.8 us  [move(): return lax.ppermute(value, 'ctx', pairs)]
    ppermute x4, starting transfers between devices: 13.8 us -> 5.5 us  [over(): return lax.ppermute(value, 'tp', [(i, i ^ bit) for i in range(8)])]
  transfers between devices with their start and end apart: 18 -> 18, of which waited for: 6 -> 6; matrix products, arithmetic and copies ran while one was open for 0% -> 0% of each run, Pallas kernels for 20% -> 86%
where the time goes in v10:
time: 215 us; the launch traced here: 212 us
  Pallas kernels  185 us (86%)
  starting transfers between devices  17.3 us (8%)
  waiting for transfers between devices  8.82 us (4%)
    pallas_call x3, Pallas kernels, attend(): pl.pallas_call(functools.partial(attend_kernel, first, last, numbers_of,...  175 us
    ppermute x14, starting transfers between devices, move(): return lax.ppermute(value, 'ctx', pairs)  11.8 us
    ppermute x14, waiting for transfers between devices, move(): return lax.ppermute(value, 'ctx', pairs)  6.77 us
    ppermute x4, starting transfers between devices, over(): return lax.ppermute(value, 'tp', [(i, i ^ bit) for i in range(8)])  5.5 us
    pallas_call x1, Pallas kernels, recur(): pl.pallas_call(recur_kernel, out_shape=(jax.ShapeDtypeStruct((ROWS, HEADS...  5.04 us
  transfers between devices with their start and end apart: 18, of which 6 were waited for; matrix products, arithmetic and copies ran while one was open for 0% of the time, Pallas kernels for 86%

profile of v10, /device:TPU:101, one launch (start us, length us, event | category | flops | bytes accessed | tf_op | source)
XLA Modules:
  0.0 211.6 jit_solution(8215216599573503129)
XLA Ops:
  0.0 1.0 beside.1.own_ref.refs_0_
  1.0 0.8 collective-permute-start
  1.8 1.2 collective-permute-done.refs_0_.refs_1_.refs_11_
  3.0 1.3 collective-permute-start.3
  4.3 1.3 collective-permute-start.1
  5.6 1.3 collective-permute-start.2
  6.9 5.0 %recur.1 = (f32[512,768]{1,0:T(8,128)S(1)}, f32[512,128]{1,0:T(8,128)S(1)}, f32[776,128]{1,0:T(8,128)S(1)}) custom-call(bf16[512,768]{1,0:T(8,128)(2,1)} %query_hbm.1, bf16[512,768]{1,0:T(8,128)(2,1)} %k_hbm.1, bf16[512,768]{1,0:T(8,128)(2,1)} %v_hbm.1, f32[6,512]{1,0:T(8,128)} %bitcast.2), custom_call_target="tpu_custom_call" | custom-call | flops 200000000 | bytes 200000 | tf_op jit(solution)/shard_map/recur/pallas_call | solution.py:91
  11.9 5.3 %attend_first.1 = (bf16[512,768]{1,0:T(8,128)(2,1)S(1)}, f32[512,768]{1,0:T(8,128)S(1)}, f32[512,128]{1,0:T(8,128)S(1)}, bf16[32,128]{1,0:T(8,128)(2,1)S(1)}) custom-call(s32[1]{0:T(128)} %bitcast.mine_ref, bf16[512,768]{1,0:T(8,128)(2,1)} %query_ref.1, bf16[512,256]{1,0:T(8,128)(2,1)S(1)} %beside.1.own_ref.refs_0_, ...), custom_call_target="tpu_custom_call" | custom-call | flops 200000000 | bytes 200000 | tf_op jit(solution)/shard_map/attend_first/pallas_call | solution.py:418
  17.2 3.0 %collective-permute-done.1.refs_1_.refs_5_.refs_14_ = bf16[512,256]{1,0:T(8,128)(2,1)S(1)} collective-permute-done((bf16[512,256]{1,0:T(8,128)(2,1)S(1)}, bf16[512,256]{1,0:T(8,128)(2,1)S(1)}, u32[]{:S(2)}, u32[]{:S(2)}) %collective-permute-start.1) | collective-permute-done | bytes 262176 | tf_op jit(solution)/shard_map/ppermute | solution.py:512
  20.2 0.0 collective-permute-done.2.refs_0_.refs_5_
  20.2 0.5 collective-permute-start.7
  20.7 0.0 collective-permute-done.3.refs_0_.refs_3_.blocks_ref.refs_12_
  20.7 0.1 stack.4
  20.8 0.1 collective-permute-start.4
  20.9 1.2 collective-permute-done.7.other_ref.core_ref
  22.1 0.1 join_cores.1
  22.2 0.6 collective-permute-start.8
  22.8 1.3 collective-permute-start.5
  24.1 1.3 collective-permute-start.6
  25.4 0.0 collective-permute-done.4.refs_4_.refs_6_.refs_13_.refs_15_
  25.4 12.5 %attend_middle.1 = (f32[512,768]{1,0:T(8,128)S(1)}, f32[512,128]{1,0:T(8,128)S(1)}, bf16[32,128]{1,0:T(8,128)(2,1)S(1)}) custom-call(s32[1]{0:T(128)} %bitcast.mine_ref, bf16[512,768]{1,0:T(8,128)(2,1)S(1)} %get-tuple-element.46.query_ref, bf16[512,256]{1,0:T(8,128)(2,1)S(1)} %beside.1.own_ref.refs_0_, f32[512,768]{1,0:T(8,128)S(1)} %get-tuple-element.52.refs_0_, ...), custom_call_target="tpu_custom_call" | custom-call | flops 200000000 | bytes 200000 | tf_op jit(solution)/shard_map/attend_middle/pallas_call | solution.py:418
  37.9 0.0 collective-permute-done.5.refs_1_.refs_7_
  37.9 0.0 collective-permute-done.6.refs_2_.refs_9_
  37.9 0.0 collective-permute-done.8.level_ref.refs_3_
  37.9 0.5 collective-permute-start.9
  38.5 0.1 stack.5
  38.5 0.1 collective-permute-start.10
  38.7 1.4 collective-permute-done.9.level_near_ref.refs_4_
  40.0 0.2 join_sides.1
  40.2 0.0 copy-start.1
  40.2 1.3 collective-permute-start.11
  41.5 1.3 collective-permute-start.12
  42.8 0.0 collective-permute-done.10.refs_6_.refs_8_.refs_10_
  42.8 157.0 %attend_last.1 = (bf16[512,768]{1,0:T(8,128)(2,1)S(1)}, f32[8,512]{1,0:T(8,128)S(1)}) custom-call(s32[1]{0:T(128)} %bitcast.mine_ref, bf16[512,768]{1,0:T(8,128)(2,1)S(1)} %get-tuple-element.46.query_ref, bf16[512,256]{1,0:T(8,128)(2,1)S(1)} %beside.1.own_ref.refs_0_, f32[512,768]{1,0:T(8,128)S(1)} %get-tuple-element.69.refs_0_, ...), custom_call_target="tpu_custom_call" | custom-call | flops 200000000 | bytes 200000 | tf_op jit(solution)/shard_map/attend_last/pallas_call | solution.py:418
  199.8 0.0 collective-permute-done.11.behind_ref
  199.8 0.0 collective-permute-done.12.beyond_ref
  199.8 0.1 hand.1.kept_ref
  199.9 0.1 collective-permute-start.16
  200.0 0.1 collective-permute-start.13
  200.1 3.3 %collective-permute-start.14 = (f32[8,512]{1,0:T(8,128)S(1)}, f32[8,512]{1,0:T(8,128)S(1)}, u32[]{:S(2)}, u32[]{:S(2)}) collective-permute-start(f32[8,512]{1,0:T(8,128)S(1)} %get-tuple-element.77), channel_id=1, source_target_pairs={{0,2},{1,3},{2,0},{3,1},{4,6},{5,7},{6,4},{7,5},{8,10},{9,11},{10,... | collective-permute-start | bytes 49160 | tf_op jit(solution)/shard_map/ppermute | solution.py:624
  203.4 0.4 collective-permute-start.15
  203.8 0.0 collective-permute-done.16.handed_ref
  203.8 0.0 copy-done.1
  203.8 0.0 copy-start
  203.8 2.5 %carry.1.linear_ref = f32[512,768]{1,0:T(8,128)S(1)} custom-call(s32[1]{0:T(128)} %bitcast.mine_ref, bf16[512,768]{1,0:T(8,128)(2,1)} %query_hbm.1, f32[512,768]{1,0:T(8,128)S(1)} %get-tuple-element.78.local_ref, f32[512,128]{1,0:T(8,128)S(1)} %get-tuple-element.79.grow_ref, f32[776,128]{1,0:T(8,128)S(1)} %hand.1.kept_ref, ...), custom_call_target="tpu_custom_call" | custom-call | flops 200000000 | bytes 200000 | tf_op jit(solution)/shard_map/carry/pallas_call | solution.py:484
  206.2 0.0 collective-permute-done.13
  206.3 0.0 collective-permute-done.14
  206.3 0.9 collective-permute-done.15
  207.2 1.7 collective-permute-start.17
  208.9 1.1 collective-permute-done.17.other_ref
  210.1 0.0 copy-done
  210.1 1.5 finish.1
  (2 shorter events, 0.0 us)
Async XLA Ops:
  1.0 1.9 collective-permute-start
  3.0 17.7 %collective-permute-start.3 = (bf16[1024,256]{1,0:T(8,128)(2,1)S(1)}, bf16[1024,256]{1,0:T(8,128)(2,1)S(1)}, u32[]{:S(2)}, u32[]{:S(2)}) collective-permute-start(bf16[1024,256]{1,0:T(8,128)(2,1)S(1)} %stack.3), channel_id=1, source_target_pairs={{0,32},{16,48},{32,64},{48,80},{64,96},{80,112},{8,72},{24,88},{40... | collective-permute-start | bytes 1572872 | tf_op jit(solution)/shard_map/ppermute | solution.py:512
  4.3 16.0 %collective-permute-start.1 = (bf16[512,256]{1,0:T(8,128)(2,1)S(1)}, bf16[512,256]{1,0:T(8,128)(2,1)S(1)}, u32[]{:S(2)}, u32[]{:S(2)}) collective-permute-start(bf16[512,256]{1,0:T(8,128)(2,1)S(1)} %beside.1.own_ref.refs_0_), channel_id=1, source_target_pairs={{0,96},{8,104},{16,112},{24,120},{1,97},{9,105},{17,113},{25,121},... | collective-permute-start | bytes 786440 | tf_op jit(solution)/shard_map/ppermute | solution.py:512
  5.6 14.7 %collective-permute-start.2 = (bf16[512,256]{1,0:T(8,128)(2,1)S(1)}, bf16[512,256]{1,0:T(8,128)(2,1)S(1)}, u32[]{:S(2)}, u32[]{:S(2)}) collective-permute-start(bf16[512,256]{1,0:T(8,128)(2,1)S(1)} %beside.1.own_ref.refs_0_), channel_id=1, source_target_pairs={{0,16},{8,24},{16,0},{24,8},{32,48},{40,56},{48,32},{56,40},{64,80... | collective-permute-start | bytes 786440 | tf_op jit(solution)/shard_map/ppermute | solution.py:512
  20.2 1.8 collective-permute-start.7
  20.8 4.6 %collective-permute-start.4 = (bf16[1536,256]{1,0:T(8,128)(2,1)S(1)}, bf16[1536,256]{1,0:T(8,128)(2,1)S(1)}, u32[]{:S(2)}, u32[]{:S(2)}) collective-permute-start(bf16[1536,256]{1,0:T(8,128)(2,1)S(1)} %stack.4), channel_id=1, source_target_pairs={{0,8},{8,0},{16,24},{24,16},{32,40},{40,32},{48,56},{56,48},{64,72... | collective-permute-start | bytes 2359304 | tf_op jit(solution)/shard_map/ppermute | solution.py:512
  22.2 15.7 %collective-permute-start.8 = (bf16[1024,256]{1,0:T(8,128)(2,1)S(1)}, bf16[1024,256]{1,0:T(8,128)(2,1)S(1)}, u32[]{:S(2)}, u32[]{:S(2)}) collective-permute-start(bf16[1024,256]{1,0:T(8,128)(2,1)S(1)} %get-tuple-element.62), channel_id=1, source_target_pairs={{0,16},{8,24},{16,0},{24,8},{32,48},{40,56},{48,32},{56,40},{64,80... | collective-permute-start | bytes 1572872 | tf_op jit(solution)/shard_map/ppermute | solution.py:512
  22.8 15.1 %collective-permute-start.5 = (bf16[512,256]{1,0:T(8,128)(2,1)S(1)}, bf16[512,256]{1,0:T(8,128)(2,1)S(1)}, u32[]{:S(2)}, u32[]{:S(2)}) collective-permute-start(bf16[512,256]{1,0:T(8,128)(2,1)S(1)} %collective-permute-done.2.refs_0_.refs_5_), channel_id=1, source_target_pairs={{0,96},{8,104},{16,112},{24,120},{1,97},{9,105},{17,113},{25,121},... | collective-permute-start | bytes 786440 | tf_op jit(solution)/shard_map/ppermute | solution.py:512
  24.1 13.8 %collective-permute-start.6 = (bf16[512,256]{1,0:T(8,128)(2,1)S(1)}, bf16[512,256]{1,0:T(8,128)(2,1)S(1)}, u32[]{:S(2)}, u32[]{:S(2)}) collective-permute-start(bf16[512,256]{1,0:T(8,128)(2,1)S(1)} %collective-permute-done.2.refs_0_.refs_5_), channel_id=1, source_target_pairs={{0,32},{8,40},{16,48},{24,56},{32,64},{40,72},{48,80},{56,88},{64,... | collective-permute-start | bytes 786440 | tf_op jit(solution)/shard_map/ppermute | solution.py:512
  37.9 2.1 collective-permute-start.9
  38.5 4.3 %collective-permute-start.10 = (bf16[1536,256]{1,0:T(8,128)(2,1)S(1)}, bf16[1536,256]{1,0:T(8,128)(2,1)S(1)}, u32[]{:S(2)}, u32[]{:S(2)}) collective-permute-start(bf16[1536,256]{1,0:T(8,128)(2,1)S(1)} %stack.5), channel_id=1, source_target_pairs={{0,8},{8,0},{16,24},{24,16},{32,40},{40,32},{48,56},{56,48},{64,72... | collective-permute-start | bytes 2359304 | tf_op jit(solution)/shard_map/ppermute | solution.py:512
  40.2 163.6 %copy-start.1 = (f32[768]{0:T(1024)S(1)}, f32[768]{0:T(1024)}, u32[]{:S(2)}) copy-start(f32[768]{0:T(1024)} %gain_ref.2) | copy-start | bytes 9220
  40.2 159.6 %collective-permute-start.11 = (f32[776,128]{1,0:T(8,128)S(1)}, f32[776,128]{1,0:T(8,128)S(1)}, u32[]{:S(2)}, u32[]{:S(2)}) collective-permute-start(f32[776,128]{1,0:T(8,128)S(1)} %get-tuple-element.68), channel_id=1, source_target_pairs={{0,32},{16,48},{32,64},{48,80},{64,96},{80,112},{8,104},{24,120},{... | collective-permute-start | bytes 1191944 | tf_op jit(solution)/shard_map/ppermute | solution.py:512
  41.5 158.3 %collective-permute-start.12 = (f32[776,128]{1,0:T(8,128)S(1)}, f32[776,128]{1,0:T(8,128)S(1)}, u32[]{:S(2)}, u32[]{:S(2)}) collective-permute-start(f32[776,128]{1,0:T(8,128)S(1)} %get-tuple-element.68), channel_id=1, source_target_pairs={{8,72},{24,88},{40,104},{56,120},{9,73},{25,89},{41,105},{57,121},... | collective-permute-start | bytes 1191944 | tf_op jit(solution)/shard_map/ppermute | solution.py:512
  199.9 3.9 %collective-permute-start.16 = (f32[776,128]{1,0:T(8,128)S(1)}, f32[776,128]{1,0:T(8,128)S(1)}, u32[]{:S(2)}, u32[]{:S(2)}) collective-permute-start(f32[776,128]{1,0:T(8,128)S(1)} %hand.1.kept_ref), channel_id=1, source_target_pairs={{0,8},{8,0},{16,24},{24,16},{32,40},{40,32},{48,56},{56,48},{64,72... | collective-permute-start | bytes 1191944 | tf_op jit(solution)/shard_map/ppermute | solution.py:512
  200.0 6.3 %collective-permute-start.13 = (f32[8,512]{1,0:T(8,128)S(1)}, f32[8,512]{1,0:T(8,128)S(1)}, u32[]{:S(2)}, u32[]{:S(2)}) collective-permute-start(f32[8,512]{1,0:T(8,128)S(1)} %get-tuple-element.77), channel_id=1, source_target_pairs={{0,4},{1,5},{2,6},{3,7},{4,0},{5,1},{6,2},{7,3},{8,12},{9,13},{10,... | collective-permute-start | bytes 49160 | tf_op jit(solution)/shard_map/ppermute | solution.py:624
  200.1 6.2 %collective-permute-start.14 = (f32[8,512]{1,0:T(8,128)S(1)}, f32[8,512]{1,0:T(8,128)S(1)}, u32[]{:S(2)}, u32[]{:S(2)}) collective-permute-start(f32[8,512]{1,0:T(8,128)S(1)} %get-tuple-element.77), channel_id=1, source_target_pairs={{0,2},{1,3},{2,0},{3,1},{4,6},{5,7},{6,4},{7,5},{8,10},{9,11},{10,... | collective-permute-start | bytes 49160 | tf_op jit(solution)/shard_map/ppermute | solution.py:624
  203.4 3.8 %collective-permute-start.15 = (f32[8,512]{1,0:T(8,128)S(1)}, f32[8,512]{1,0:T(8,128)S(1)}, u32[]{:S(2)}, u32[]{:S(2)}) collective-permute-start(f32[8,512]{1,0:T(8,128)S(1)} %get-tuple-element.77), channel_id=1, source_target_pairs={{0,6},{1,7},{2,4},{3,5},{4,2},{5,3},{6,0},{7,1},{8,14},{9,15},{10,... | collective-permute-start | bytes 49160 | tf_op jit(solution)/shard_map/ppermute | solution.py:624
  203.8 6.3 %copy-start = (f32[768]{0:T(1024)S(1)}, f32[768]{0:T(1024)}, u32[]{:S(2)}) copy-start(f32[768]{0:T(1024)} %gain_ref.3) | copy-start | bytes 9220
  207.2 2.9 %collective-permute-start.17 = (f32[8,512]{1,0:T(8,128)S(1)}, f32[8,512]{1,0:T(8,128)S(1)}, u32[]{:S(2)}, u32[]{:S(2)}) collective-permute-start(f32[8,512]{1,0:T(8,128)S(1)} %add_add_fusion.square_ref), channel_id=1, source_target_pairs={{0,1},{1,0},{2,3},{3,2},{4,5},{5,4},{6,7},{7,6},{8,9},{9,8},{10,11... | collective-permute-start | bytes 49160 | tf_op jit(solution)/shard_map/ppermute | solution.py:624

commit v11 on v10

--- a/solution.py
+++ b/solution.py
@@ -387,7 +387,7 @@
             out_ref[:, head(h)] = result
             result = result.astype(f32)
             squares = squares + result * result
-        square_ref[...] = dot(jnp.ones((8, HD), f32), squares, ((1,), (1,)), highest)
+        square_ref[...] = dot(jnp.ones((8, HD), f32), squares, ((1,), (1,)), highest)[:1, :]
 
 
 def attend(mine, query, own, carry, blocks, numbers_of, kept=None, kept_numbers_of=None):
@@ -404,7 +404,7 @@
     if last:
         out_shape = (
             jax.ShapeDtypeStruct((ROWS, HEADS * HD), bf16),
-            jax.ShapeDtypeStruct((8, ROWS), f32),
+            jax.ShapeDtypeStruct((1, ROWS), f32),
         )
         scratch += [pltpu.VMEM(top, bf16), pltpu.VMEM((HEADS, ROWS, HD), f32)]
     else:
@@ -474,6 +474,7 @@
 
 def finish_kernel(features, attention_ref, square_ref, other_ref, linear_ref, gain_ref, out_ref):
     factor = lax.rsqrt((square_ref[...] + other_ref[...]) / features + EPS)
+    factor = jnp.broadcast_to(factor, (8, ROWS))
     factor = dot(factor, jnp.full((8, HD), 0.125, f32), ((0,), (0,)), highest)
     for h in range(HEADS):
         part = attention_ref[:, head(h)].astype(f32) * factor * gain_ref[head(h)][None, :]

time: 215 us -> 215 us (level)
  starting transfers between devices: 17.3 us -> 158 us
  Pallas kernels: 185 us -> 44.9 us
    pallas_call x3, Pallas kernels: 175 us -> 34.3 us  [attend(): pl.pallas_call(functools.partial(attend_kernel, first, last, numbers_of,...]
    ppermute x14, starting transfers between devices: 11.8 us -> 143 us  [move(): return lax.ppermute(value, 'ctx', pairs)]
    ppermute x4, starting transfers between devices: 5.5 us -> 14.5 us  [over(): return lax.ppermute(value, 'tp', [(i, i ^ bit) for i in range(8)])]
  transfers between devices with their start and end apart: 18 -> 18, of which waited for: 6 -> 6; matrix products, arithmetic and copies ran while one was open for 0% -> 0% of each run, Pallas kernels for 86% -> 20%
where the time goes in v11:
time: 215 us; the launch traced here: 211 us
  starting transfers between devices  158 us (73%)
  Pallas kernels  44.9 us (21%)
  waiting for transfers between devices  8.5 us (4%)
    ppermute x14, starting transfers between devices, move(): return lax.ppermute(value, 'ctx', pairs)  143 us
    pallas_call x3, Pallas kernels, attend(): pl.pallas_call(functools.partial(attend_kernel, first, last, numbers_of,...  34.3 us
    ppermute x4, starting transfers between devices, over(): return lax.ppermute(value, 'tp', [(i, i ^ bit) for i in range(8)])  14.5 us
    ppermute x14, waiting for transfers between devices, move(): return lax.ppermute(value, 'ctx', pairs)  6.79 us
    pallas_call x1, Pallas kernels, recur(): pl.pallas_call(recur_kernel, out_shape=(jax.ShapeDtypeStruct((ROWS, HEADS...  5.04 us
  transfers between devices with their start and end apart: 18, of which 6 were waited for; matrix products, arithmetic and copies ran while one was open for 0% of the time, Pallas kernels for 20%

profile of v11, /device:TPU:101, one launch (start us, length us, event | category | flops | bytes accessed | tf_op | source)
XLA Modules:
  0.0 211.3 jit_solution(306775643850318099)
XLA Ops:
  0.0 1.0 beside.1.own_ref.refs_0_
  1.0 0.8 collective-permute-start
  1.8 1.2 collective-permute-done.refs_0_.refs_1_.refs_11_
  3.0 1.3 collective-permute-start.3
  4.3 1.3 collective-permute-start.1
  5.6 1.3 collective-permute-start.2
  6.9 5.0 %recur.1 = (f32[512,768]{1,0:T(8,128)S(1)}, f32[512,128]{1,0:T(8,128)S(1)}, f32[776,128]{1,0:T(8,128)S(1)}) custom-call(bf16[512,768]{1,0:T(8,128)(2,1)} %query_hbm.1, bf16[512,768]{1,0:T(8,128)(2,1)} %k_hbm.1, bf16[512,768]{1,0:T(8,128)(2,1)} %v_hbm.1, f32[6,512]{1,0:T(8,128)} %bitcast.2), custom_call_target="tpu_custom_call" | custom-call | flops 200000000 | bytes 200000 | tf_op jit(solution)/shard_map/recur/pallas_call | solution.py:91
  11.9 5.3 %attend_first.1 = (bf16[512,768]{1,0:T(8,128)(2,1)S(1)}, f32[512,768]{1,0:T(8,128)S(1)}, f32[512,128]{1,0:T(8,128)S(1)}, bf16[32,128]{1,0:T(8,128)(2,1)S(1)}) custom-call(s32[1]{0:T(128)} %bitcast.mine_ref, bf16[512,768]{1,0:T(8,128)(2,1)} %query_ref.1, bf16[512,256]{1,0:T(8,128)(2,1)S(1)} %beside.1.own_ref.refs_0_, ...), custom_call_target="tpu_custom_call" | custom-call | flops 200000000 | bytes 200000 | tf_op jit(solution)/shard_map/attend_first/pallas_call | solution.py:418
  17.2 3.0 %collective-permute-done.1.refs_1_.refs_5_.refs_14_ = bf16[512,256]{1,0:T(8,128)(2,1)S(1)} collective-permute-done((bf16[512,256]{1,0:T(8,128)(2,1)S(1)}, bf16[512,256]{1,0:T(8,128)(2,1)S(1)}, u32[]{:S(2)}, u32[]{:S(2)}) %collective-permute-start.1) | collective-permute-done | bytes 262176 | tf_op jit(solution)/shard_map/ppermute | solution.py:513
  20.2 0.0 collective-permute-done.2.refs_0_.refs_5_
  20.2 0.5 collective-permute-start.7
  20.7 0.0 collective-permute-done.3.refs_0_.refs_3_.blocks_ref.refs_12_
  20.7 0.1 stack.4
  20.8 0.1 collective-permute-start.4
  20.9 1.2 collective-permute-done.7.other_ref.core_ref
  22.1 0.1 join_cores.1
  22.2 0.6 collective-permute-start.8
  22.8 1.3 collective-permute-start.5
  24.1 1.3 collective-permute-start.6
  25.4 0.0 collective-permute-done.4.refs_4_.refs_6_.refs_13_.refs_15_
  25.4 12.5 %attend_middle.1 = (f32[512,768]{1,0:T(8,128)S(1)}, f32[512,128]{1,0:T(8,128)S(1)}, bf16[32,128]{1,0:T(8,128)(2,1)S(1)}) custom-call(s32[1]{0:T(128)} %bitcast.mine_ref, bf16[512,768]{1,0:T(8,128)(2,1)S(1)} %get-tuple-element.46.query_ref, bf16[512,256]{1,0:T(8,128)(2,1)S(1)} %beside.1.own_ref.refs_0_, f32[512,768]{1,0:T(8,128)S(1)} %get-tuple-element.52.refs_0_, ...), custom_call_target="tpu_custom_call" | custom-call | flops 200000000 | bytes 200000 | tf_op jit(solution)/shard_map/attend_middle/pallas_call | solution.py:418
  37.9 0.0 collective-permute-done.5.refs_1_.refs_7_
  37.9 0.0 collective-permute-done.6.refs_2_.refs_9_
  37.9 0.0 collective-permute-done.8.level_ref.refs_3_
  37.9 0.5 collective-permute-start.9
  38.5 0.1 stack.5
  38.5 0.1 collective-permute-start.10
  38.7 1.4 collective-permute-done.9.level_near_ref.refs_4_
  40.0 0.2 join_sides.1
  40.2 0.0 copy-start.1
  40.2 1.3 collective-permute-start.11
  41.5 1.3 collective-permute-start.12
  42.8 0.0 collective-permute-done.10.refs_6_.refs_8_.refs_10_
  42.8 16.6 %attend_last.1 = (bf16[512,768]{1,0:T(8,128)(2,1)S(1)}, f32[1,512]{1,0:T(1,128)S(1)}) custom-call(s32[1]{0:T(128)} %bitcast.mine_ref, bf16[512,768]{1,0:T(8,128)(2,1)S(1)} %get-tuple-element.46.query_ref, bf16[512,256]{1,0:T(8,128)(2,1)S(1)} %beside.1.own_ref.refs_0_, f32[512,768]{1,0:T(8,128)S(1)} %get-tuple-element.69.refs_0_, ...), custom_call_target="tpu_custom_call" | custom-call | flops 200000000 | bytes 200000 | tf_op jit(solution)/shard_map/attend_last/pallas_call | solution.py:418
  59.4 0.0 collective-permute-done.11.behind_ref
  59.4 0.0 collective-permute-done.12.beyond_ref
  59.4 0.1 hand.1.kept_ref
  59.5 131.5 %collective-permute-start.16 = (f32[776,128]{1,0:T(8,128)S(1)}, f32[776,128]{1,0:T(8,128)S(1)}, u32[]{:S(2)}, u32[]{:S(2)}) collective-permute-start(f32[776,128]{1,0:T(8,128)S(1)} %hand.1.kept_ref), channel_id=1, source_target_pairs={{0,8},{8,0},{16,24},{24,16},{32,40},{40,32},{48,56},{56,48},{64,72... | collective-permute-start | bytes 1191944 | tf_op jit(solution)/shard_map/ppermute | solution.py:513
  191.0 12.0 %collective-permute-start.13 = (f32[1,512]{1,0:T(1,128)S(1)}, f32[1,512]{1,0:T(1,128)S(1)}, u32[]{:S(2)}, u32[]{:S(2)}) collective-permute-start(f32[1,512]{1,0:T(1,128)S(1)} %get-tuple-element.77), channel_id=1, source_target_pairs={{0,4},{1,5},{2,6},{3,7},{4,0},{5,1},{6,2},{7,3},{8,12},{9,13},{10,... | collective-permute-start | bytes 6152 | tf_op jit(solution)/shard_map/ppermute | solution.py:625
  203.0 0.4 collective-permute-start.14
  203.4 0.4 collective-permute-start.15
  203.8 0.0 collective-permute-done.16.handed_ref
  203.8 0.0 copy-done.1
  203.8 0.0 copy-start
  203.8 2.5 %carry.1.linear_ref = f32[512,768]{1,0:T(8,128)S(1)} custom-call(s32[1]{0:T(128)} %bitcast.mine_ref, bf16[512,768]{1,0:T(8,128)(2,1)} %query_hbm.1, f32[512,768]{1,0:T(8,128)S(1)} %get-tuple-element.78.local_ref, f32[512,128]{1,0:T(8,128)S(1)} %get-tuple-element.79.grow_ref, f32[776,128]{1,0:T(8,128)S(1)} %hand.1.kept_ref, ...), custom_call_target="tpu_custom_call" | custom-call | flops 200000000 | bytes 200000 | tf_op jit(solution)/shard_map/carry/pallas_call | solution.py:485
  206.3 0.0 collective-permute-done.13
  206.3 0.0 collective-permute-done.14
  206.3 0.7 collective-permute-done.15
  207.0 1.7 collective-permute-start.17
  208.8 1.0 collective-permute-done.17.other_ref
  209.8 0.0 copy-done
  209.8 1.5 finish.1
  (2 shorter events, 0.0 us)
Async XLA Ops:
  1.0 1.9 collective-permute-start
  3.0 17.7 %collective-permute-start.3 = (bf16[1024,256]{1,0:T(8,128)(2,1)S(1)}, bf16[1024,256]{1,0:T(8,128)(2,1)S(1)}, u32[]{:S(2)}, u32[]{:S(2)}) collective-permute-start(bf16[1024,256]{1,0:T(8,128)(2,1)S(1)} %stack.3), channel_id=1, source_target_pairs={{0,32},{16,48},{32,64},{48,80},{64,96},{80,112},{8,72},{24,88},{40... | collective-permute-start | bytes 1572872 | tf_op jit(solution)/shard_map/ppermute | solution.py:513
  4.3 16.0 %collective-permute-start.1 = (bf16[512,256]{1,0:T(8,128)(2,1)S(1)}, bf16[512,256]{1,0:T(8,128)(2,1)S(1)}, u32[]{:S(2)}, u32[]{:S(2)}) collective-permute-start(bf16[512,256]{1,0:T(8,128)(2,1)S(1)} %beside.1.own_ref.refs_0_), channel_id=1, source_target_pairs={{0,96},{8,104},{16,112},{24,120},{1,97},{9,105},{17,113},{25,121},... | collective-permute-start | bytes 786440 | tf_op jit(solution)/shard_map/ppermute | solution.py:513
  5.6 14.7 %collective-permute-start.2 = (bf16[512,256]{1,0:T(8,128)(2,1)S(1)}, bf16[512,256]{1,0:T(8,128)(2,1)S(1)}, u32[]{:S(2)}, u32[]{:S(2)}) collective-permute-start(bf16[512,256]{1,0:T(8,128)(2,1)S(1)} %beside.1.own_ref.refs_0_), channel_id=1, source_target_pairs={{0,16},{8,24},{16,0},{24,8},{32,48},{40,56},{48,32},{56,40},{64,80... | collective-permute-start | bytes 786440 | tf_op jit(solution)/shard_map/ppermute | solution.py:513
  20.2 1.8 collective-permute-start.7
  20.8 4.6 %collective-permute-start.4 = (bf16[1536,256]{1,0:T(8,128)(2,1)S(1)}, bf16[1536,256]{1,0:T(8,128)(2,1)S(1)}, u32[]{:S(2)}, u32[]{:S(2)}) collective-permute-start(bf16[1536,256]{1,0:T(8,128)(2,1)S(1)} %stack.4), channel_id=1, source_target_pairs={{0,8},{8,0},{16,24},{24,16},{32,40},{40,32},{48,56},{56,48},{64,72... | collective-permute-start | bytes 2359304 | tf_op jit(solution)/shard_map/ppermute | solution.py:513
  22.2 15.7 %collective-permute-start.8 = (bf16[1024,256]{1,0:T(8,128)(2,1)S(1)}, bf16[1024,256]{1,0:T(8,128)(2,1)S(1)}, u32[]{:S(2)}, u32[]{:S(2)}) collective-permute-start(bf16[1024,256]{1,0:T(8,128)(2,1)S(1)} %get-tuple-element.62), channel_id=1, source_target_pairs={{0,16},{8,24},{16,0},{24,8},{32,48},{40,56},{48,32},{56,40},{64,80... | collective-permute-start | bytes 1572872 | tf_op jit(solution)/shard_map/ppermute | solution.py:513
  22.8 15.1 %collective-permute-start.5 = (bf16[512,256]{1,0:T(8,128)(2,1)S(1)}, bf16[512,256]{1,0:T(8,128)(2,1)S(1)}, u32[]{:S(2)}, u32[]{:S(2)}) collective-permute-start(bf16[512,256]{1,0:T(8,128)(2,1)S(1)} %collective-permute-done.2.refs_0_.refs_5_), channel_id=1, source_target_pairs={{0,96},{8,104},{16,112},{24,120},{1,97},{9,105},{17,113},{25,121},... | collective-permute-start | bytes 786440 | tf_op jit(solution)/shard_map/ppermute | solution.py:513
  24.1 13.8 %collective-permute-start.6 = (bf16[512,256]{1,0:T(8,128)(2,1)S(1)}, bf16[512,256]{1,0:T(8,128)(2,1)S(1)}, u32[]{:S(2)}, u32[]{:S(2)}) collective-permute-start(bf16[512,256]{1,0:T(8,128)(2,1)S(1)} %collective-permute-done.2.refs_0_.refs_5_), channel_id=1, source_target_pairs={{0,32},{8,40},{16,48},{24,56},{32,64},{40,72},{48,80},{56,88},{64,... | collective-permute-start | bytes 786440 | tf_op jit(solution)/shard_map/ppermute | solution.py:513
  37.9 2.1 collective-permute-start.9
  38.5 4.3 %collective-permute-start.10 = (bf16[1536,256]{1,0:T(8,128)(2,1)S(1)}, bf16[1536,256]{1,0:T(8,128)(2,1)S(1)}, u32[]{:S(2)}, u32[]{:S(2)}) collective-permute-start(bf16[1536,256]{1,0:T(8,128)(2,1)S(1)} %stack.5), channel_id=1, source_target_pairs={{0,8},{8,0},{16,24},{24,16},{32,40},{40,32},{48,56},{56,48},{64,72... | collective-permute-start | bytes 2359304 | tf_op jit(solution)/shard_map/ppermute | solution.py:513
  40.2 163.6 %copy-start.1 = (f32[768]{0:T(1024)S(1)}, f32[768]{0:T(1024)}, u32[]{:S(2)}) copy-start(f32[768]{0:T(1024)} %gain_ref.2) | copy-start | bytes 9220
  40.2 19.2 %collective-permute-start.11 = (f32[776,128]{1,0:T(8,128)S(1)}, f32[776,128]{1,0:T(8,128)S(1)}, u32[]{:S(2)}, u32[]{:S(2)}) collective-permute-start(f32[776,128]{1,0:T(8,128)S(1)} %get-tuple-element.68), channel_id=1, source_target_pairs={{0,32},{16,48},{32,64},{48,80},{64,96},{80,112},{8,104},{24,120},{... | collective-permute-start | bytes 1191944 | tf_op jit(solution)/shard_map/ppermute | solution.py:513
  41.5 17.9 %collective-permute-start.12 = (f32[776,128]{1,0:T(8,128)S(1)}, f32[776,128]{1,0:T(8,128)S(1)}, u32[]{:S(2)}, u32[]{:S(2)}) collective-permute-start(f32[776,128]{1,0:T(8,128)S(1)} %get-tuple-element.68), channel_id=1, source_target_pairs={{8,72},{24,88},{40,104},{56,120},{9,73},{25,89},{41,105},{57,121},... | collective-permute-start | bytes 1191944 | tf_op jit(solution)/shard_map/ppermute | solution.py:513
  59.5 144.3 %collective-permute-start.16 = (f32[776,128]{1,0:T(8,128)S(1)}, f32[776,128]{1,0:T(8,128)S(1)}, u32[]{:S(2)}, u32[]{:S(2)}) collective-permute-start(f32[776,128]{1,0:T(8,128)S(1)} %hand.1.kept_ref), channel_id=1, source_target_pairs={{0,8},{8,0},{16,24},{24,16},{32,40},{40,32},{48,56},{56,48},{64,72... | collective-permute-start | bytes 1191944 | tf_op jit(solution)/shard_map/ppermute | solution.py:513
  191.0 15.3 %collective-permute-start.13 = (f32[1,512]{1,0:T(1,128)S(1)}, f32[1,512]{1,0:T(1,128)S(1)}, u32[]{:S(2)}, u32[]{:S(2)}) collective-permute-start(f32[1,512]{1,0:T(1,128)S(1)} %get-tuple-element.77), channel_id=1, source_target_pairs={{0,4},{1,5},{2,6},{3,7},{4,0},{5,1},{6,2},{7,3},{8,12},{9,13},{10,... | collective-permute-start | bytes 6152 | tf_op jit(solution)/shard_map/ppermute | solution.py:625
  203.0 3.3 %collective-permute-start.14 = (f32[1,512]{1,0:T(1,128)S(1)}, f32[1,512]{1,0:T(1,128)S(1)}, u32[]{:S(2)}, u32[]{:S(2)}) collective-permute-start(f32[1,512]{1,0:T(1,128)S(1)} %get-tuple-element.77), channel_id=1, source_target_pairs={{0,2},{1,3},{2,0},{3,1},{4,6},{5,7},{6,4},{7,5},{8,10},{9,11},{10,... | collective-permute-start | bytes 6152 | tf_op jit(solution)/shard_map/ppermute | solution.py:625
  203.4 3.6 %collective-permute-start.15 = (f32[1,512]{1,0:T(1,128)S(1)}, f32[1,512]{1,0:T(1,128)S(1)}, u32[]{:S(2)}, u32[]{:S(2)}) collective-permute-start(f32[1,512]{1,0:T(1,128)S(1)} %get-tuple-element.77), channel_id=1, source_target_pairs={{0,6},{1,7},{2,4},{3,5},{4,2},{5,3},{6,0},{7,1},{8,14},{9,15},{10,... | collective-permute-start | bytes 6152 | tf_op jit(solution)/shard_map/ppermute | solution.py:625
  203.8 6.0 %copy-start = (f32[768]{0:T(1024)S(1)}, f32[768]{0:T(1024)}, u32[]{:S(2)}) copy-start(f32[768]{0:T(1024)} %gain_ref.3) | copy-start | bytes 9220
  207.0 2.7 %collective-permute-start.17 = (f32[1,512]{1,0:T(1,128)S(1)}, f32[1,512]{1,0:T(1,128)S(1)}, u32[]{:S(2)}, u32[]{:S(2)}) collective-permute-start(f32[1,512]{1,0:T(1,128)S(1)} %add_add_fusion.square_ref), channel_id=1, source_target_pairs={{0,1},{1,0},{2,3},{3,2},{4,5},{5,4},{6,7},{7,6},{8,9},{9,8},{10,11... | collective-permute-start | bytes 6152 | tf_op jit(solution)/shard_map/ppermute | solution.py:625
